TPU v7x, 256 devices: a whole 4x4x8 slice. The times are simulated.
256 devices in a mesh: freq: 8 (over z_lo, y), slab: 32 (over z_hi, x, core).
Axes of the slice: x: 4, y: 4, z: 8 (z_hi: 4, z_lo: 2; z = z_hi * 2 + z_lo), core: 2. Of those that a mesh axis runs over, the one named last changes fastest.
Arguments:
- wavefield: float32 [2, 8, 2048, 2048], P(None, 'freq', 'slab'), may hold values from -6 to 6
- freqs: float32 [8], P('freq'), may hold values from 0.15 to 0.45
- velocity: float32 [3, 2048, 2048], P(None, 'slab', 'freq'), may hold values from 0.7 to 1.6
- ref_slow: float32 [3, 2], replicated, may hold values from 0.6 to 1.5, as said below
Outputs:
- migrated: float32 [2, 8, 2048, 2048], P(None, 'freq', 'slab')
Inputs may be any that keep to these rules, and one draw needn't show every extreme that they name: ref_slow[d, 1] - ref_slow[d, 0] lies between 0.3 and 0.6 for every depth step.
All inputs are finite; a program needn't handle non-finite values.
Results may differ from a plain program's by a relative error of at most 0.0003.
Values sent between devices are 32-bit elements; how exact they have to be, the bound alone decides.
No kernel may reach another device: no remote copies, remote signals or barrier semaphores. Data moves between devices by JAX's collectives and lax.ppermute only.
A program may use at most 64 MiB of HBM per device.

v0:
```python
import math

import jax
import jax.numpy as jnp
from jax import lax
from jax.sharding import PartitionSpec as P

two_pi = 2.0 * math.pi
depth_step = 2.0


def dft_matrix(length, sign):
    index = jnp.arange(length, dtype=jnp.int32)
    product = index[:, None] * index[None, :] % length
    angle = sign * two_pi / length * product.astype(jnp.float32)
    scale = 1.0 / math.sqrt(length)
    return (jnp.cos(angle) * scale, jnp.sin(angle) * scale)


def twiddle(outer, inner, sign):
    length = outer * inner
    product = (
        jnp.arange(outer, dtype=jnp.int32)[:, None]
        * jnp.arange(inner, dtype=jnp.int32)[None, :]
        % length
    )
    angle = sign * two_pi / length * product.astype(jnp.float32)
    return (jnp.cos(angle), jnp.sin(angle))


def complex_mix(form, mat_real, mat_imag, data_real, data_imag):

    def product(matrix, data):
        return jnp.einsum(form, matrix, data, precision=lax.Precision.HIGHEST)

    return (
        product(mat_real, data_real) - product(mat_imag, data_imag),
        product(mat_real, data_imag) + product(mat_imag, data_real),
    )


def transform(real, imag, trailing, sign):
    length = real.shape[-2] if trailing else real.shape[-1]
    inner = min(length, 128)
    outer = length // inner
    outer_real, outer_imag = dft_matrix(outer, sign)
    inner_real, inner_imag = dft_matrix(inner, sign)
    turn_real, turn_imag = twiddle(outer, inner, sign)
    if trailing:
        leading = real.shape[:-2]
        tail = real.shape[-1:]
        form_outer = "ka,...abm->...kbm"
        form_inner = "bj,...kbm->...kjm"
        turn_real = turn_real[:, :, None]
        turn_imag = turn_imag[:, :, None]
    else:
        leading = real.shape[:-1]
        tail = ()
        form_outer = "ka,...ab->...kb"
        form_inner = "bj,...kb->...kj"
    split_shape = leading + (outer, inner) + tail
    real = real.reshape(split_shape)
    imag = imag.reshape(split_shape)
    if sign < 0:
        real, imag = complex_mix(form_outer, outer_real, outer_imag, real, imag)
        real, imag = (real * turn_real - imag * turn_imag, real * turn_imag + imag * turn_real)
        real, imag = complex_mix(form_inner, inner_real, inner_imag, real, imag)
    else:
        real, imag = complex_mix(form_inner, inner_real, inner_imag, real, imag)
        real, imag = (real * turn_real - imag * turn_imag, real * turn_imag + imag * turn_real)
        real, imag = complex_mix(form_outer, outer_real, outer_imag, real, imag)
    joined = leading + (length,) + tail
    return (real.reshape(joined), imag.reshape(joined))


def wave_numbers(positions, length):
    inner = min(length, 128)
    outer = length // inner
    number = positions // inner + outer * (positions % inner)
    number = jnp.where(number < length // 2, number, number - length)
    return number.astype(jnp.float32) / length


def forward_x(items):
    real, imag = transform(items[0], items[1], True, -1)
    return jnp.stack((real, imag))


def inverse_y(items):
    real, imag = transform(items[:, 0], items[:, 1], False, 1)
    return jnp.stack((real, imag), axis=1)


def shards(wavefield, freqs, velocity, ref_slow):
    slabs = lax.axis_size("slab")
    slab_index = lax.axis_index("slab")
    rows = wavefield.shape[2]
    width_x = rows * slabs
    width_y = wavefield.shape[3]
    columns = width_y // slabs
    depth = ref_slow.shape[0]
    along_x = wave_numbers(jnp.arange(width_x, dtype=jnp.int32), width_x)
    along_y = wave_numbers(slab_index * columns + jnp.arange(columns, dtype=jnp.int32), width_y)
    square = along_x[:, None] ** 2 + along_y[None, :] ** 2
    freq_col = freqs[:, None, None]

    def advance(level, field):
        local_tile = lax.dynamic_index_in_dim(velocity, level, 0, keepdims=False)
        tile = lax.all_gather(local_tile, "freq", axis=1, tiled=True)
        real, imag = transform(field[0], field[1], False, -1)
        spectrum = forward_x(
            lax.all_to_all(jnp.stack((real, imag)), "slab", split_axis=3, concat_axis=2, tiled=True)
        )
        slow_pair = lax.dynamic_index_in_dim(ref_slow, level, 0, keepdims=False)
        slowness = 1.0 / tile
        upper_weight = jnp.clip((slowness - slow_pair[0]) / (slow_pair[1] - slow_pair[0]), 0.0, 1.0)
        weights = [1.0 - upper_weight, upper_weight]
        shifted = []
        for branch in range(2):
            target = (freq_col * slow_pair[branch]) ** 2 - square[None]
            angle = two_pi * depth_step * jnp.sqrt(jnp.abs(target))
            live = target >= 0
            prop_real = jnp.where(live, jnp.cos(angle), jnp.exp(-angle))
            prop_imag = jnp.where(live, jnp.sin(angle), jnp.zeros_like(angle))
            spec_real = spectrum[0] * prop_real - spectrum[1] * prop_imag
            spec_imag = spectrum[0] * prop_imag + spectrum[1] * prop_real
            back_real, back_imag = transform(spec_real, spec_imag, True, 1)
            shifted.append(jnp.stack((back_real, back_imag)))
        pieces = []
        for branch in range(2):
            moved = lax.all_to_all(shifted[branch], "slab", split_axis=2, concat_axis=3, tiled=True)
            pieces.append(inverse_y(moved[None])[0])
        spatial = jnp.stack(pieces)
        new_real = jnp.zeros_like(field[0])
        new_imag = jnp.zeros_like(field[1])
        for branch in range(2):
            theta = two_pi * depth_step * freq_col * (slowness - slow_pair[branch])[None]
            weight = weights[branch][None]
            cosine = jnp.cos(theta)
            sine = jnp.sin(theta)
            part_real = spatial[branch, 0]
            part_imag = spatial[branch, 1]
            new_real = new_real + weight * (cosine * part_real - sine * part_imag)
            new_imag = new_imag + weight * (cosine * part_imag + sine * part_real)
        return jnp.stack((new_real, new_imag))

    return lax.fori_loop(0, depth, advance, wavefield)


def solution(mesh):
    return jax.shard_map(
        shards,
        mesh=mesh,
        in_specs=(P(None, "freq", "slab", None), P("freq"), P(None, "slab", "freq"), P()),
        out_specs=P(None, "freq", "slab", None),
        check_vma=False,
    )
```

profile of v0, /device:TPU:2, one launch (start us, length us, event | category | flops | bytes accessed | tf_op | source)
XLA Modules:
  0.0 745.5 jit_solution(8301258523140960908)
XLA Ops:
  1.2 743.0 %while.17 = (s32[]{:T(128)}, f32[2,1,64,2048]{3,2,1,0:T(8,128)S(1)}, f32[3,64,256]{2,1,0:T(8,128)}, f32[3,2]{0,1:T(2,128)S(1)}, f32[1,1,1]{2,1,0:T(1,128)}, /*in...) while((s32[]{:T(128)}, ...), condition=%wide.region_1.2_spmd.clone, body=%wide.region_0.1_spmd.clone.sunk | while | flops 5460087808 | bytes 181871536 | solution.py:147
  13.6 8.4 %reduce.12 = f32[2048,2,64]{2,1,0:T(2,128)} reduce(f32[2048,2,1,64]{3,2,1,0:T(1,128)S(1)} %fusion.669, f32[]{:T(128)} %broadcast.1857), dimensions={2}, to_apply=%fusion.426.reduce_sub_computation | reduce | bytes 2097156 | tf_op jit(solution)/shard_map/while
  26.1 12.3 %all-to-all-start = ((f32[32,1,8192]{2,1,0:T(1,128)}), f32[32,1,8192]{2,1,0:T(1,128)S(1)}, u32[]{:S(2)}, u32[]{:S(2)}) async-start(f32[32,1,8192]{2,1,0:T(1,128)} %reshape.1313), calls=%async_computation | async-start | bytes 2097152 | tf_op jit(solution)/shard_map/while/body/eval_jaxpr/all_to_all | solution.py:112
  49.6 15.6 %all-to-all-done = f32[32,1,8192]{2,1,0:T(1,128)S(1)} async-done(((f32[32,1,8192]{2,1,0:T(1,128)}), f32[32,1,8192]{2,1,0:T(1,128)S(1)}, u32[]{:S(2)}, u32[]{:S(2)}) %all-to-all-start) | async-done | bytes 1048608 | tf_op jit(solution)/shard_map/while/body/eval_jaxpr/all_to_all | solution.py:112
  98.4 8.4 %reduce.16 = f32[2048,2,64]{2,1,0:T(2,128)} reduce(f32[2048,2,1,64]{3,2,1,0:T(1,128)S(1)} %fusion.699, f32[]{:T(128)} %broadcast.1861), dimensions={2}, to_apply=%fusion.425.reduce_sub_computation | reduce | bytes 2097156 | tf_op jit(solution)/shard_map/while
  111.0 7.1 all-to-all-start.2
  130.6 8.4 %reduce.14 = f32[2048,2,64]{2,1,0:T(2,128)} reduce(f32[2048,2,1,64]{3,2,1,0:T(1,128)S(1)} %fusion.690, f32[]{:T(128)} %broadcast.1859), dimensions={2}, to_apply=%fusion.424.reduce_sub_computation | reduce | bytes 2097156 | tf_op jit(solution)/shard_map/while
  145.9 7.1 all-to-all-start.1
  153.0 48.0 %all-gather.3 = f32[1,64,2048]{2,1,0:T(8,128)} all-gather(f32[1,64,256]{2,1,0:T(8,128)S(1)} %constant_dynamic-slice_fusion.5), channel_id=2, replica_groups=mesh['freq'=8,'slab'=32] {'freq'}, dimensions={2}, use_global_device_ids=true | all-gather | bytes 589824 | tf_op jit(solution)/shard_map/while/body/eval_jaxpr/all_gather | solution.py:109
  201.6 4.4 reduce.17
  220.7 5.4 reduce.15
  242.5 5.6 fusion.704
  260.6 8.4 %reduce.12 = f32[2048,2,64]{2,1,0:T(2,128)} reduce(f32[2048,2,1,64]{3,2,1,0:T(1,128)S(1)} %fusion.669, f32[]{:T(128)} %broadcast.1857), dimensions={2}, to_apply=%fusion.426.reduce_sub_computation | reduce | bytes 2097156 | tf_op jit(solution)/shard_map/while
  273.2 13.7 %all-to-all-start = ((f32[32,1,8192]{2,1,0:T(1,128)}), f32[32,1,8192]{2,1,0:T(1,128)S(1)}, u32[]{:S(2)}, u32[]{:S(2)}) async-start(f32[32,1,8192]{2,1,0:T(1,128)} %reshape.1313), calls=%async_computation | async-start | bytes 2097152 | tf_op jit(solution)/shard_map/while/body/eval_jaxpr/all_to_all | solution.py:112
  298.1 16.4 %all-to-all-done = f32[32,1,8192]{2,1,0:T(1,128)S(1)} async-done(((f32[32,1,8192]{2,1,0:T(1,128)}), f32[32,1,8192]{2,1,0:T(1,128)S(1)}, u32[]{:S(2)}, u32[]{:S(2)}) %all-to-all-start) | async-done | bytes 1048608 | tf_op jit(solution)/shard_map/while/body/eval_jaxpr/all_to_all | solution.py:112
  347.7 8.4 %reduce.16 = f32[2048,2,64]{2,1,0:T(2,128)} reduce(f32[2048,2,1,64]{3,2,1,0:T(1,128)S(1)} %fusion.699, f32[]{:T(128)} %broadcast.1861), dimensions={2}, to_apply=%fusion.425.reduce_sub_computation | reduce | bytes 2097156 | tf_op jit(solution)/shard_map/while
  360.3 6.7 all-to-all-start.2
  379.5 8.4 %reduce.14 = f32[2048,2,64]{2,1,0:T(2,128)} reduce(f32[2048,2,1,64]{3,2,1,0:T(1,128)S(1)} %fusion.690, f32[]{:T(128)} %broadcast.1859), dimensions={2}, to_apply=%fusion.424.reduce_sub_computation | reduce | bytes 2097156 | tf_op jit(solution)/shard_map/while
  394.1 7.9 %all-to-all-start.1 = ((f32[32,1,8192]{2,1,0:T(1,128)}), f32[32,1,8192]{2,1,0:T(1,128)}, u32[]{:S(2)}, u32[]{:S(2)}) async-start(f32[32,1,8192]{2,1,0:T(1,128)} %reshape.1317), calls=%async_computation.1 | async-start | bytes 2097152 | tf_op jit(solution)/shard_map/while/body/eval_jaxpr/all_to_all | solution.py:131
  401.9 47.3 %all-gather.3 = f32[1,64,2048]{2,1,0:T(8,128)} all-gather(f32[1,64,256]{2,1,0:T(8,128)S(1)} %constant_dynamic-slice_fusion.5), channel_id=2, replica_groups=mesh['freq'=8,'slab'=32] {'freq'}, dimensions={2}, use_global_device_ids=true | all-gather | bytes 589824 | tf_op jit(solution)/shard_map/while/body/eval_jaxpr/all_gather | solution.py:109
  469.0 5.4 reduce.15
  490.8 5.6 fusion.704
  508.9 8.4 %reduce.12 = f32[2048,2,64]{2,1,0:T(2,128)} reduce(f32[2048,2,1,64]{3,2,1,0:T(1,128)S(1)} %fusion.669, f32[]{:T(128)} %broadcast.1857), dimensions={2}, to_apply=%fusion.426.reduce_sub_computation | reduce | bytes 2097156 | tf_op jit(solution)/shard_map/while
  521.4 11.3 %all-to-all-start = ((f32[32,1,8192]{2,1,0:T(1,128)}), f32[32,1,8192]{2,1,0:T(1,128)S(1)}, u32[]{:S(2)}, u32[]{:S(2)}) async-start(f32[32,1,8192]{2,1,0:T(1,128)} %reshape.1313), calls=%async_computation | async-start | bytes 2097152 | tf_op jit(solution)/shard_map/while/body/eval_jaxpr/all_to_all | solution.py:112
  543.9 16.5 %all-to-all-done = f32[32,1,8192]{2,1,0:T(1,128)S(1)} async-done(((f32[32,1,8192]{2,1,0:T(1,128)}), f32[32,1,8192]{2,1,0:T(1,128)S(1)}, u32[]{:S(2)}, u32[]{:S(2)}) %all-to-all-start) | async-done | bytes 1048608 | tf_op jit(solution)/shard_map/while/body/eval_jaxpr/all_to_all | solution.py:112
  593.6 8.4 %reduce.16 = f32[2048,2,64]{2,1,0:T(2,128)} reduce(f32[2048,2,1,64]{3,2,1,0:T(1,128)S(1)} %fusion.699, f32[]{:T(128)} %broadcast.1861), dimensions={2}, to_apply=%fusion.425.reduce_sub_computation | reduce | bytes 2097156 | tf_op jit(solution)/shard_map/while
  606.2 6.6 all-to-all-start.2
  625.4 8.4 %reduce.14 = f32[2048,2,64]{2,1,0:T(2,128)} reduce(f32[2048,2,1,64]{3,2,1,0:T(1,128)S(1)} %fusion.690, f32[]{:T(128)} %broadcast.1859), dimensions={2}, to_apply=%fusion.424.reduce_sub_computation | reduce | bytes 2097156 | tf_op jit(solution)/shard_map/while
  640.3 7.4 all-to-all-start.1
  647.8 48.3 %all-gather.3 = f32[1,64,2048]{2,1,0:T(8,128)} all-gather(f32[1,64,256]{2,1,0:T(8,128)S(1)} %constant_dynamic-slice_fusion.5), channel_id=2, replica_groups=mesh['freq'=8,'slab'=32] {'freq'}, dimensions={2}, use_global_device_ids=true | all-gather | bytes 589824 | tf_op jit(solution)/shard_map/while/body/eval_jaxpr/all_gather | solution.py:109
  715.7 5.4 reduce.15
  737.5 5.6 fusion.704
  (361 shorter events, 344.5 us)
Async XLA Ops:
  26.1 39.1 %all-to-all-start = ((f32[32,1,8192]{2,1,0:T(1,128)}), f32[32,1,8192]{2,1,0:T(1,128)S(1)}, u32[]{:S(2)}, u32[]{:S(2)}) async-start(f32[32,1,8192]{2,1,0:T(1,128)} %reshape.1313), calls=%async_computation | async-start | bytes 2097152 | tf_op jit(solution)/shard_map/while/body/eval_jaxpr/all_to_all | solution.py:112
  76.2 2.7 copy-start.4
  76.2 2.7 copy-start.5
  76.2 2.7 copy-start.6
  76.2 2.7 copy-start.7
  111.0 34.9 %all-to-all-start.2 = ((f32[32,1,8192]{2,1,0:T(1,128)}), f32[32,1,8192]{2,1,0:T(1,128)}, u32[]{:S(2)}, u32[]{:S(2)}) async-start(f32[32,1,8192]{2,1,0:T(1,128)} %reshape.1319), calls=%async_computation.2 | async-start | bytes 2097152 | tf_op jit(solution)/shard_map/while/body/eval_jaxpr/all_to_all | solution.py:131
  145.9 74.3 %all-to-all-start.1 = ((f32[32,1,8192]{2,1,0:T(1,128)}), f32[32,1,8192]{2,1,0:T(1,128)}, u32[]{:S(2)}, u32[]{:S(2)}) async-start(f32[32,1,8192]{2,1,0:T(1,128)} %reshape.1317), calls=%async_computation.1 | async-start | bytes 2097152 | tf_op jit(solution)/shard_map/while/body/eval_jaxpr/all_to_all | solution.py:131
  237.6 2.2 copy-start.3
  239.1 1.4 copy-start.2
  241.2 1.4 copy-start.1
  273.2 41.3 %all-to-all-start = ((f32[32,1,8192]{2,1,0:T(1,128)}), f32[32,1,8192]{2,1,0:T(1,128)S(1)}, u32[]{:S(2)}, u32[]{:S(2)}) async-start(f32[32,1,8192]{2,1,0:T(1,128)} %reshape.1313), calls=%async_computation | async-start | bytes 2097152 | tf_op jit(solution)/shard_map/while/body/eval_jaxpr/all_to_all | solution.py:112
  325.5 2.7 copy-start.4
  325.5 2.7 copy-start.5
  325.5 2.7 copy-start.6
  325.5 2.7 copy-start.7
  360.3 33.7 %all-to-all-start.2 = ((f32[32,1,8192]{2,1,0:T(1,128)}), f32[32,1,8192]{2,1,0:T(1,128)}, u32[]{:S(2)}, u32[]{:S(2)}) async-start(f32[32,1,8192]{2,1,0:T(1,128)} %reshape.1319), calls=%async_computation.2 | async-start | bytes 2097152 | tf_op jit(solution)/shard_map/while/body/eval_jaxpr/all_to_all | solution.py:131
  374.1 1.3 copy-start
  394.1 74.4 %all-to-all-start.1 = ((f32[32,1,8192]{2,1,0:T(1,128)}), f32[32,1,8192]{2,1,0:T(1,128)}, u32[]{:S(2)}, u32[]{:S(2)}) async-start(f32[32,1,8192]{2,1,0:T(1,128)} %reshape.1317), calls=%async_computation.1 | async-start | bytes 2097152 | tf_op jit(solution)/shard_map/while/body/eval_jaxpr/all_to_all | solution.py:131
  485.9 2.2 copy-start.3
  487.4 1.4 copy-start.2
  489.4 1.4 copy-start.1
  521.4 39.0 %all-to-all-start = ((f32[32,1,8192]{2,1,0:T(1,128)}), f32[32,1,8192]{2,1,0:T(1,128)S(1)}, u32[]{:S(2)}, u32[]{:S(2)}) async-start(f32[32,1,8192]{2,1,0:T(1,128)} %reshape.1313), calls=%async_computation | async-start | bytes 2097152 | tf_op jit(solution)/shard_map/while/body/eval_jaxpr/all_to_all | solution.py:112
  571.4 2.7 copy-start.4
  571.4 2.7 copy-start.5
  571.4 2.7 copy-start.6
  571.4 2.7 copy-start.7
  606.2 34.1 %all-to-all-start.2 = ((f32[32,1,8192]{2,1,0:T(1,128)}), f32[32,1,8192]{2,1,0:T(1,128)}, u32[]{:S(2)}, u32[]{:S(2)}) async-start(f32[32,1,8192]{2,1,0:T(1,128)} %reshape.1319), calls=%async_computation.2 | async-start | bytes 2097152 | tf_op jit(solution)/shard_map/while/body/eval_jaxpr/all_to_all | solution.py:131
  619.9 1.3 copy-start
  640.3 74.8 %all-to-all-start.1 = ((f32[32,1,8192]{2,1,0:T(1,128)}), f32[32,1,8192]{2,1,0:T(1,128)}, u32[]{:S(2)}, u32[]{:S(2)}) async-start(f32[32,1,8192]{2,1,0:T(1,128)} %reshape.1317), calls=%async_computation.1 | async-start | bytes 2097152 | tf_op jit(solution)/shard_map/while/body/eval_jaxpr/all_to_all | solution.py:131
  732.6 2.2 copy-start.3
  734.1 1.4 copy-start.2
  736.2 1.4 copy-start.1
  (4 other events, 4.8 us)
where the time goes:
time: 751 us; the launch traced here: 746 us
  other arithmetic  178 us (24%)
  local copies, waits for them, and re-layouts  150 us (20%)
  blocking collectives  144 us (19%)
  matrix products  122 us (16%)
  starting transfers between devices  80 us (11%)
  waiting for transfers between devices  55.7 us (7%)
  loops' own time  15.2 us (2%)
    all_gather x3, blocking collectives, advance(): tile = lax.all_gather(local_tile, 'freq', axis=1, tiled=True)  144 us
    dot_general x144, matrix products, product(): return jnp.einsum(form, matrix, data, precision=lax.Precision.HIGHEST)  122 us
    while x21, other arithmetic  121 us
    while x117, local copies, waits for them, and re-layouts  83.6 us
    all_to_all x3, waiting for transfers between devices, advance(): lax.all_to_all(jnp.stack((real, imag)), 'slab', split_axis=3, concat_axis...  48.6 us
    all_to_all x6, starting transfers between devices, advance(): lax.all_to_all(shifted[branch], 'slab', split_axis=2, concat_axis=3, tile...  42.8 us
    all_to_all x3, starting transfers between devices, advance(): lax.all_to_all(jnp.stack((real, imag)), 'slab', split_axis=3, concat_axis...  37.2 us
    all_to_all x6, other arithmetic, advance(): lax.all_to_all(shifted[branch], 'slab', split_axis=2, concat_axis=3, tile...  29.5 us
  transfers between devices with their start and end apart: 9, of which 6 were waited for; matrix products, arithmetic and copies ran while one was open for 21% of the time, Pallas kernels for 0%

commit v1 on v0

v1 whole, which is shorter than its diff:
```python
import math

import jax
import jax.numpy as jnp
import numpy as np
from jax import lax
from jax.experimental import pallas as pl
from jax.experimental.pallas import tpu as pltpu
from jax.sharding import PartitionSpec as P

two_pi = 2.0 * math.pi
depth_step = 2.0

length = 2048
outer = 16
inner = 128
half = 64
rows = 64
parts = 32
sub = 8


def split_bf16(matrix):
    matrix = np.asarray(matrix, np.float32)
    high = matrix.astype(jnp.bfloat16)
    low = (matrix - high.astype(np.float32)).astype(jnp.bfloat16)
    return high, low


def dft_inner(sign):
    index = np.arange(inner)
    angle = sign * two_pi / inner * (index[:, None] * index[None, :] % inner)
    scale = 1.0 / math.sqrt(length)
    return np.cos(angle) * scale, np.sin(angle) * scale


def packed_order():
    low = np.arange(half)
    return np.concatenate([low, inner + low, half + low, inner + half + low])


def forward_y_matrix():
    real, imag = dft_inner(-1)
    full = np.block([[real, imag], [-imag, real]])
    return split_bf16(full[:, packed_order()])


def inverse_y_matrix():
    real, imag = dft_inner(1)
    full = np.block([[real, imag], [-imag, real]])
    return split_bf16(full[packed_order(), :])


def x_matrix(sign):
    real, imag = dft_inner(sign)
    return split_bf16(np.block([[real, -imag], [imag, real]]))


def y_turns():
    angle = two_pi / length * (np.arange(outer)[:, None] * np.arange(inner)[None, :])
    return np.cos(angle).astype(np.float32), np.sin(angle).astype(np.float32)


def x_turns():
    upper = (np.arange(inner) >= half).astype(np.int64)
    k = 2 * np.arange(outer // 2)[:, None, None] + upper[None, None, :]
    angle = two_pi / length * (k * np.arange(inner)[None, :, None])
    return np.cos(angle).astype(np.float32), np.sin(angle).astype(np.float32)


def lane_turns():
    upper = (np.arange(inner) >= half).astype(np.float64)
    angle = two_pi / outer * (np.arange(outer // 2)[:, None] * upper[None, :])
    return np.cos(angle).astype(np.float32), np.sin(angle).astype(np.float32)


def fit_even(function, terms):
    nodes = np.cos(np.pi * (np.arange(256) + 0.5) / 256)
    basis = np.stack([nodes ** (2 * n) for n in range(terms)], axis=1)
    solved = np.linalg.lstsq(basis, function(nodes), rcond=None)[0]
    return [float(c) for c in solved]


cos_fit = fit_even(lambda z: np.cos(np.pi * z), 9)
sin_fit = fit_even(lambda z: np.pi * np.sinc(z), 9)


def cis(cycles):
    z = 2.0 * (cycles - jnp.floor(cycles + 0.5))
    square = z * z
    cosine = cos_fit[-1]
    for c in cos_fit[-2::-1]:
        cosine = cosine * square + c
    sine = sin_fit[-1]
    for c in sin_fit[-2::-1]:
        sine = sine * square + c
    return cosine, sine * z


def times(a, b):
    return (a[0] * b[0] - a[1] * b[1], a[0] * b[1] + a[1] * b[0])


def times_conj(a, b):
    return (a[0] * b[0] + a[1] * b[1], a[1] * b[0] - a[0] * b[1])


def plus(a, b):
    return (a[0] + b[0], a[1] + b[1])


def minus(a, b):
    return (a[0] - b[0], a[1] - b[1])


def times_root(a, power, n, sign):
    eighth = (8 * power) % (8 * n)
    real, imag = a
    if eighth % n == 0:
        step = (eighth // n) % 8
        if sign < 0:
            step = (8 - step) % 8
        if step == 0:
            return a
        if step == 2:
            return (-imag, real)
        if step == 4:
            return (-real, -imag)
        if step == 6:
            return (imag, -real)
        root = math.sqrt(0.5)
        total = (real + imag) * root
        differ = (real - imag) * root
        if step == 1:
            return (differ, total)
        if step == 3:
            return (-total, differ)
        if step == 5:
            return (-differ, -total)
        return (total, -differ)
    angle = sign * two_pi * power / n
    c, s = math.cos(angle), math.sin(angle)
    return (real * c - imag * s, real * s + imag * c)


def dft(values, sign):
    n = len(values)
    if n == 2:
        return [plus(*values), minus(*values)]
    if n == 4:
        t0, t1 = plus(values[0], values[2]), minus(values[0], values[2])
        t2, t3 = plus(values[1], values[3]), minus(values[1], values[3])
        if sign > 0:
            y1 = (t1[0] - t3[1], t1[1] + t3[0])
            y3 = (t1[0] + t3[1], t1[1] - t3[0])
        else:
            y1 = (t1[0] + t3[1], t1[1] - t3[0])
            y3 = (t1[0] - t3[1], t1[1] + t3[0])
        return [plus(t0, t2), y1, minus(t0, t2), y3]
    radix = 2 if n == 8 else 4
    m = n // radix
    inside = [dft(values[s::radix], sign) for s in range(radix)]
    out = [None] * n
    for k in range(m):
        turned = [times_root(inside[s][k], s * k, n, sign) for s in range(radix)]
        for step, value in enumerate(dft(turned, sign)):
            out[k + m * step] = value
    return out


def cut(x):
    high = x.astype(jnp.bfloat16)
    low = (x - high.astype(jnp.float32)).astype(jnp.bfloat16)
    return high, low


def product(a, b):
    return jnp.dot(a, b, preferred_element_type=jnp.float32)


def mix(a, b):
    (a_high, a_low), (b_high, b_low) = a, b
    return product(a_high, b_high) + (product(a_high, b_low) + product(a_low, b_high))


def block_rows(step):
    return pl.ds(pl.multiple_of(step * sub, sub), sub)


def forward_y(read, out, spectrum, matrix_high, matrix_low, turn_cos, turn_sin):
    def step(c, carry):
        here = block_rows(c)
        values = dft([read(here, a) for a in range(outer)], -1)
        for k in range(outer):
            turn = (turn_cos[k : k + 1, :], turn_sin[k : k + 1, :])
            value = values[k] if k == 0 else times_conj(values[k], turn)
            spectrum[k, here, :inner] = value[0]
            spectrum[k, here, inner:] = value[1]
        return carry

    lax.fori_loop(0, rows // sub, step, 0)
    matrix = (matrix_high[...], matrix_low[...])
    for k in range(0, outer, 4):
        block = spectrum[k : k + 4].reshape(4 * rows, 2 * inner)
        result = mix(cut(block), matrix)
        for n in range(4):
            one = result[n * rows : (n + 1) * rows]
            out[2 * (k + n)] = one[:, :inner]
            out[2 * (k + n) + 1] = one[:, inner:]


def start_kernel(real, imag, matrix_high, matrix_low, turn_cos, turn_sin, out, spectrum):
    def read(here, a):
        columns = slice(a * inner, (a + 1) * inner)
        return real[here, columns], imag[here, columns]

    forward_y(read, out, spectrum, matrix_high, matrix_low, turn_cos, turn_sin)


def combine_kernel(
    last,
    scalars,
    moved,
    velocity,
    back_high,
    back_low,
    matrix_high,
    matrix_low,
    turn_cos,
    turn_sin,
    out,
    fields,
    weighted,
    spectrum,
):
    freq, lower, inverse_gap, turn_real, turn_imag = (scalars[n] for n in range(5))

    matrix = (back_high[...], back_low[...])
    for branch in range(2):
        for k in range(0, outer, 4):
            block = jnp.concatenate(
                [
                    jnp.concatenate([moved[2 * n, branch], moved[2 * n + 1, branch]], axis=1)
                    for n in range(k, k + 4)
                ],
                axis=0,
            )
            result = mix(cut(block), matrix)
            fields[branch, k : k + 4] = result.reshape(4, rows, 2 * inner)

    def weigh(c, carry):
        here = block_rows(c)
        for a in range(outer):
            speed = velocity[a // 2, here, (a % 2) * inner : (a % 2 + 1) * inner]
            slowness = 1.0 / speed
            excess = slowness - lower
            upper_weight = jnp.clip(excess * inverse_gap, 0.0, 1.0)
            lower_weight = 1.0 - upper_weight
            cosine, sine = cis((depth_step * freq) * excess)
            columns = slice(a * inner, (a + 1) * inner)
            weighted[0, here, columns] = lower_weight * cosine
            weighted[1, here, columns] = lower_weight * sine
            weighted[2, here, columns] = upper_weight * (cosine * turn_real - sine * turn_imag)
            weighted[3, here, columns] = upper_weight * (cosine * turn_imag + sine * turn_real)
        return carry

    lax.fori_loop(0, rows // sub, weigh, 0)

    def back(c, carry):
        here = block_rows(c)
        for branch in range(2):
            values = []
            for k in range(outer):
                value = (fields[branch, k, here, :inner], fields[branch, k, here, inner:])
                turn = (turn_cos[k : k + 1, :], turn_sin[k : k + 1, :])
                values.append(value if k == 0 else times(value, turn))
            values = dft(values, 1)
            for a in range(outer):
                columns = slice(a * inner, (a + 1) * inner)
                weight = (weighted[2 * branch, here, columns], weighted[2 * branch + 1, here, columns])
                value = times(values[a], weight)
                if last:
                    if branch == 0:
                        out[0, here, columns] = value[0]
                        out[1, here, columns] = value[1]
                    else:
                        out[0, here, columns] += value[0]
                        out[1, here, columns] += value[1]
                else:
                    if branch == 1:
                        value = (
                            value[0] + weighted[0, here, columns],
                            value[1] + weighted[1, here, columns],
                        )
                    weighted[0, here, columns] = value[0]
                    weighted[1, here, columns] = value[1]
        return carry

    lax.fori_loop(0, rows // sub, back, 0)
    if last:
        return

    def read(here, a):
        columns = slice(a * inner, (a + 1) * inner)
        return weighted[0, here, columns], weighted[1, here, columns]

    forward_y(read, out, spectrum, matrix_high, matrix_low, turn_cos, turn_sin)


def shift_kernel(
    scalars,
    square_y,
    arrived,
    there_high,
    there_low,
    back_high,
    back_low,
    turn_cos,
    turn_sin,
    lane_cos,
    lane_sin,
    out,
    spectrum,
    shifted,
):
    lane = lax.broadcasted_iota(jnp.int32, (sub, inner), 1)
    low_lanes = lane < half
    groups = outer // 2
    steps = inner // sub

    def there(c, carry):
        here = block_rows(c)
        values = []
        for a in range(groups):
            first = arrived[pl.ds(pl.multiple_of(a * inner + c * sub, sub), sub), :]
            second = arrived[pl.ds(pl.multiple_of((a + groups) * inner + c * sub, sub), sub), :]
            total, differ = first + second, first - second
            value = (
                jnp.where(low_lanes, total, pltpu.roll(differ, half, 1)),
                jnp.where(low_lanes, pltpu.roll(total, half, 1), differ),
            )
            turn = (lane_cos[a : a + 1, :], lane_sin[a : a + 1, :])
            values.append(value if a == 0 else times_conj(value, turn))
        values = dft(values, -1)
        second_half = pl.ds(pl.multiple_of(inner + c * sub, sub), sub)
        for k in range(groups):
            value = times_conj(values[k], (turn_cos[k, here, :], turn_sin[k, here, :]))
            columns = slice(k * inner, (k + 1) * inner)
            spectrum[here, columns] = value[0]
            spectrum[second_half, columns] = value[1]
        return carry

    lax.fori_loop(0, steps, there, 0)
    matrix = (there_high[...], there_low[...])
    for n in range(4):
        columns = slice(n * 2 * inner, (n + 1) * 2 * inner)
        spectrum[:, columns] = mix(matrix, cut(spectrum[:, columns]))

    sub_row = lax.broadcasted_iota(jnp.int32, (sub, inner), 0)
    fy = square_y[0:1, :]

    def propagate(c, carry):
        here = block_rows(c)
        second_half = pl.ds(pl.multiple_of(inner + c * sub, sub), sub)
        for k in range(groups):
            number = 2 * k + jnp.where(low_lanes, 0, 1) + outer * (c * sub + sub_row)
            fx = jnp.minimum(number, length - number).astype(jnp.float32) * (1.0 / length)
            square = fx * fx + fy
            columns = slice(k * inner, (k + 1) * inner)
            value = (spectrum[here, columns], spectrum[second_half, columns])
            for branch in range(2):
                target = scalars[branch] - square
                cycles = depth_step * jnp.sqrt(jnp.abs(target))
                cosine, sine = cis(cycles)
                live = target >= 0
                shift = (
                    jnp.where(live, cosine, jnp.exp(-two_pi * cycles)),
                    jnp.where(live, sine, 0.0),
                )
                moved = times(value, shift)
                shifted[branch, here, columns] = moved[0]
                shifted[branch, second_half, columns] = moved[1]
        return carry

    lax.fori_loop(0, steps, propagate, 0)
    matrix = (back_high[...], back_low[...])
    for branch in range(2):
        for n in range(4):
            columns = slice(n * 2 * inner, (n + 1) * 2 * inner)
            shifted[branch, :, columns] = mix(matrix, cut(shifted[branch, :, columns]))

    for top in range(2):

        def back(c, carry):
            position = top * half + c * sub
            here = pl.ds(pl.multiple_of(position, sub), sub)
            second_half = pl.ds(pl.multiple_of(inner + position, sub), sub)
            local = block_rows(c)
            for branch in range(2):
                values = []
                for k in range(groups):
                    columns = slice(k * inner, (k + 1) * inner)
                    value = (shifted[branch, here, columns], shifted[branch, second_half, columns])
                    values.append(times(value, (turn_cos[k, here, :], turn_sin[k, here, :])))
                values = dft(values, 1)
                for a in range(groups):
                    value = values[a]
                    if a > 0:
                        value = times(value, (lane_cos[a : a + 1, :], lane_sin[a : a + 1, :]))
                    even = jnp.where(low_lanes, value[0], pltpu.roll(value[1], half, 1))
                    odd = jnp.where(low_lanes, pltpu.roll(value[0], half, 1), value[1])
                    out[2 * a + top, branch, local, :] = even + odd
                    out[2 * (a + groups) + top, branch, local, :] = even - odd
            return carry

        lax.fori_loop(0, half // sub, back, 0)


def call(kernel, shape, scratch, operands, smem):
    vmem = pl.BlockSpec(memory_space=pltpu.VMEM)
    specs = [pl.BlockSpec(memory_space=pltpu.SMEM)] * smem + [vmem] * (len(operands) - smem)
    return pl.pallas_call(
        kernel,
        out_shape=jax.ShapeDtypeStruct(shape, jnp.float32),
        in_specs=specs,
        out_specs=vmem,
        scratch_shapes=[pltpu.VMEM(s, jnp.float32) for s in scratch],
        compiler_params=pltpu.CompilerParams(vmem_limit_bytes=28 * 1024 * 1024),
    )(*operands)


def shards(wavefield, freqs, velocity, ref_slow):
    depth = ref_slow.shape[0]
    slab_index = lax.axis_index("slab")
    freq = freqs[0]

    gathered = lax.all_gather(velocity.reshape(depth * rows, -1), "freq", axis=0, tiled=True)
    gathered = gathered.reshape(outer // 2, depth, rows, 2 * inner)

    fy_matrix = forward_y_matrix()
    iy_matrix = inverse_y_matrix()
    fx_matrix = x_matrix(-1)
    ix_matrix = x_matrix(1)
    turn_y = y_turns()
    turn_x = x_turns()
    turn_lane = lane_turns()

    lanes = jnp.arange(inner, dtype=jnp.int32) % half
    number = slab_index // 2 + outer * (half * (slab_index % 2) + lanes)
    fy = jnp.minimum(number, length - number).astype(jnp.float32) / length
    square_y = jnp.broadcast_to((fy * fy)[None, :], (sub, inner))

    packed = (parts, rows, inner)
    spectrum_shape = (outer, rows, 2 * inner)
    sent = call(
        start_kernel,
        packed,
        [spectrum_shape],
        (wavefield[0, 0], wavefield[1, 0], *fy_matrix, *turn_y),
        0,
    )
    for level in range(depth):
        lower, upper = ref_slow[level, 0], ref_slow[level, 1]
        arrived = lax.all_to_all(sent, "slab", split_axis=0, concat_axis=0, tiled=True)
        shifted = call(
            shift_kernel,
            (parts, 2, rows, inner),
            [(2 * inner, length // 2), (2, 2 * inner, length // 2)],
            (
                jnp.stack([(freq * lower) ** 2, (freq * upper) ** 2]),
                square_y,
                arrived.reshape(length, inner),
                *fx_matrix,
                *ix_matrix,
                *turn_x,
                *turn_lane,
            ),
            1,
        )
        moved = lax.all_to_all(shifted, "slab", split_axis=0, concat_axis=0, tiled=True)
        turn = two_pi * depth_step * freq * (lower - upper)
        scalars = jnp.stack([freq, lower, 1.0 / (upper - lower), jnp.cos(turn), jnp.sin(turn)])
        last = level == depth - 1

        def kernel(*refs, last=last):
            combine_kernel(last, *refs)

        sent = call(
            kernel,
            (2, rows, length) if last else packed,
            [(2, *spectrum_shape), (4, rows, length), spectrum_shape],
            (scalars, moved, gathered[:, level], *iy_matrix, *fy_matrix, *turn_y),
            1,
        )
    return sent[:, None]


def solution(mesh):
    return jax.shard_map(
        shards,
        mesh=mesh,
        in_specs=(P(None, "freq", "slab", None), P("freq"), P(None, "slab", "freq"), P()),
        out_specs=P(None, "freq", "slab", None),
        check_vma=False,
    )
```

time: 751 us -> 365 us (0.49)
  the two profiles are of different devices: /device:TPU:2 before, /device:TPU:9 now
where the time goes in v1:
time: 365 us; the launch traced here: 364 us
  waiting for transfers between devices  234 us (64%)
  starting transfers between devices  44.7 us (12%)
  Pallas kernels  39.9 us (11%)
  between operations  26.3 us (7%)
  local copies, waits for them, and re-layouts  19.1 us (5%)
    all_to_all x3, waiting for transfers between devices, shards(): lax.all_to_all(shifted, 'slab', split_axis=0, concat_axis=0, tiled=True)  94.8 us
    all_to_all x3, waiting for transfers between devices, shards(): lax.all_to_all(sent, 'slab', split_axis=0, concat_axis=0, tiled=True)  78.9 us
    all_gather x1, waiting for transfers between devices, shards(): lax.all_gather(velocity.reshape(depth * rows, -1), 'freq', axis=0, tiled=...  59.7 us
    pallas_call x7, Pallas kernels, call(): pl.pallas_call(kernel, out_shape=jax.ShapeDtypeStruct(shape, jnp.float32)...  39.9 us
    all_to_all x3, starting transfers between devices, shards(): lax.all_to_all(sent, 'slab', split_axis=0, concat_axis=0, tiled=True)  27.3 us
    all_to_all x3, starting transfers between devices, shards(): lax.all_to_all(shifted, 'slab', split_axis=0, concat_axis=0, tiled=True)  17.3 us
    unnamed x84, local copies, waits for them, and re-layouts  11.3 us
  transfers between devices with their start and end apart: 7, of which 6 were waited for; matrix products, arithmetic and copies ran while one was open for 2% of the time, Pallas kernels for 0%

profile of v1, /device:TPU:9, one launch (start us, length us, event | category | flops | bytes accessed | tf_op | source)
XLA Modules:
  0.0 364.4 jit_solution(7514092648982784005)
XLA Ops:
  6.5 1.3 slice_bitcast_fusion.3
  8.0 1.9 shard_map.172
  9.9 11.8 %all-to-all-start = ((f32[32,64,128]{2,1,0:T(8,128)}), f32[32,64,128]{2,1,0:T(8,128)S(1)}, u32[]{:S(2)}, u32[]{:S(2)}) async-start(f32[32,64,128]{2,1,0:T(8,128)} %shard_map.172), calls=%async_computation | async-start | bytes 2097152 | tf_op jit(solution)/shard_map/all_to_all | solution.py:464
  24.4 24.9 %all-to-all-done = f32[32,64,128]{2,1,0:T(8,128)S(1)} async-done(((f32[32,64,128]{2,1,0:T(8,128)}), f32[32,64,128]{2,1,0:T(8,128)S(1)}, u32[]{:S(2)}, u32[]{:S(2)}) %all-to-all-start) | async-done | bytes 1048608 | tf_op jit(solution)/shard_map/all_to_all | solution.py:464
  49.4 8.3 %shard_map.173 = f32[32,2,64,128]{3,2,1,0:T(8,128)S(1)} custom-call(f32[2]{0:T(128)S(1)} %pad_maximum_fusion.2.scalars, f32[8,128]{1,0:T(8,128)S(1)} %broadcast_in_dim.4.square_y, f32[2048,128]{1,0:T(8,128)S(1)} %bitcast.56, bf16[256,256]{1,0:T(8,128)(2,1)S(1)} %copy-done.16, bf16[256,256]{1,0:T(8,128)(2,1)S(1)} %copy-done.19, ...), custom_call_target="tpu_custom_call" | custom-call | tf_op jit(solution)/shard_map/pallas_call | solution.py:422
  57.7 1.3 copy-done
  59.1 6.4 %all-to-all-start.1 = ((f32[32,2,64,128]{3,2,1,0:T(8,128)}), f32[32,2,64,128]{3,2,1,0:T(8,128)S(1)}, u32[]{:S(2)}, u32[]{:S(2)}) async-start(f32[32,2,64,128]{3,2,1,0:T(8,128)} %copy-done), calls=%async_computation.1 | async-start | bytes 4194304 | tf_op jit(solution)/shard_map/all_to_all | solution.py:480
  69.0 1.3 stack.80.refs_0_
  70.3 59.7 %all-gather.2.cloned.1.call-done = f32[1536,256]{1,0:T(8,128)} async-done(((f32[192,256]{1,0:T(8,128)}), f32[1536,256]{1,0:T(8,128)}) %all-gather.2.cloned.1.call-update) | async-done | bytes 1572880 | tf_op jit(solution)/shard_map/all_gather | solution.py:437
  130.0 2.5 slice_bitcast_fusion
  132.5 1.0 copy-done.11
  133.6 0.9 copy-done.13
  135.1 4.3 %shard_map.174 = f32[32,64,128]{2,1,0:T(8,128)S(1)} custom-call(f32[5]{0:T(128)S(1)} %copy-done.39, f32[32,2,64,128]{3,2,1,0:T(8,128)S(1)} %all-to-all-done.1.refs_1_, f32[8,64,256]{2,1,0:T(8,128)S(1)} %copy-done.11, bf16[256,256]{1,0:T(8,128)(2,1)S(1)} %copy-done.12, bf16[256,256]{1,0:T(8,128)(2,1)S(1)} %copy-done.13, bf16[256,256]{1,0:T(8,128)(2,1)S(1)} %copy-done.7, ...), custom_call_target="tpu_custom_call" | custom-call | tf_op jit(solution)/shard_map/pallas_call | solution.py:422
  139.5 1.0 copy-done.6
  140.5 9.3 %all-to-all-start.2 = ((f32[32,64,128]{2,1,0:T(8,128)}), f32[32,64,128]{2,1,0:T(8,128)S(1)}, u32[]{:S(2)}, u32[]{:S(2)}) async-start(f32[32,64,128]{2,1,0:T(8,128)} %copy-done.6), calls=%async_computation.2 | async-start | bytes 2097152 | tf_op jit(solution)/shard_map/all_to_all | solution.py:464
  151.2 27.3 %all-to-all-done.2 = f32[32,64,128]{2,1,0:T(8,128)S(1)} async-done(((f32[32,64,128]{2,1,0:T(8,128)}), f32[32,64,128]{2,1,0:T(8,128)S(1)}, u32[]{:S(2)}, u32[]{:S(2)}) %all-to-all-start.2) | async-done | bytes 1048608 | tf_op jit(solution)/shard_map/all_to_all | solution.py:464
  178.5 8.3 %shard_map.175 = f32[32,2,64,128]{3,2,1,0:T(8,128)S(1)} custom-call(f32[2]{0:T(128)S(1)} %pad_maximum_fusion.1.scalars, f32[8,128]{1,0:T(8,128)S(1)} %copy-done.31, f32[2048,128]{1,0:T(8,128)S(1)} %bitcast.58, bf16[256,256]{1,0:T(8,128)(2,1)S(1)} %copy-done.17, bf16[256,256]{1,0:T(8,128)(2,1)S(1)} %copy-done.20, bf16[256,256]{1,0:T(8,128)(2,1)S(1)} %copy-done.23, ...), custom_call_target="tpu_custom_call" | custom-call | tf_op jit(solution)/shard_map/pallas_call | solution.py:422
  186.9 1.3 copy-done.2
  188.2 5.5 %all-to-all-start.3 = ((f32[32,2,64,128]{3,2,1,0:T(8,128)}), f32[32,2,64,128]{3,2,1,0:T(8,128)S(1)}, u32[]{:S(2)}, u32[]{:S(2)}) async-start(f32[32,2,64,128]{3,2,1,0:T(8,128)} %copy-done.2), calls=%async_computation.3 | async-start | bytes 4194304 | tf_op jit(solution)/shard_map/all_to_all | solution.py:480
  196.4 1.3 stack.73.refs_0_
  197.7 47.1 %all-to-all-done.3.refs_1_ = f32[32,2,64,128]{3,2,1,0:T(8,128)S(1)} async-done(((f32[32,2,64,128]{3,2,1,0:T(8,128)}), f32[32,2,64,128]{3,2,1,0:T(8,128)S(1)}, u32[]{:S(2)}, u32[]{:S(2)}) %all-to-all-start.3) | async-done | bytes 2097184 | tf_op jit(solution)/shard_map/all_to_all | solution.py:480
  244.8 1.0 copy-done.10
  245.8 0.9 copy-done.14
  247.3 4.3 %shard_map.176 = f32[32,64,128]{2,1,0:T(8,128)S(1)} custom-call(f32[5]{0:T(128)S(1)} %copy-done.40, f32[32,2,64,128]{3,2,1,0:T(8,128)S(1)} %all-to-all-done.3.refs_1_, f32[8,64,256]{2,1,0:T(8,128)S(1)} %copy-done.10, bf16[256,256]{1,0:T(8,128)(2,1)S(1)} %copy-done.12, bf16[256,256]{1,0:T(8,128)(2,1)S(1)} %copy-done.14, bf16[256,256]{1,0:T(8,128)(2,1)S(1)} %copy-done.7, ...), custom_call_target="tpu_custom_call" | custom-call | tf_op jit(solution)/shard_map/pallas_call | solution.py:422
  251.7 1.0 copy-done.5
  252.7 6.2 %all-to-all-start.4 = ((f32[32,64,128]{2,1,0:T(8,128)}), f32[32,64,128]{2,1,0:T(8,128)S(1)}, u32[]{:S(2)}, u32[]{:S(2)}) async-start(f32[32,64,128]{2,1,0:T(8,128)} %copy-done.5), calls=%async_computation.4 | async-start | bytes 2097152 | tf_op jit(solution)/shard_map/all_to_all | solution.py:464
  260.2 26.7 %all-to-all-done.4 = f32[32,64,128]{2,1,0:T(8,128)S(1)} async-done(((f32[32,64,128]{2,1,0:T(8,128)}), f32[32,64,128]{2,1,0:T(8,128)S(1)}, u32[]{:S(2)}, u32[]{:S(2)}) %all-to-all-start.4) | async-done | bytes 1048608 | tf_op jit(solution)/shard_map/all_to_all | solution.py:464
  287.0 8.3 %shard_map.177 = f32[32,2,64,128]{3,2,1,0:T(8,128)S(1)} custom-call(f32[2]{0:T(128)S(1)} %pad_maximum_fusion.scalars, f32[8,128]{1,0:T(8,128)S(1)} %copy-done.32, f32[2048,128]{1,0:T(8,128)S(1)} %bitcast.57, bf16[256,256]{1,0:T(8,128)(2,1)S(1)} %copy-done.18, bf16[256,256]{1,0:T(8,128)(2,1)S(1)} %copy-done.21, bf16[256,256]{1,0:T(8,128)(2,1)S(1)} %copy-done.24, ...), custom_call_target="tpu_custom_call" | custom-call | tf_op jit(solution)/shard_map/pallas_call | solution.py:422
  295.3 1.3 copy-done.1
  296.7 5.4 %all-to-all-start.5 = ((f32[32,2,64,128]{3,2,1,0:T(8,128)}), f32[32,2,64,128]{3,2,1,0:T(8,128)S(1)}, u32[]{:S(2)}, u32[]{:S(2)}) async-start(f32[32,2,64,128]{3,2,1,0:T(8,128)} %copy-done.1), calls=%async_computation.5 | async-start | bytes 4194304 | tf_op jit(solution)/shard_map/all_to_all | solution.py:480
  305.4 47.7 %all-to-all-done.5.refs_1_ = f32[32,2,64,128]{3,2,1,0:T(8,128)S(1)} async-done(((f32[32,2,64,128]{3,2,1,0:T(8,128)}), f32[32,2,64,128]{3,2,1,0:T(8,128)S(1)}, u32[]{:S(2)}, u32[]{:S(2)}) %all-to-all-start.5) | async-done | bytes 2097184 | tf_op jit(solution)/shard_map/all_to_all | solution.py:480
  353.1 4.4 %shard_map.178 = f32[2,64,2048]{2,1,0:T(8,128)} custom-call(f32[5]{0:T(128)S(1)} %stack.66.refs_0_, f32[32,2,64,128]{3,2,1,0:T(8,128)S(1)} %all-to-all-done.5.refs_1_, f32[8,64,256]{2,1,0:T(8,128)S(1)} %copy-done.9, bf16[256,256]{1,0:T(8,128)(2,1)S(1)} %copy-done.12, bf16[256,256]{1,0:T(8,128)(2,1)S(1)} %copy-done.15, bf16[256,256]{1,0:T(8,128)(2,1)S(1)} %copy-done.7, ...), custom_call_target="tpu_custom_call" | custom-call | tf_op jit(solution)/shard_map/pallas_call | solution.py:422
  (85 shorter events, 3.8 us)
Async XLA Ops:
  7.9 41.4 %copy-start.3 = (f32[8,128,128]{2,1,0:T(8,128)S(1)}, f32[8,128,128]{2,1,0:T(8,128)}, u32[]{:S(2)}) copy-start(f32[8,128,128]{2,1,0:T(8,128)} %constant.90.clone.turn_cos) | copy-start | bytes 1572868
  8.0 41.3 %copy-start.4 = (f32[8,128,128]{2,1,0:T(8,128)S(1)}, f32[8,128,128]{2,1,0:T(8,128)}, u32[]{:S(2)}) copy-start(f32[8,128,128]{2,1,0:T(8,128)} %constant.91.clone.turn_sin) | copy-start | bytes 1572868
  8.0 41.3 %copy-start.16 = (bf16[256,256]{1,0:T(8,128)(2,1)S(1)}, bf16[256,256]{1,0:T(8,128)(2,1)}, u32[]{:S(2)}) copy-start(bf16[256,256]{1,0:T(8,128)(2,1)} %constant.86.clone.there_high) | copy-start | bytes 393220
  8.0 41.3 %copy-start.19 = (bf16[256,256]{1,0:T(8,128)(2,1)S(1)}, bf16[256,256]{1,0:T(8,128)(2,1)}, u32[]{:S(2)}) copy-start(bf16[256,256]{1,0:T(8,128)(2,1)} %constant.87.clone.there_low) | copy-start | bytes 393220
  8.0 41.3 %copy-start.22 = (bf16[256,256]{1,0:T(8,128)(2,1)S(1)}, bf16[256,256]{1,0:T(8,128)(2,1)}, u32[]{:S(2)}) copy-start(bf16[256,256]{1,0:T(8,128)(2,1)} %constant.88.clone.back_high) | copy-start | bytes 393220
  8.0 41.3 %copy-start.25 = (bf16[256,256]{1,0:T(8,128)(2,1)S(1)}, bf16[256,256]{1,0:T(8,128)(2,1)}, u32[]{:S(2)}) copy-start(bf16[256,256]{1,0:T(8,128)(2,1)} %constant.89.clone.back_low) | copy-start | bytes 393220
  8.0 41.3 %copy-start.33 = (f32[8,128]{1,0:T(8,128)S(1)}, f32[8,128]{1,0:T(8,128)}, u32[]{:S(2)}) copy-start(f32[8,128]{1,0:T(8,128)} %constant.92.clone.lane_cos) | copy-start | bytes 12292
  8.0 41.3 %copy-start.36 = (f32[8,128]{1,0:T(8,128)S(1)}, f32[8,128]{1,0:T(8,128)}, u32[]{:S(2)}) copy-start(f32[8,128]{1,0:T(8,128)} %constant.93.clone.lane_sin) | copy-start | bytes 12292
  9.9 39.4 %all-to-all-start = ((f32[32,64,128]{2,1,0:T(8,128)}), f32[32,64,128]{2,1,0:T(8,128)S(1)}, u32[]{:S(2)}, u32[]{:S(2)}) async-start(f32[32,64,128]{2,1,0:T(8,128)} %shard_map.172), calls=%async_computation | async-start | bytes 2097152 | tf_op jit(solution)/shard_map/all_to_all | solution.py:464
  59.1 73.5 %all-to-all-start.1 = ((f32[32,2,64,128]{3,2,1,0:T(8,128)}), f32[32,2,64,128]{3,2,1,0:T(8,128)S(1)}, u32[]{:S(2)}, u32[]{:S(2)}) async-start(f32[32,2,64,128]{3,2,1,0:T(8,128)} %copy-done), calls=%async_computation.1 | async-start | bytes 4194304 | tf_op jit(solution)/shard_map/all_to_all | solution.py:480
  65.5 67.0 %copy-start.12 = (bf16[256,256]{1,0:T(8,128)(2,1)S(1)}, bf16[256,256]{1,0:T(8,128)(2,1)}, u32[]{:S(2)}) copy-start(bf16[256,256]{1,0:T(8,128)(2,1)} %constant.94.clone.refs_3_) | copy-start | bytes 393220
  65.5 64.5 %all-gather.2.cloned.1.call-start = ((), (), s32[]{:S(2)}) async-start(), calls=%async_computation.6 | async-start | bytes 1769472 | tf_op jit(solution)/shard_map/all_gather | solution.py:437
  140.4 38.0 %copy-start.17 = (bf16[256,256]{1,0:T(8,128)(2,1)S(1)}, bf16[256,256]{1,0:T(8,128)(2,1)}, u32[]{:S(2)}) copy-start(bf16[256,256]{1,0:T(8,128)(2,1)} %constant.86.clone.there_high) | copy-start | bytes 393220
  140.4 38.0 %copy-start.20 = (bf16[256,256]{1,0:T(8,128)(2,1)S(1)}, bf16[256,256]{1,0:T(8,128)(2,1)}, u32[]{:S(2)}) copy-start(bf16[256,256]{1,0:T(8,128)(2,1)} %constant.87.clone.there_low) | copy-start | bytes 393220
  140.4 38.0 %copy-start.23 = (bf16[256,256]{1,0:T(8,128)(2,1)S(1)}, bf16[256,256]{1,0:T(8,128)(2,1)}, u32[]{:S(2)}) copy-start(bf16[256,256]{1,0:T(8,128)(2,1)} %constant.88.clone.back_high) | copy-start | bytes 393220
  140.4 38.0 %copy-start.26 = (bf16[256,256]{1,0:T(8,128)(2,1)S(1)}, bf16[256,256]{1,0:T(8,128)(2,1)}, u32[]{:S(2)}) copy-start(bf16[256,256]{1,0:T(8,128)(2,1)} %constant.89.clone.back_low) | copy-start | bytes 393220
  140.4 38.1 %copy-start.31 = (f32[8,128]{1,0:T(8,128)S(1)}, f32[8,128]{1,0:T(8,128)}, u32[]{:S(2)}) copy-start(f32[8,128]{1,0:T(8,128)} %copy-done.30) | copy-start | bytes 12292
  140.5 38.1 %copy-start.34 = (f32[8,128]{1,0:T(8,128)S(1)}, f32[8,128]{1,0:T(8,128)}, u32[]{:S(2)}) copy-start(f32[8,128]{1,0:T(8,128)} %constant.92.clone.lane_cos) | copy-start | bytes 12292
  140.5 38.0 %copy-start.37 = (f32[8,128]{1,0:T(8,128)S(1)}, f32[8,128]{1,0:T(8,128)}, u32[]{:S(2)}) copy-start(f32[8,128]{1,0:T(8,128)} %constant.93.clone.lane_sin) | copy-start | bytes 12292
  140.5 38.0 %all-to-all-start.2 = ((f32[32,64,128]{2,1,0:T(8,128)}), f32[32,64,128]{2,1,0:T(8,128)S(1)}, u32[]{:S(2)}, u32[]{:S(2)}) async-start(f32[32,64,128]{2,1,0:T(8,128)} %copy-done.6), calls=%async_computation.2 | async-start | bytes 2097152 | tf_op jit(solution)/shard_map/all_to_all | solution.py:464
  188.2 56.6 %all-to-all-start.3 = ((f32[32,2,64,128]{3,2,1,0:T(8,128)}), f32[32,2,64,128]{3,2,1,0:T(8,128)S(1)}, u32[]{:S(2)}, u32[]{:S(2)}) async-start(f32[32,2,64,128]{3,2,1,0:T(8,128)} %copy-done.2), calls=%async_computation.3 | async-start | bytes 4194304 | tf_op jit(solution)/shard_map/all_to_all | solution.py:480
  252.6 34.3 %copy-start.18 = (bf16[256,256]{1,0:T(8,128)(2,1)S(1)}, bf16[256,256]{1,0:T(8,128)(2,1)}, u32[]{:S(2)}) copy-start(bf16[256,256]{1,0:T(8,128)(2,1)} %constant.86.clone.there_high) | copy-start | bytes 393220
  252.6 34.3 %copy-start.21 = (bf16[256,256]{1,0:T(8,128)(2,1)S(1)}, bf16[256,256]{1,0:T(8,128)(2,1)}, u32[]{:S(2)}) copy-start(bf16[256,256]{1,0:T(8,128)(2,1)} %constant.87.clone.there_low) | copy-start | bytes 393220
  252.6 34.3 %copy-start.24 = (bf16[256,256]{1,0:T(8,128)(2,1)S(1)}, bf16[256,256]{1,0:T(8,128)(2,1)}, u32[]{:S(2)}) copy-start(bf16[256,256]{1,0:T(8,128)(2,1)} %constant.88.clone.back_high) | copy-start | bytes 393220
  252.6 34.3 %copy-start.27 = (bf16[256,256]{1,0:T(8,128)(2,1)S(1)}, bf16[256,256]{1,0:T(8,128)(2,1)}, u32[]{:S(2)}) copy-start(bf16[256,256]{1,0:T(8,128)(2,1)} %constant.89.clone.back_low) | copy-start | bytes 393220
  252.7 34.3 %copy-start.32 = (f32[8,128]{1,0:T(8,128)S(1)}, f32[8,128]{1,0:T(8,128)}, u32[]{:S(2)}) copy-start(f32[8,128]{1,0:T(8,128)} %copy-done.30) | copy-start | bytes 12292
  252.7 34.3 %copy-start.35 = (f32[8,128]{1,0:T(8,128)S(1)}, f32[8,128]{1,0:T(8,128)}, u32[]{:S(2)}) copy-start(f32[8,128]{1,0:T(8,128)} %constant.92.clone.lane_cos) | copy-start | bytes 12292
  252.7 34.3 %copy-start.38 = (f32[8,128]{1,0:T(8,128)S(1)}, f32[8,128]{1,0:T(8,128)}, u32[]{:S(2)}) copy-start(f32[8,128]{1,0:T(8,128)} %constant.93.clone.lane_sin) | copy-start | bytes 12292
  252.7 34.2 %all-to-all-start.4 = ((f32[32,64,128]{2,1,0:T(8,128)}), f32[32,64,128]{2,1,0:T(8,128)S(1)}, u32[]{:S(2)}, u32[]{:S(2)}) async-start(f32[32,64,128]{2,1,0:T(8,128)} %copy-done.5), calls=%async_computation.4 | async-start | bytes 2097152 | tf_op jit(solution)/shard_map/all_to_all | solution.py:464
  296.7 56.5 %copy-start.9 = (f32[8,64,256]{2,1,0:T(8,128)S(1)}, f32[8,64,256]{2,1,0:T(8,128)}, u32[]{:S(2)}) copy-start(f32[8,64,256]{2,1,0:T(8,128)} %get-tuple-element.5.refs_2_) | copy-start | bytes 1572868
  296.7 56.5 %copy-start.15 = (bf16[256,256]{1,0:T(8,128)(2,1)S(1)}, bf16[256,256]{1,0:T(8,128)(2,1)}, u32[]{:S(2)}) copy-start(bf16[256,256]{1,0:T(8,128)(2,1)} %constant.95.clone.refs_4_) | copy-start | bytes 393220
  296.7 56.5 %all-to-all-start.5 = ((f32[32,2,64,128]{3,2,1,0:T(8,128)}), f32[32,2,64,128]{3,2,1,0:T(8,128)S(1)}, u32[]{:S(2)}, u32[]{:S(2)}) async-start(f32[32,2,64,128]{3,2,1,0:T(8,128)} %copy-done.1), calls=%async_computation.5 | async-start | bytes 4194304 | tf_op jit(solution)/shard_map/all_to_all | solution.py:480
  (17 other events, 39.5 us)
Sparse Core Ops, SparseCore 0:
  68.1 61.8 all-gather.1

commit v2 on v1

--- a/solution.py
+++ b/solution.py
@@ -1,3 +1,4 @@
+import functools
 import math
 
 import jax
@@ -18,6 +19,7 @@
 rows = 64
 parts = 32
 sub = 8
+tile_count = 8
 
 
 def split_bf16(matrix):
@@ -183,6 +185,15 @@
     return product(a_high, b_high) + (product(a_high, b_low) + product(a_low, b_high))
 
 
+def folded(number):
+    return jnp.minimum(number, length - number).astype(jnp.float32) * (1.0 / length)
+
+
+def tile_of(me, n):
+    group = me // 4 if n < 4 else 1 - me // 4
+    return 4 * group + (me + 4 - n % 4) % 4
+
+
 def block_rows(step):
     return pl.ds(pl.multiple_of(step * sub, sub), sub)
 
@@ -209,19 +220,20 @@
             out[2 * (k + n) + 1] = one[:, inner:]
 
 
-def start_kernel(real, imag, matrix_high, matrix_low, turn_cos, turn_sin, out, spectrum):
+def start_kernel(
+    place, freqs, ref_slow, wavefield, matrix_high, matrix_low, turn_cos, turn_sin, out, spectrum
+):
     def read(here, a):
         columns = slice(a * inner, (a + 1) * inner)
-        return real[here, columns], imag[here, columns]
+        return wavefield[0, 0, here, columns], wavefield[1, 0, here, columns]
 
     forward_y(read, out, spectrum, matrix_high, matrix_low, turn_cos, turn_sin)
 
 
 def combine_kernel(
     last,
-    scalars,
     moved,
-    velocity,
+    weights,
     back_high,
     back_low,
     matrix_high,
@@ -230,11 +242,9 @@
     turn_sin,
     out,
     fields,
-    weighted,
+    summed,
     spectrum,
 ):
-    freq, lower, inverse_gap, turn_real, turn_imag = (scalars[n] for n in range(5))
-
     matrix = (back_high[...], back_low[...])
     for branch in range(2):
         for k in range(0, outer, 4):
@@ -248,24 +258,6 @@
             result = mix(cut(block), matrix)
             fields[branch, k : k + 4] = result.reshape(4, rows, 2 * inner)
 
-    def weigh(c, carry):
-        here = block_rows(c)
-        for a in range(outer):
-            speed = velocity[a // 2, here, (a % 2) * inner : (a % 2 + 1) * inner]
-            slowness = 1.0 / speed
-            excess = slowness - lower
-            upper_weight = jnp.clip(excess * inverse_gap, 0.0, 1.0)
-            lower_weight = 1.0 - upper_weight
-            cosine, sine = cis((depth_step * freq) * excess)
-            columns = slice(a * inner, (a + 1) * inner)
-            weighted[0, here, columns] = lower_weight * cosine
-            weighted[1, here, columns] = lower_weight * sine
-            weighted[2, here, columns] = upper_weight * (cosine * turn_real - sine * turn_imag)
-            weighted[3, here, columns] = upper_weight * (cosine * turn_imag + sine * turn_real)
-        return carry
-
-    lax.fori_loop(0, rows // sub, weigh, 0)
-
     def back(c, carry):
         here = block_rows(c)
         for branch in range(2):
@@ -277,23 +269,16 @@
             values = dft(values, 1)
             for a in range(outer):
                 columns = slice(a * inner, (a + 1) * inner)
-                weight = (weighted[2 * branch, here, columns], weighted[2 * branch + 1, here, columns])
+                weight = (weights[2 * branch, a, here, :], weights[2 * branch + 1, a, here, :])
                 value = times(values[a], weight)
-                if last:
-                    if branch == 0:
-                        out[0, here, columns] = value[0]
-                        out[1, here, columns] = value[1]
-                    else:
-                        out[0, here, columns] += value[0]
-                        out[1, here, columns] += value[1]
+                if branch == 1:
+                    value = plus(value, (summed[0, a, here, :], summed[1, a, here, :]))
+                if last and branch == 1:
+                    out[0, 0, here, columns] = value[0]
+                    out[1, 0, here, columns] = value[1]
                 else:
-                    if branch == 1:
-                        value = (
-                            value[0] + weighted[0, here, columns],
-                            value[1] + weighted[1, here, columns],
-                        )
-                    weighted[0, here, columns] = value[0]
-                    weighted[1, here, columns] = value[1]
+                    summed[0, a, here, :] = value[0]
+                    summed[1, a, here, :] = value[1]
         return carry
 
     lax.fori_loop(0, rows // sub, back, 0)
@@ -301,15 +286,106 @@
         return
 
     def read(here, a):
-        columns = slice(a * inner, (a + 1) * inner)
-        return weighted[0, here, columns], weighted[1, here, columns]
+        return summed[0, a, here, :], summed[1, a, here, :]
 
     forward_y(read, out, spectrum, matrix_high, matrix_low, turn_cos, turn_sin)
 
 
-def shift_kernel(
-    scalars,
-    square_y,
+def weigh(level, place, freqs, ref_slow, tiles, weights):
+    def full(value):
+        return jnp.full((sub, inner), value, jnp.float32)
+
+    lower, upper = full(ref_slow[level, 0]), full(ref_slow[level, 1])
+    pace = depth_step * full(freqs[0])
+    inverse_gap = 1.0 / (upper - lower)
+    turn = cis(pace * (lower - upper))
+
+    def step(c, carry):
+        here = block_rows(c)
+        for n in range(outer):
+            slowness = 1.0 / tiles[n // 2][level, here, (n % 2) * inner : (n % 2 + 1) * inner]
+            excess = slowness - lower
+            upper_weight = jnp.clip(excess * inverse_gap, 0.0, 1.0)
+            lower_weight = 1.0 - upper_weight
+            phase = cis(pace * excess)
+            other = times(phase, turn)
+            a = 2 * tile_of(place[0], n // 2) + n % 2
+            weights[0, a, here, :] = lower_weight * phase[0]
+            weights[1, a, here, :] = lower_weight * phase[1]
+            weights[2, a, here, :] = upper_weight * other[0]
+            weights[3, a, here, :] = upper_weight * other[1]
+        return carry
+
+    lax.fori_loop(0, rows // sub, step, 0)
+
+
+def propagators(level, place, freqs, ref_slow):
+    lane = lax.broadcasted_iota(jnp.int32, (sub, inner), 1)
+    sub_row = lax.broadcasted_iota(jnp.int32, (sub, inner), 0)
+    fy = folded(place[1] // 2 + outer * (half * (place[1] % 2) + lane % half))
+    fy = fy * fy
+    squares = []
+    for branch in range(2):
+        wave = jnp.full((sub, inner), freqs[0]) * jnp.full((sub, inner), ref_slow[level, branch])
+        squares.append(wave * wave)
+
+    def at(c, k):
+        fx = folded(2 * k + jnp.where(lane < half, 0, 1) + outer * (c * sub + sub_row))
+        square = fx * fx + fy
+        shifts = []
+        for branch in range(2):
+            target = squares[branch] - square
+            cycles = depth_step * jnp.sqrt(jnp.abs(target))
+            cosine, sine = cis(cycles)
+            live = target >= 0
+            shifts.append(
+                (
+                    jnp.where(live, cosine, jnp.exp(-two_pi * cycles)),
+                    jnp.where(live, sine, 0.0),
+                )
+            )
+        return shifts
+
+    return at
+
+
+def tables_kernel(depth, place, freqs, ref_slow, *refs):
+    tiles, refs = refs[:tile_count], refs[tile_count:]
+    for level in range(depth):
+        weigh(level, place, freqs, ref_slow, tiles, refs[level])
+    for level in range(1, depth):
+        at = propagators(level, place, freqs, ref_slow)
+        table = refs[depth + level - 1]
+
+        def step(c, carry, at=at, table=table):
+            here = block_rows(c)
+            second_half = pl.ds(pl.multiple_of(inner + c * sub, sub), sub)
+            for k in range(outer // 2):
+                columns = slice(k * inner, (k + 1) * inner)
+                for branch, shift in enumerate(at(c, k)):
+                    table[branch, here, columns] = shift[0]
+                    table[branch, second_half, columns] = shift[1]
+            return carry
+
+        lax.fori_loop(0, inner // sub, step, 0)
+
+
+def first_shift_kernel(place, freqs, ref_slow, *refs):
+    shift(propagators(0, place, freqs, ref_slow), *refs)
+
+
+def later_shift_kernel(table, *refs):
+    def at(c, k):
+        here = block_rows(c)
+        second_half = pl.ds(pl.multiple_of(inner + c * sub, sub), sub)
+        columns = slice(k * inner, (k + 1) * inner)
+        return [(table[n, here, columns], table[n, second_half, columns]) for n in range(2)]
+
+    shift(at, *refs)
+
+
+def shift(
+    propagators_at,
     arrived,
     there_high,
     there_low,
@@ -356,28 +432,14 @@
         columns = slice(n * 2 * inner, (n + 1) * 2 * inner)
         spectrum[:, columns] = mix(matrix, cut(spectrum[:, columns]))
 
-    sub_row = lax.broadcasted_iota(jnp.int32, (sub, inner), 0)
-    fy = square_y[0:1, :]
-
     def propagate(c, carry):
         here = block_rows(c)
         second_half = pl.ds(pl.multiple_of(inner + c * sub, sub), sub)
         for k in range(groups):
-            number = 2 * k + jnp.where(low_lanes, 0, 1) + outer * (c * sub + sub_row)
-            fx = jnp.minimum(number, length - number).astype(jnp.float32) * (1.0 / length)
-            square = fx * fx + fy
             columns = slice(k * inner, (k + 1) * inner)
             value = (spectrum[here, columns], spectrum[second_half, columns])
-            for branch in range(2):
-                target = scalars[branch] - square
-                cycles = depth_step * jnp.sqrt(jnp.abs(target))
-                cosine, sine = cis(cycles)
-                live = target >= 0
-                shift = (
-                    jnp.where(live, cosine, jnp.exp(-two_pi * cycles)),
-                    jnp.where(live, sine, 0.0),
-                )
-                moved = times(value, shift)
+            for branch, factor in enumerate(propagators_at(c, k)):
+                moved = times(value, factor)
                 shifted[branch, here, columns] = moved[0]
                 shifted[branch, second_half, columns] = moved[1]
         return carry
@@ -416,26 +478,39 @@
         lax.fori_loop(0, half // sub, back, 0)
 
 
-def call(kernel, shape, scratch, operands, smem):
+def call(kernel, shapes, scratch, scalars, operands):
     vmem = pl.BlockSpec(memory_space=pltpu.VMEM)
-    specs = [pl.BlockSpec(memory_space=pltpu.SMEM)] * smem + [vmem] * (len(operands) - smem)
+    smem = pl.BlockSpec(memory_space=pltpu.SMEM)
     return pl.pallas_call(
         kernel,
-        out_shape=jax.ShapeDtypeStruct(shape, jnp.float32),
-        in_specs=specs,
-        out_specs=vmem,
+        out_shape=[jax.ShapeDtypeStruct(s, jnp.float32) for s in shapes],
+        in_specs=[smem] * len(scalars) + [vmem] * len(operands),
+        out_specs=[vmem] * len(shapes),
         scratch_shapes=[pltpu.VMEM(s, jnp.float32) for s in scratch],
         compiler_params=pltpu.CompilerParams(vmem_limit_bytes=28 * 1024 * 1024),
-    )(*operands)
+    )(*scalars, *operands)
+
+
+def velocity_tiles(velocity):
+    other = lax.ppermute(velocity, "freq", [(n, (n + 4) % 8) for n in range(8)])
+    tiles = []
+    for tile in (velocity, other):
+        tiles.append(tile)
+        for back in range(1, 4):
+            pairs = [(n, n // 4 * 4 + (n + back) % 4) for n in range(8)]
+            tiles.append(lax.ppermute(tile, "freq", pairs))
+    return tiles
+
+
+def exchange(values):
+    return lax.all_to_all(values, "slab", split_axis=0, concat_axis=0, tiled=True)
 
 
 def shards(wavefield, freqs, velocity, ref_slow):
     depth = ref_slow.shape[0]
-    slab_index = lax.axis_index("slab")
-    freq = freqs[0]
-
-    gathered = lax.all_gather(velocity.reshape(depth * rows, -1), "freq", axis=0, tiled=True)
-    gathered = gathered.reshape(outer // 2, depth, rows, 2 * inner)
+    place = jnp.stack([lax.axis_index("freq"), lax.axis_index("slab")])
+    common = (place, freqs, ref_slow)
+    tiles = velocity_tiles(velocity)
 
     fy_matrix = forward_y_matrix()
     iy_matrix = inverse_y_matrix()
@@ -445,54 +520,46 @@
     turn_x = x_turns()
     turn_lane = lane_turns()
 
-    lanes = jnp.arange(inner, dtype=jnp.int32) % half
-    number = slab_index // 2 + outer * (half * (slab_index % 2) + lanes)
-    fy = jnp.minimum(number, length - number).astype(jnp.float32) / length
-    square_y = jnp.broadcast_to((fy * fy)[None, :], (sub, inner))
-
     packed = (parts, rows, inner)
     spectrum_shape = (outer, rows, 2 * inner)
-    sent = call(
-        start_kernel,
-        packed,
-        [spectrum_shape],
-        (wavefield[0, 0], wavefield[1, 0], *fy_matrix, *turn_y),
-        0,
+    folded_shape = (2 * inner, length // 2)
+    weights_shape = (4, outer, rows, inner)
+    (sent,) = call(
+        start_kernel, [packed], [spectrum_shape], common, (wavefield, *fy_matrix, *turn_y)
+    )
+    tables = call(
+        functools.partial(tables_kernel, depth),
+        [weights_shape] * depth + [(2, *folded_shape)] * (depth - 1),
+        [],
+        common,
+        velocity_tiles(velocity),
     )
     for level in range(depth):
-        lower, upper = ref_slow[level, 0], ref_slow[level, 1]
-        arrived = lax.all_to_all(sent, "slab", split_axis=0, concat_axis=0, tiled=True)
-        shifted = call(
-            shift_kernel,
-            (parts, 2, rows, inner),
-            [(2 * inner, length // 2), (2, 2 * inner, length // 2)],
+        arrived = exchange(sent).reshape(length, inner)
+        (shifted,) = call(
+            later_shift_kernel if level else first_shift_kernel,
+            [(parts, 2, rows, inner)],
+            [folded_shape, (2, *folded_shape)],
+            () if level else common,
             (
-                jnp.stack([(freq * lower) ** 2, (freq * upper) ** 2]),
-                square_y,
-                arrived.reshape(length, inner),
+                *tables[depth + level - 1 : depth + level][: 1 if level else 0],
+                arrived,
                 *fx_matrix,
                 *ix_matrix,
                 *turn_x,
                 *turn_lane,
             ),
-            1,
         )
-        moved = lax.all_to_all(shifted, "slab", split_axis=0, concat_axis=0, tiled=True)
-        turn = two_pi * depth_step * freq * (lower - upper)
-        scalars = jnp.stack([freq, lower, 1.0 / (upper - lower), jnp.cos(turn), jnp.sin(turn)])
+        moved = exchange(shifted)
         last = level == depth - 1
-
-        def kernel(*refs, last=last):
-            combine_kernel(last, *refs)
-
-        sent = call(
-            kernel,
-            (2, rows, length) if last else packed,
-            [(2, *spectrum_shape), (4, rows, length), spectrum_shape],
-            (scalars, moved, gathered[:, level], *iy_matrix, *fy_matrix, *turn_y),
-            1,
+        (sent,) = call(
+            functools.partial(combine_kernel, last),
+            [(2, 1, rows, length) if last else packed],
+            [(2, *spectrum_shape), (2, outer, rows, inner), spectrum_shape],
+            (),
+            (moved, tables[level], *iy_matrix, *fy_matrix, *turn_y),
         )
-    return sent[:, None]
+    return sent
 
 
 def solution(mesh):

time: 365 us -> 357 us (0.978)
  the two profiles are of different devices: /device:TPU:9 before, /device:TPU:2 now
where the time goes in v2:
time: 357 us; the launch traced here: 354 us
  blocking collectives  223 us (62%)
  waiting for transfers between devices  55.9 us (16%)
  Pallas kernels  40.2 us (11%)
  local copies, waits for them, and re-layouts  16.9 us (5%)
  starting transfers between devices  16.5 us (5%)
    all_to_all x5, blocking collectives, exchange(): lax.all_to_all(values, 'slab', split_axis=0, concat_axis=0, tiled=True)  223 us
    ppermute x1, waiting for transfers between devices, velocity_tiles(): other = lax.ppermute(velocity, 'freq', [(n, (n + 4) % 8) for n in range(8)])  45.6 us
    pallas_call x8, Pallas kernels, call(): pl.pallas_call(kernel, out_shape=[jax.ShapeDtypeStruct(s, jnp.float32) fo...  40.2 us
    unnamed x83, local copies, waits for them, and re-layouts  16.9 us
    ppermute x6, waiting for transfers between devices, velocity_tiles(): tiles.append(lax.ppermute(tile, 'freq', pairs))  10.3 us
    ppermute x6, starting transfers between devices, velocity_tiles(): tiles.append(lax.ppermute(tile, 'freq', pairs))  9.13 us
  transfers between devices with their start and end apart: 8, of which 4 were waited for; matrix products, arithmetic and copies ran while one was open for 0% of the time, Pallas kernels for 3%

profile of v2, /device:TPU:2, one launch (start us, length us, event | category | flops | bytes accessed | tf_op | source)
XLA Modules:
  0.0 353.9 jit_solution(10769203924652824470)
XLA Ops:
  1.5 0.9 copy-done.2
  2.4 0.9 copy-done.4
  3.3 1.2 copy-done.27
  6.0 1.5 shard_map.173
  7.5 38.9 %all_to_all.30 = f32[32,64,128]{2,1,0:T(8,128)S(1)} all-to-all(f32[32,64,128]{2,1,0:T(8,128)S(1)} %shard_map.173), channel_id=1, replica_groups=mesh['freq'=8,'slab'=32] {'slab'}, dimensions={0} | all-to-all | bytes 2097152 | tf_op jit(solution)/shard_map/all_to_all | solution.py:506
  46.5 9.7 %shard_map.174 = f32[32,2,64,128]{3,2,1,0:T(8,128)} custom-call(s32[2]{0:T(128)S(1)} %pad_add_fusion.place, f32[1]{0:T(128)S(6)} %copy.22.freqs, f32[3,2]{1,0:T(4,128)S(1)} %copy.19.ref_slow, f32[2048,128]{1,0:T(8,128)S(1)} %bitcast.5, bf16[256,256]{1,0:T(8,128)(2,1)S(1)} %copy-done.25, bf16[256,256]{1,0:T(8,128)(2,1)S(1)} %copy-done.23, ...), custom_call_target="tpu_custom_call" | custom-call | tf_op jit(solution)/shard_map/pallas_call | solution.py:484
  56.2 6.8 %all-to-all-start.1 = ((f32[32,2,64,128]{3,2,1,0:T(8,128)}), f32[32,2,64,128]{3,2,1,0:T(8,128)S(1)}, u32[]{:S(2)}, u32[]{:S(2)}) async-start(f32[32,2,64,128]{3,2,1,0:T(8,128)} %shard_map.174), calls=%async_computation.1 | async-start | bytes 4194304 | tf_op jit(solution)/shard_map/all_to_all | solution.py:506
  63.6 3.0 collective-permute-start.2
  67.2 1.0 collective-permute-start
  68.1 45.6 %collective-permute-done.3.refs_4_ = f32[3,64,256]{2,1,0:T(8,128)S(1)} collective-permute-done((f32[3,64,256]{2,1,0:T(8,128)}, f32[3,64,256]{2,1,0:T(8,128)S(1)}, u32[]{:S(2)}, u32[]{:S(2)}) %collective-permute-start.3) | collective-permute-done | bytes 196640 | tf_op jit(solution)/shard_map/ppermute | solution.py:495
  113.8 3.0 collective-permute-start.6
  117.4 1.0 collective-permute-start.4
  118.3 6.6 %collective-permute-done.6.refs_7_ = f32[3,64,256]{2,1,0:T(8,128)S(1)} collective-permute-done((f32[3,64,256]{2,1,0:T(8,128)S(1)}, f32[3,64,256]{2,1,0:T(8,128)S(1)}, u32[]{:S(2)}, u32[]{:S(2)}) %collective-permute-start.6) | collective-permute-done | bytes 196640 | tf_op jit(solution)/shard_map/ppermute | solution.py:501
  124.9 1.2 collective-permute-done.5.refs_6_
  126.1 2.5 collective-permute-done.4.refs_5_
  128.6 0.9 copy-done.28
  130.9 8.9 %shard_map.172 = (f32[4,16,64,128]{3,2,1,0:T(8,128)S(1)}, f32[4,16,64,128]{3,2,1,0:T(8,128)S(1)}, f32[4,16,64,128]{3,2,1,0:T(8,128)S(1)}, f32[2,256,1024]{2,1,0:T(8,128)S(1)}, f32[2,256,1024]{2,1,0:T(8,128)S(1)}) custom-call(s32[2]{0:T(128)S(1)} %copy-done.40, f32[1]{0:T(128)S(6)} %copy.22.freqs, f32[3,2]{1,0:T(4,128)S(1)} %copy-done.38, ...), custom_call_target="tpu_custom_call" | custom-call | tf_op jit(solution)/shard_map/pallas_call | solution.py:484
  139.8 1.3 copy-done.6
  141.1 1.3 copy-done.8
  142.5 1.4 copy-done.10
  143.8 1.3 copy-done.12
  145.2 1.4 copy-done.14
  146.6 1.6 copy-done.15
  149.1 3.0 shard_map.175
  152.2 37.9 %all_to_all.31 = f32[32,64,128]{2,1,0:T(8,128)S(1)} all-to-all(f32[32,64,128]{2,1,0:T(8,128)S(1)} %shard_map.175), channel_id=1, replica_groups=mesh['freq'=8,'slab'=32] {'slab'}, dimensions={0} | all-to-all | bytes 2097152 | tf_op jit(solution)/shard_map/all_to_all | solution.py:506
  190.2 5.6 %shard_map.176 = f32[32,2,64,128]{3,2,1,0:T(8,128)S(1)} custom-call(f32[2,256,1024]{2,1,0:T(8,128)S(1)} %copy-done.13, f32[2048,128]{1,0:T(8,128)S(1)} %bitcast.7, bf16[256,256]{1,0:T(8,128)(2,1)S(1)} %copy-done.26, bf16[256,256]{1,0:T(8,128)(2,1)S(1)} %copy-done.24, bf16[256,256]{1,0:T(8,128)(2,1)S(1)} %copy-done.22, bf16[256,256]{1,0:T(8,128)(2,1)S(1)} %copy-done.20, ...), custom_call_target="tpu_custom_call" | custom-call | tf_op jit(solution)/shard_map/pallas_call | solution.py:484
  195.7 56.4 %all_to_all.32.moved = f32[32,2,64,128]{3,2,1,0:T(8,128)S(1)} all-to-all(f32[32,2,64,128]{3,2,1,0:T(8,128)S(1)} %shard_map.176), channel_id=1, replica_groups=mesh['freq'=8,'slab'=32] {'slab'}, dimensions={0} | all-to-all | bytes 4194304 | tf_op jit(solution)/shard_map/all_to_all | solution.py:506
  252.1 3.0 shard_map.177
  255.2 33.8 %all_to_all.33 = f32[32,64,128]{2,1,0:T(8,128)S(1)} all-to-all(f32[32,64,128]{2,1,0:T(8,128)S(1)} %shard_map.177), channel_id=1, replica_groups=mesh['freq'=8,'slab'=32] {'slab'}, dimensions={0} | all-to-all | bytes 2097152 | tf_op jit(solution)/shard_map/all_to_all | solution.py:506
  289.0 5.5 %shard_map.178 = f32[32,2,64,128]{3,2,1,0:T(8,128)S(1)} custom-call(f32[2,256,1024]{2,1,0:T(8,128)S(1)} %copy-done.9, f32[2048,128]{1,0:T(8,128)S(1)} %bitcast.6, bf16[256,256]{1,0:T(8,128)(2,1)S(1)} %copy-done.26, bf16[256,256]{1,0:T(8,128)(2,1)S(1)} %copy-done.24, bf16[256,256]{1,0:T(8,128)(2,1)S(1)} %copy-done.22, bf16[256,256]{1,0:T(8,128)(2,1)S(1)} %copy-done.20, ...), custom_call_target="tpu_custom_call" | custom-call | tf_op jit(solution)/shard_map/pallas_call | solution.py:484
  294.5 56.5 %all_to_all.34.moved = f32[32,2,64,128]{3,2,1,0:T(8,128)S(1)} all-to-all(f32[32,2,64,128]{3,2,1,0:T(8,128)S(1)} %shard_map.178), channel_id=1, replica_groups=mesh['freq'=8,'slab'=32] {'slab'}, dimensions={0} | all-to-all | bytes 4194304 | tf_op jit(solution)/shard_map/all_to_all | solution.py:506
  351.0 3.0 shard_map.179
  (81 shorter events, 6.4 us)
Async XLA Ops:
  1.4 45.0 %copy-start.37 = (f32[3,2]{1,0:T(4,128)}, f32[3,2]{1,0:T(4,128)S(1)}, u32[]{:S(2)}) copy-start(f32[3,2]{1,0:T(4,128)S(1)} %copy.19.ref_slow) | copy-start | bytes 76
  5.9 40.5 %copy-start.39 = (s32[2]{0:T(128)}, s32[2]{0:T(128)S(1)}, u32[]{:S(2)}) copy-start(s32[2]{0:T(128)S(1)} %pad_add_fusion.place) | copy-start | bytes 28
  5.9 40.5 %copy-start = (f32[8,128,128]{2,1,0:T(8,128)S(1)}, f32[8,128,128]{2,1,0:T(8,128)}, u32[]{:S(2)}) copy-start(f32[8,128,128]{2,1,0:T(8,128)} %constant.46.clone.refs_6_) | copy-start | bytes 1572868
  5.9 40.5 %copy-start.1 = (f32[8,128,128]{2,1,0:T(8,128)S(1)}, f32[8,128,128]{2,1,0:T(8,128)}, u32[]{:S(2)}) copy-start(f32[8,128,128]{2,1,0:T(8,128)} %constant.45.clone.refs_5_) | copy-start | bytes 1572868
  5.9 40.5 %copy-start.19 = (bf16[256,256]{1,0:T(8,128)(2,1)S(1)}, bf16[256,256]{1,0:T(8,128)(2,1)}, u32[]{:S(2)}) copy-start(bf16[256,256]{1,0:T(8,128)(2,1)} %constant.44.clone.refs_4_) | copy-start | bytes 393220
  5.9 40.5 %copy-start.21 = (bf16[256,256]{1,0:T(8,128)(2,1)S(1)}, bf16[256,256]{1,0:T(8,128)(2,1)}, u32[]{:S(2)}) copy-start(bf16[256,256]{1,0:T(8,128)(2,1)} %constant.43.clone.refs_3_) | copy-start | bytes 393220
  5.9 40.5 %copy-start.23 = (bf16[256,256]{1,0:T(8,128)(2,1)S(1)}, bf16[256,256]{1,0:T(8,128)(2,1)}, u32[]{:S(2)}) copy-start(bf16[256,256]{1,0:T(8,128)(2,1)} %constant.42.clone.refs_2_) | copy-start | bytes 393220
  6.0 40.5 %copy-start.25 = (bf16[256,256]{1,0:T(8,128)(2,1)S(1)}, bf16[256,256]{1,0:T(8,128)(2,1)}, u32[]{:S(2)}) copy-start(bf16[256,256]{1,0:T(8,128)(2,1)} %constant.41.clone.refs_1_) | copy-start | bytes 393220
  6.0 40.5 %copy-start.33 = (f32[8,128]{1,0:T(8,128)S(1)}, f32[8,128]{1,0:T(8,128)}, u32[]{:S(2)}) copy-start(f32[8,128]{1,0:T(8,128)} %constant.48.clone.refs_8_) | copy-start | bytes 12292
  6.0 40.5 %copy-start.35 = (f32[8,128]{1,0:T(8,128)S(1)}, f32[8,128]{1,0:T(8,128)}, u32[]{:S(2)}) copy-start(f32[8,128]{1,0:T(8,128)} %constant.47.clone.refs_7_) | copy-start | bytes 12292
  56.2 90.4 %copy-start.3 = (bf16[256,256]{1,0:T(8,128)(2,1)S(1)}, bf16[256,256]{1,0:T(8,128)(2,1)}, u32[]{:S(2)}) copy-start(bf16[256,256]{1,0:T(8,128)(2,1)} %constant.38.clone.matrix_low) | copy-start | bytes 393220
  56.2 90.4 %copy-start.5 = (bf16[256,256]{1,0:T(8,128)(2,1)S(1)}, bf16[256,256]{1,0:T(8,128)(2,1)}, u32[]{:S(2)}) copy-start(bf16[256,256]{1,0:T(8,128)(2,1)} %constant.37.clone.matrix_high) | copy-start | bytes 393220
  56.2 90.4 %copy-start.16 = (bf16[256,256]{1,0:T(8,128)(2,1)S(1)}, bf16[256,256]{1,0:T(8,128)(2,1)}, u32[]{:S(2)}) copy-start(bf16[256,256]{1,0:T(8,128)(2,1)} %constant.50.clone.back_low) | copy-start | bytes 393220
  56.2 90.4 %copy-start.30 = (f32[16,128]{1,0:T(8,128)S(1)}, f32[16,128]{1,0:T(8,128)}, u32[]{:S(2)}) copy-start(f32[16,128]{1,0:T(8,128)} %constant.40.clone.turn_sin) | copy-start | bytes 24580
  56.2 90.4 %copy-start.32 = (f32[16,128]{1,0:T(8,128)S(1)}, f32[16,128]{1,0:T(8,128)}, u32[]{:S(2)}) copy-start(f32[16,128]{1,0:T(8,128)} %constant.39.clone.turn_cos) | copy-start | bytes 24580
  56.2 90.4 %all-to-all-start.1 = ((f32[32,2,64,128]{3,2,1,0:T(8,128)}), f32[32,2,64,128]{3,2,1,0:T(8,128)S(1)}, u32[]{:S(2)}, u32[]{:S(2)}) async-start(f32[32,2,64,128]{3,2,1,0:T(8,128)} %shard_map.174), calls=%async_computation.1 | async-start | bytes 4194304 | tf_op jit(solution)/shard_map/all_to_all | solution.py:506
  63.0 50.7 %collective-permute-start.3 = (f32[3,64,256]{2,1,0:T(8,128)}, f32[3,64,256]{2,1,0:T(8,128)S(1)}, u32[]{:S(2)}, u32[]{:S(2)}) collective-permute-start(f32[3,64,256]{2,1,0:T(8,128)} %refs_0_.1), channel_id=1, source_target_pairs={{0,128},{32,160},{64,192},{96,224},{128,0},{160,32},{192,64},{224,... | collective-permute-start | bytes 589832 | tf_op jit(solution)/shard_map/ppermute | solution.py:495
  63.6 53.8 %collective-permute-start.2 = (f32[3,64,256]{2,1,0:T(8,128)}, f32[3,64,256]{2,1,0:T(8,128)S(1)}, u32[]{:S(2)}, u32[]{:S(2)}) collective-permute-start(f32[3,64,256]{2,1,0:T(8,128)} %refs_0_.1), channel_id=1, source_target_pairs={{0,96},{32,0},{64,32},{96,64},{128,224},{160,128},{192,160},{224,1... | collective-permute-start | bytes 589832 | tf_op jit(solution)/shard_map/ppermute | solution.py:501
  66.5 51.8 %collective-permute-start.1 = (f32[3,64,256]{2,1,0:T(8,128)}, f32[3,64,256]{2,1,0:T(8,128)S(1)}, u32[]{:S(2)}, u32[]{:S(2)}) collective-permute-start(f32[3,64,256]{2,1,0:T(8,128)} %refs_0_.1), channel_id=1, source_target_pairs={{0,64},{32,96},{64,0},{96,32},{128,192},{160,224},{192,128},{224,1... | collective-permute-start | bytes 589832 | tf_op jit(solution)/shard_map/ppermute | solution.py:501
  67.2 51.2 %collective-permute-start = (f32[3,64,256]{2,1,0:T(8,128)}, f32[3,64,256]{2,1,0:T(8,128)S(1)}, u32[]{:S(2)}, u32[]{:S(2)}) collective-permute-start(f32[3,64,256]{2,1,0:T(8,128)} %refs_0_.1), channel_id=1, source_target_pairs={{0,32},{32,64},{64,96},{96,0},{128,160},{160,192},{192,224},{224,1... | collective-permute-start | bytes 589832 | tf_op jit(solution)/shard_map/ppermute | solution.py:501
  113.8 11.1 %collective-permute-start.6 = (f32[3,64,256]{2,1,0:T(8,128)S(1)}, f32[3,64,256]{2,1,0:T(8,128)S(1)}, u32[]{:S(2)}, u32[]{:S(2)}) collective-permute-start(f32[3,64,256]{2,1,0:T(8,128)S(1)} %collective-permute-done.3.refs_4_), channel_id=1, source_target_pairs={{0,96},{32,0},{64,32},{96,64},{128,224},{160,128},{192,160},{224,1... | collective-permute-start | bytes 589832 | tf_op jit(solution)/shard_map/ppermute | solution.py:501
  116.7 9.4 %collective-permute-start.5 = (f32[3,64,256]{2,1,0:T(8,128)S(1)}, f32[3,64,256]{2,1,0:T(8,128)S(1)}, u32[]{:S(2)}, u32[]{:S(2)}) collective-permute-start(f32[3,64,256]{2,1,0:T(8,128)S(1)} %collective-permute-done.3.refs_4_), channel_id=1, source_target_pairs={{0,64},{32,96},{64,0},{96,32},{128,192},{160,224},{192,128},{224,1... | collective-permute-start | bytes 589832 | tf_op jit(solution)/shard_map/ppermute | solution.py:501
  117.4 11.2 %collective-permute-start.4 = (f32[3,64,256]{2,1,0:T(8,128)S(1)}, f32[3,64,256]{2,1,0:T(8,128)S(1)}, u32[]{:S(2)}, u32[]{:S(2)}) collective-permute-start(f32[3,64,256]{2,1,0:T(8,128)S(1)} %collective-permute-done.3.refs_4_), channel_id=1, source_target_pairs={{0,32},{32,64},{64,96},{96,0},{128,160},{160,192},{192,224},{224,1... | collective-permute-start | bytes 589832 | tf_op jit(solution)/shard_map/ppermute | solution.py:501
  149.1 41.0 %copy-start.20 = (bf16[256,256]{1,0:T(8,128)(2,1)S(1)}, bf16[256,256]{1,0:T(8,128)(2,1)}, u32[]{:S(2)}) copy-start(bf16[256,256]{1,0:T(8,128)(2,1)} %constant.44.clone.refs_4_) | copy-start | bytes 393220
  149.1 41.0 %copy-start.22 = (bf16[256,256]{1,0:T(8,128)(2,1)S(1)}, bf16[256,256]{1,0:T(8,128)(2,1)}, u32[]{:S(2)}) copy-start(bf16[256,256]{1,0:T(8,128)(2,1)} %constant.43.clone.refs_3_) | copy-start | bytes 393220
  149.1 41.0 %copy-start.24 = (bf16[256,256]{1,0:T(8,128)(2,1)S(1)}, bf16[256,256]{1,0:T(8,128)(2,1)}, u32[]{:S(2)}) copy-start(bf16[256,256]{1,0:T(8,128)(2,1)} %constant.42.clone.refs_2_) | copy-start | bytes 393220
  149.1 41.0 %copy-start.26 = (bf16[256,256]{1,0:T(8,128)(2,1)S(1)}, bf16[256,256]{1,0:T(8,128)(2,1)}, u32[]{:S(2)}) copy-start(bf16[256,256]{1,0:T(8,128)(2,1)} %constant.41.clone.refs_1_) | copy-start | bytes 393220
  149.1 41.0 %copy-start.34 = (f32[8,128]{1,0:T(8,128)S(1)}, f32[8,128]{1,0:T(8,128)}, u32[]{:S(2)}) copy-start(f32[8,128]{1,0:T(8,128)} %constant.48.clone.refs_8_) | copy-start | bytes 12292
  149.1 41.0 %copy-start.36 = (f32[8,128]{1,0:T(8,128)S(1)}, f32[8,128]{1,0:T(8,128)}, u32[]{:S(2)}) copy-start(f32[8,128]{1,0:T(8,128)} %constant.47.clone.refs_7_) | copy-start | bytes 12292
  195.7 56.4 %copy-start.11 = (f32[4,16,64,128]{3,2,1,0:T(8,128)S(1)}, f32[4,16,64,128]{3,2,1,0:T(8,128)}, u32[]{:S(2)}) copy-start(f32[4,16,64,128]{3,2,1,0:T(8,128)} %copy-done.10) | copy-start | bytes 6291460
  195.7 56.4 %copy-start.18 = (bf16[256,256]{1,0:T(8,128)(2,1)S(1)}, bf16[256,256]{1,0:T(8,128)(2,1)}, u32[]{:S(2)}) copy-start(bf16[256,256]{1,0:T(8,128)(2,1)} %constant.49.clone.back_high) | copy-start | bytes 393220
  294.5 56.5 %copy-start.7 = (f32[4,16,64,128]{3,2,1,0:T(8,128)S(1)}, f32[4,16,64,128]{3,2,1,0:T(8,128)}, u32[]{:S(2)}) copy-start(f32[4,16,64,128]{3,2,1,0:T(8,128)} %copy-done.6) | copy-start | bytes 6291460
  (17 other events, 87.7 us)

commit v3 on v2

--- a/solution.py
+++ b/solution.py
@@ -7,6 +7,7 @@
 from jax import lax
 from jax.experimental import pallas as pl
 from jax.experimental.pallas import tpu as pltpu
+from jax.sharding import Mesh
 from jax.sharding import PartitionSpec as P
 
 two_pi = 2.0 * math.pi
@@ -19,7 +20,12 @@
 rows = 64
 parts = 32
 sub = 8
-tile_count = 8
+depth = 3
+ring = 8
+quarter = 16
+cell_start = 8 * rows
+freq_start = cell_start + depth * 2 * quarter
+message = freq_start + sub
 
 
 def split_bf16(matrix):
@@ -189,16 +195,13 @@
     return jnp.minimum(number, length - number).astype(jnp.float32) * (1.0 / length)
 
 
-def tile_of(me, n):
-    group = me // 4 if n < 4 else 1 - me // 4
-    return 4 * group + (me + 4 - n % 4) % 4
-
-
 def block_rows(step):
     return pl.ds(pl.multiple_of(step * sub, sub), sub)
 
 
-def forward_y(read, out, spectrum, matrix_high, matrix_low, turn_cos, turn_sin):
+def forward_y(read, write, spectrum, matrices, turns):
+    turn_cos, turn_sin = turns[0], turns[1]
+
     def step(c, carry):
         here = block_rows(c)
         values = dft([read(here, a) for a in range(outer)], -1)
@@ -210,42 +213,51 @@
         return carry
 
     lax.fori_loop(0, rows // sub, step, 0)
-    matrix = (matrix_high[...], matrix_low[...])
+    matrix = (matrices[0], matrices[1])
     for k in range(0, outer, 4):
         block = spectrum[k : k + 4].reshape(4 * rows, 2 * inner)
         result = mix(cut(block), matrix)
         for n in range(4):
             one = result[n * rows : (n + 1) * rows]
-            out[2 * (k + n)] = one[:, :inner]
-            out[2 * (k + n) + 1] = one[:, inner:]
-
-
-def start_kernel(
-    place, freqs, ref_slow, wavefield, matrix_high, matrix_low, turn_cos, turn_sin, out, spectrum
-):
+            write(2 * (k + n), one[:, :inner])
+            write(2 * (k + n) + 1, one[:, inner:])
+
+
+def start_kernel(freqs, wavefield, velocity, matrices, turns, out, spectrum):
     def read(here, a):
         columns = slice(a * inner, (a + 1) * inner)
         return wavefield[0, 0, here, columns], wavefield[1, 0, here, columns]
 
-    forward_y(read, out, spectrum, matrix_high, matrix_low, turn_cos, turn_sin)
+    def write(part, value):
+        y, x, c = part // 8, part // 2 % 4, part % 2
+        place = (4 * c + x) * rows
+        out[y, place : place + rows, :] = value
+
+    forward_y(read, write, spectrum, matrices, turns)
+    for y in range(4):
+        for level in range(depth):
+            for t in range(2):
+                place = cell_start + (2 * level + t) * quarter
+                out[y, place : place + quarter, :] = velocity[
+                    level, y * quarter : (y + 1) * quarter, t * inner : (t + 1) * inner
+                ]
+        out[y, freq_start:, :] = jnp.full((sub, inner), freqs[0], jnp.float32)
 
 
 def combine_kernel(
     last,
     moved,
     weights,
-    back_high,
-    back_low,
-    matrix_high,
-    matrix_low,
-    turn_cos,
-    turn_sin,
+    back_matrices,
+    matrices,
+    turns,
     out,
     fields,
     summed,
     spectrum,
 ):
-    matrix = (back_high[...], back_low[...])
+    turn_cos, turn_sin = turns[0], turns[1]
+    matrix = (back_matrices[0], back_matrices[1])
     for branch in range(2):
         for k in range(0, outer, 4):
             block = jnp.concatenate(
@@ -268,14 +280,15 @@
                 values.append(value if k == 0 else times(value, turn))
             values = dft(values, 1)
             for a in range(outer):
-                columns = slice(a * inner, (a + 1) * inner)
                 weight = (weights[2 * branch, a, here, :], weights[2 * branch + 1, a, here, :])
                 value = times(values[a], weight)
                 if branch == 1:
                     value = plus(value, (summed[0, a, here, :], summed[1, a, here, :]))
                 if last and branch == 1:
-                    out[0, 0, here, columns] = value[0]
-                    out[1, 0, here, columns] = value[1]
+                    columns = slice(a * inner, (a + 1) * inner)
+                    inside = pl.ds(pl.multiple_of(c % 2 * sub, sub), sub)
+                    out[c // 2, 0, inside, columns] = value[0]
+                    out[c // 2, 1, inside, columns] = value[1]
                 else:
                     summed[0, a, here, :] = value[0]
                     summed[1, a, here, :] = value[1]
@@ -288,45 +301,56 @@
     def read(here, a):
         return summed[0, a, here, :], summed[1, a, here, :]
 
-    forward_y(read, out, spectrum, matrix_high, matrix_low, turn_cos, turn_sin)
-
-
-def weigh(level, place, freqs, ref_slow, tiles, weights):
+    def write(part, value):
+        out[part] = value
+
+    forward_y(read, write, spectrum, matrices, turns)
+
+
+def weigh_kernel(level, place, freqs, ref_slow, *refs):
     def full(value):
         return jnp.full((sub, inner), value, jnp.float32)
 
     lower, upper = full(ref_slow[level, 0]), full(ref_slow[level, 1])
-    pace = depth_step * full(freqs[0])
+    pace = depth_step * full(freqs[place[0]])
     inverse_gap = 1.0 / (upper - lower)
     turn = cis(pace * (lower - upper))
 
-    def step(c, carry):
-        here = block_rows(c)
-        for n in range(outer):
-            slowness = 1.0 / tiles[n // 2][level, here, (n % 2) * inner : (n % 2 + 1) * inner]
-            excess = slowness - lower
-            upper_weight = jnp.clip(excess * inverse_gap, 0.0, 1.0)
-            lower_weight = 1.0 - upper_weight
-            phase = cis(pace * excess)
-            other = times(phase, turn)
-            a = 2 * tile_of(place[0], n // 2) + n % 2
-            weights[0, a, here, :] = lower_weight * phase[0]
-            weights[1, a, here, :] = lower_weight * phase[1]
-            weights[2, a, here, :] = upper_weight * other[0]
-            weights[3, a, here, :] = upper_weight * other[1]
-        return carry
-
-    lax.fori_loop(0, rows // sub, step, 0)
+    tiles, weights = refs[:ring], refs[ring]
+    z = 2 * place[0] + place[1]
+    for n in range(ring):
+        source = (z + n) % ring
+        tile = tiles[n]
+
+        def step(c, carry, source=source, tile=tile):
+            from_y = c // 2
+            inside = pl.ds(pl.multiple_of(c % 2 * sub, sub), sub)
+            here = pl.ds(pl.multiple_of(source // 2 * quarter + c % 2 * sub, sub), sub)
+            for t in range(2):
+                slowness = 1.0 / tile[from_y, 2 * level + t, inside, :]
+                excess = slowness - lower
+                upper_weight = jnp.clip(excess * inverse_gap, 0.0, 1.0)
+                lower_weight = 1.0 - upper_weight
+                phase = cis(pace * excess)
+                other = times(phase, turn)
+                a = 2 * (source % 2 * 4 + from_y) + t
+                weights[0, a, here, :] = lower_weight * phase[0]
+                weights[1, a, here, :] = lower_weight * phase[1]
+                weights[2, a, here, :] = upper_weight * other[0]
+                weights[3, a, here, :] = upper_weight * other[1]
+            return carry
+
+        lax.fori_loop(0, 8, step, 0, unroll=2)
 
 
 def propagators(level, place, freqs, ref_slow):
     lane = lax.broadcasted_iota(jnp.int32, (sub, inner), 1)
     sub_row = lax.broadcasted_iota(jnp.int32, (sub, inner), 0)
-    fy = folded(place[1] // 2 + outer * (half * (place[1] % 2) + lane % half))
+    fy = folded(place[2] // 2 + outer * (half * (place[2] % 2) + lane % half))
     fy = fy * fy
     squares = []
     for branch in range(2):
-        wave = jnp.full((sub, inner), freqs[0]) * jnp.full((sub, inner), ref_slow[level, branch])
+        wave = jnp.full((sub, inner), freqs[place[0]]) * jnp.full((sub, inner), ref_slow[level, branch])
         squares.append(wave * wave)
 
     def at(c, k):
@@ -349,52 +373,43 @@
     return at
 
 
-def tables_kernel(depth, place, freqs, ref_slow, *refs):
-    tiles, refs = refs[:tile_count], refs[tile_count:]
-    for level in range(depth):
-        weigh(level, place, freqs, ref_slow, tiles, refs[level])
-    for level in range(1, depth):
-        at = propagators(level, place, freqs, ref_slow)
-        table = refs[depth + level - 1]
-
-        def step(c, carry, at=at, table=table):
-            here = block_rows(c)
-            second_half = pl.ds(pl.multiple_of(inner + c * sub, sub), sub)
-            for k in range(outer // 2):
-                columns = slice(k * inner, (k + 1) * inner)
-                for branch, shift in enumerate(at(c, k)):
-                    table[branch, here, columns] = shift[0]
-                    table[branch, second_half, columns] = shift[1]
-            return carry
-
-        lax.fori_loop(0, inner // sub, step, 0)
-
-
-def first_shift_kernel(place, freqs, ref_slow, *refs):
-    shift(propagators(0, place, freqs, ref_slow), *refs)
-
-
-def later_shift_kernel(table, *refs):
-    def at(c, k):
+def propagator_kernel(level, place, freqs, ref_slow, table):
+    at = propagators(level, place, freqs, ref_slow)
+
+    def step(c, carry):
         here = block_rows(c)
         second_half = pl.ds(pl.multiple_of(inner + c * sub, sub), sub)
-        columns = slice(k * inner, (k + 1) * inner)
-        return [(table[n, here, columns], table[n, second_half, columns]) for n in range(2)]
-
-    shift(at, *refs)
-
-
-def shift(
-    propagators_at,
+        for k in range(outer // 2):
+            columns = slice(k * inner, (k + 1) * inner)
+            for branch, factor in enumerate(at(c, k)):
+                table[branch, here, columns] = factor[0]
+                table[branch, second_half, columns] = factor[1]
+        return carry
+
+    lax.fori_loop(0, inner // sub, step, 0)
+
+
+def slab_rows(a, top, c):
+    return ((a // 4 * 2 + top) * 4 + a % 4) * rows + c * sub
+
+
+def plane_chunk(a, top, c):
+    return c // 2 * 8 + a % 4 * 2 + top, a // 4 * quarter + c % 2 * sub
+
+
+def plane_rows(a, top, c):
+    chunk, row = plane_chunk(a, top, c)
+    return chunk * rows + row
+
+
+def shift_kernel(
+    rows_of,
     arrived,
-    there_high,
-    there_low,
-    back_high,
-    back_low,
-    turn_cos,
-    turn_sin,
-    lane_cos,
-    lane_sin,
+    table,
+    there_matrices,
+    back_matrices,
+    turns,
+    lane_turn,
     out,
     spectrum,
     shifted,
@@ -404,30 +419,32 @@
     groups = outer // 2
     steps = inner // sub
 
-    def there(c, carry):
-        here = block_rows(c)
+    def there(top, c, carry):
+        position = top * half + c * sub
+        here = pl.ds(pl.multiple_of(position, sub), sub)
+        second_half = pl.ds(pl.multiple_of(inner + position, sub), sub)
         values = []
         for a in range(groups):
-            first = arrived[pl.ds(pl.multiple_of(a * inner + c * sub, sub), sub), :]
-            second = arrived[pl.ds(pl.multiple_of((a + groups) * inner + c * sub, sub), sub), :]
+            first = arrived[pl.ds(pl.multiple_of(rows_of(a, top, c), sub), sub), :]
+            second = arrived[pl.ds(pl.multiple_of(rows_of(a + groups, top, c), sub), sub), :]
             total, differ = first + second, first - second
             value = (
                 jnp.where(low_lanes, total, pltpu.roll(differ, half, 1)),
                 jnp.where(low_lanes, pltpu.roll(total, half, 1), differ),
             )
-            turn = (lane_cos[a : a + 1, :], lane_sin[a : a + 1, :])
+            turn = (lane_turn[0, a : a + 1, :], lane_turn[1, a : a + 1, :])
             values.append(value if a == 0 else times_conj(value, turn))
         values = dft(values, -1)
-        second_half = pl.ds(pl.multiple_of(inner + c * sub, sub), sub)
         for k in range(groups):
-            value = times_conj(values[k], (turn_cos[k, here, :], turn_sin[k, here, :]))
+            value = times_conj(values[k], (turns[0, k, here, :], turns[1, k, here, :]))
             columns = slice(k * inner, (k + 1) * inner)
             spectrum[here, columns] = value[0]
             spectrum[second_half, columns] = value[1]
         return carry
 
-    lax.fori_loop(0, steps, there, 0)
-    matrix = (there_high[...], there_low[...])
+    for top in range(2):
+        lax.fori_loop(0, half // sub, functools.partial(there, top), 0)
+    matrix = (there_matrices[0], there_matrices[1])
     for n in range(4):
         columns = slice(n * 2 * inner, (n + 1) * 2 * inner)
         spectrum[:, columns] = mix(matrix, cut(spectrum[:, columns]))
@@ -438,14 +455,14 @@
         for k in range(groups):
             columns = slice(k * inner, (k + 1) * inner)
             value = (spectrum[here, columns], spectrum[second_half, columns])
-            for branch, factor in enumerate(propagators_at(c, k)):
-                moved = times(value, factor)
+            for branch in range(2):
+                moved = times(value, (table[branch, here, columns], table[branch, second_half, columns]))
                 shifted[branch, here, columns] = moved[0]
                 shifted[branch, second_half, columns] = moved[1]
         return carry
 
     lax.fori_loop(0, steps, propagate, 0)
-    matrix = (back_high[...], back_low[...])
+    matrix = (back_matrices[0], back_matrices[1])
     for branch in range(2):
         for n in range(4):
             columns = slice(n * 2 * inner, (n + 1) * 2 * inner)
@@ -453,26 +470,26 @@
 
     for top in range(2):
 
-        def back(c, carry):
+        def back(c, carry, top=top):
             position = top * half + c * sub
             here = pl.ds(pl.multiple_of(position, sub), sub)
             second_half = pl.ds(pl.multiple_of(inner + position, sub), sub)
-            local = block_rows(c)
             for branch in range(2):
                 values = []
                 for k in range(groups):
                     columns = slice(k * inner, (k + 1) * inner)
                     value = (shifted[branch, here, columns], shifted[branch, second_half, columns])
-                    values.append(times(value, (turn_cos[k, here, :], turn_sin[k, here, :])))
+                    values.append(times(value, (turns[0, k, here, :], turns[1, k, here, :])))
                 values = dft(values, 1)
                 for a in range(groups):
                     value = values[a]
                     if a > 0:
-                        value = times(value, (lane_cos[a : a + 1, :], lane_sin[a : a + 1, :]))
+                        value = times(value, (lane_turn[0, a : a + 1, :], lane_turn[1, a : a + 1, :]))
                     even = jnp.where(low_lanes, value[0], pltpu.roll(value[1], half, 1))
                     odd = jnp.where(low_lanes, pltpu.roll(value[0], half, 1), value[1])
-                    out[2 * a + top, branch, local, :] = even + odd
-                    out[2 * (a + groups) + top, branch, local, :] = even - odd
+                    for at, result in ((a, even + odd), (a + groups, even - odd)):
+                        chunk, row = plane_chunk(at, top, c)
+                        out[chunk, branch, pl.ds(pl.multiple_of(row, sub), sub), :] = result
             return carry
 
         lax.fori_loop(0, half // sub, back, 0)
@@ -491,82 +508,97 @@
     )(*scalars, *operands)
 
 
-def velocity_tiles(velocity):
-    other = lax.ppermute(velocity, "freq", [(n, (n + 4) % 8) for n in range(8)])
-    tiles = []
-    for tile in (velocity, other):
-        tiles.append(tile)
-        for back in range(1, 4):
-            pairs = [(n, n // 4 * 4 + (n + back) % 4) for n in range(8)]
-            tiles.append(lax.ppermute(tile, "freq", pairs))
+def exchange(values, axes):
+    return lax.all_to_all(values, axes, split_axis=0, concat_axis=0, tiled=True)
+
+
+def around_z(tile):
+    axes = ("zl", "zh")
+    index = [n % 2 * 4 + n // 2 for n in range(ring)]
+    down = [(index[n], index[n - 1]) for n in range(ring)]
+    up = [(index[n - 1], index[n]) for n in range(ring)]
+    tiles = [tile] + [None] * (ring - 1)
+    above = below = tile
+    for n in range(1, 5):
+        above = lax.ppermute(above, axes, down)
+        tiles[n] = above
+        if n < 4:
+            below = lax.ppermute(below, axes, up)
+            tiles[ring - n] = below
     return tiles
 
 
-def exchange(values):
-    return lax.all_to_all(values, "slab", split_axis=0, concat_axis=0, tiled=True)
-
-
 def shards(wavefield, freqs, velocity, ref_slow):
-    depth = ref_slow.shape[0]
-    place = jnp.stack([lax.axis_index("freq"), lax.axis_index("slab")])
-    common = (place, freqs, ref_slow)
-    tiles = velocity_tiles(velocity)
-
-    fy_matrix = forward_y_matrix()
-    iy_matrix = inverse_y_matrix()
-    fx_matrix = x_matrix(-1)
-    ix_matrix = x_matrix(1)
-    turn_y = y_turns()
-    turn_x = x_turns()
-    turn_lane = lane_turns()
-
+    zh, zl = lax.axis_index("zh"), lax.axis_index("zl")
+    part = (lax.axis_index("y") * 4 + lax.axis_index("x")) * 2 + lax.axis_index("c")
+    place = jnp.stack([zh, zl, part])
+
+    fy_matrix = np.stack(forward_y_matrix())
+    iy_matrix = np.stack(inverse_y_matrix())
+    fx_matrix = np.stack(x_matrix(-1))
+    ix_matrix = np.stack(x_matrix(1))
+    turn_y = np.stack(y_turns())
+    turn_x = np.stack(x_turns())
+    turn_lane = np.stack(lane_turns())
+
+    plane = ("y", "x", "c")
     packed = (parts, rows, inner)
     spectrum_shape = (outer, rows, 2 * inner)
     folded_shape = (2 * inner, length // 2)
-    weights_shape = (4, outer, rows, inner)
     (sent,) = call(
-        start_kernel, [packed], [spectrum_shape], common, (wavefield, *fy_matrix, *turn_y)
+        start_kernel,
+        [(4, message, inner)],
+        [spectrum_shape],
+        (freqs,),
+        (wavefield, velocity, fy_matrix, turn_y),
     )
-    tables = call(
-        functools.partial(tables_kernel, depth),
-        [weights_shape] * depth + [(2, *folded_shape)] * (depth - 1),
-        [],
-        common,
-        velocity_tiles(velocity),
-    )
+    sent = exchange(sent, ("y",))
+    freqs = sent[:, freq_start, 0]
+    tile = sent[:, cell_start:freq_start].reshape(4, 2 * depth, quarter, inner)
+    arrived = exchange(sent[:, :cell_start].reshape(packed), ("zh", "c", "x"))
+    arrived, tile = lax.optimization_barrier((arrived, tile))
+    tiles = around_z(tile)
+    common = (place, freqs, ref_slow)
     for level in range(depth):
-        arrived = exchange(sent).reshape(length, inner)
+        if level:
+            arrived = exchange(sent, plane)
+        (table,) = call(
+            functools.partial(propagator_kernel, level), [(2, *folded_shape)], [], common, ()
+        )
         (shifted,) = call(
-            later_shift_kernel if level else first_shift_kernel,
+            functools.partial(shift_kernel, plane_rows if level else slab_rows),
             [(parts, 2, rows, inner)],
             [folded_shape, (2, *folded_shape)],
-            () if level else common,
-            (
-                *tables[depth + level - 1 : depth + level][: 1 if level else 0],
-                arrived,
-                *fx_matrix,
-                *ix_matrix,
-                *turn_x,
-                *turn_lane,
-            ),
+            (),
+            (arrived.reshape(length, inner), table, fx_matrix, ix_matrix, turn_x, turn_lane),
         )
-        moved = exchange(shifted)
+        moved = exchange(shifted, plane)
+        (weights,) = call(
+            functools.partial(weigh_kernel, level), [(4, outer, rows, inner)], [], common, tiles
+        )
         last = level == depth - 1
         (sent,) = call(
             functools.partial(combine_kernel, last),
-            [(2, 1, rows, length) if last else packed],
+            [(4, 2, quarter, length) if last else packed],
             [(2, *spectrum_shape), (2, outer, rows, inner), spectrum_shape],
             (),
-            (moved, tables[level], *iy_matrix, *fy_matrix, *turn_y),
+            (moved, weights, iy_matrix, fy_matrix, turn_y),
         )
-    return sent
+    back = exchange(exchange(sent, ("zh",)), ("y",))
+    return back.transpose(1, 0, 2, 3).reshape(2, 1, rows, length)
 
 
 def solution(mesh):
+    axes = ("zl", "y", "zh", "x", "c")
     return jax.shard_map(
         shards,
-        mesh=mesh,
-        in_specs=(P(None, "freq", "slab", None), P("freq"), P(None, "slab", "freq"), P()),
-        out_specs=P(None, "freq", "slab", None),
+        mesh=Mesh(mesh.devices.reshape(2, 4, 4, 4, 2), axes),
+        in_specs=(
+            P(None, axes[:2], axes[2:], None),
+            P(axes[:2]),
+            P(None, axes[2:], axes[:2]),
+            P(),
+        ),
+        out_specs=P(None, axes[:2], axes[2:], None),
         check_vma=False,
     )

time: 357 us -> 321 us (0.90)
  blocking collectives: 223 us -> 70.3 us
  waiting for transfers between devices: 55.9 us -> 103 us
  starting transfers between devices: 16.5 us -> 52.5 us
  local copies, waits for them, and re-layouts: 16.9 us -> 46 us
  Pallas kernels: 40.2 us -> 44.9 us
    all_to_all x5 -> x3, blocking collectives: 223 us -> 70.3 us  [exchange(): return lax.all_to_all(values, axes, split_axis=0, concat_axis=0, tiled=True)]
    all_to_all x1 -> x6, waiting for transfers between devices: 0.01 us -> 87.8 us  [exchange(): return lax.all_to_all(values, axes, split_axis=0, concat_axis=0, tiled=True)]
    ppermute x7, waiting for transfers between devices: 55.9 us -> 15.6 us  [the longest x4 15.6 us: around_z(): above = lax.ppermute(above, axes, down)]
    all_to_all x1 -> x6, starting transfers between devices: 6.81 us -> 41.7 us  [exchange(): return lax.all_to_all(values, axes, split_axis=0, concat_axis=0, tiled=True)]
    unnamed x83 -> x109, local copies, waits for them, and re-layouts: 16.9 us -> 42.1 us
    pallas_call x8 -> x13, Pallas kernels: 40.2 us -> 44.9 us  [call(): pl.pallas_call(kernel, out_shape=[jax.ShapeDtypeStruct(s, jnp.float32) fo...]
  transfers between devices with their start and end apart: 8 -> 13, of which waited for: 4 -> 9; matrix products, arithmetic and copies ran while one was open for 0% -> 1% of each run, Pallas kernels for 3% -> 5%
where the time goes in v3:
time: 321 us; the launch traced here: 318 us
  waiting for transfers between devices  103 us (32%)
  blocking collectives  70.3 us (22%)
  starting transfers between devices  52.5 us (16%)
  local copies, waits for them, and re-layouts  46 us (14%)
  Pallas kernels  44.9 us (14%)
    all_to_all x6, waiting for transfers between devices, exchange(): return lax.all_to_all(values, axes, split_axis=0, concat_axis=0, tiled=True)  87.8 us
    all_to_all x3, blocking collectives, exchange(): return lax.all_to_all(values, axes, split_axis=0, concat_axis=0, tiled=True)  70.3 us
    pallas_call x13, Pallas kernels, call(): pl.pallas_call(kernel, out_shape=[jax.ShapeDtypeStruct(s, jnp.float32) fo...  44.9 us
    unnamed x109, local copies, waits for them, and re-layouts  42.1 us
    all_to_all x6, starting transfers between devices, exchange(): return lax.all_to_all(values, axes, split_axis=0, concat_axis=0, tiled=True)  41.7 us
    ppermute x4, waiting for transfers between devices, around_z(): above = lax.ppermute(above, axes, down)  15.6 us
    ppermute x4, starting transfers between devices, around_z(): above = lax.ppermute(above, axes, down)  9.19 us
  transfers between devices with their start and end apart: 13, of which 9 were waited for; matrix products, arithmetic and copies ran while one was open for 1% of the time, Pallas kernels for 5%

profile of v3, /device:TPU:2, one launch (start us, length us, event | category | flops | bytes accessed | tf_op | source)
XLA Modules:
  0.0 318.3 jit_solution(8174979427028241190)
XLA Ops:
  5.4 21.6 %all_to_all.45 = f32[4,616,128]{2,1,0:T(8,128)S(1)} all-to-all(f32[4,616,128]{2,1,0:T(8,128)S(1)} %shard_map.109), channel_id=1, replica_groups=mesh['zl'=2,'y'=4,'zh'=4,'x'=4,'c'=2] {'y'}, dimensions={0} | all-to-all | bytes 2523136 | tf_op jit(solution)/shard_map/all_to_all | solution.py:512
  28.2 11.8 %all-to-all-start.1 = ((f32[32,64,128]{2,1,0:T(8,128)}), f32[32,64,128]{2,1,0:T(8,128)}, u32[]{:S(2)}, u32[]{:S(2)}) async-start(f32[32,64,128]{2,1,0:T(8,128)} %bitcast.17), calls=%async_computation.1 | async-start | bytes 2097152 | tf_op jit(solution)/shard_map/all_to_all | solution.py:512
  40.3 2.8 shard_map.110.table
  44.8 23.8 %all-to-all-done.1 = f32[32,64,128]{2,1,0:T(8,128)} async-done(((f32[32,64,128]{2,1,0:T(8,128)}), f32[32,64,128]{2,1,0:T(8,128)}, u32[]{:S(2)}, u32[]{:S(2)}) %all-to-all-start.1) | async-done | bytes 1048608 | tf_op jit(solution)/shard_map/all_to_all | solution.py:512
  69.5 6.8 %shard_map.111 = f32[32,2,64,128]{3,2,1,0:T(8,128)S(1)} custom-call(f32[2048,128]{1,0:T(8,128)} %bitcast.2.arrived, f32[2,256,1024]{2,1,0:T(8,128)S(1)} %shard_map.110.table, bf16[2,256,256]{2,1,0:T(8,128)(2,1)S(1)} %copy-done.20, bf16[2,256,256]{2,1,0:T(8,128)(2,1)S(1)} %copy-done.23, f32[2,8,128,128]{3,2,1,0:T(8,128)S(1)} %copy-done, ...), custom_call_target="tpu_custom_call" | custom-call | tf_op jit(solution)/shard_map/pallas_call | solution.py:501
  77.7 5.4 %all-to-all-start.2 = ((f32[32,2,64,128]{3,2,1,0:T(8,128)}), f32[32,2,64,128]{3,2,1,0:T(8,128)S(1)}, u32[]{:S(2)}, u32[]{:S(2)}) async-start(f32[32,2,64,128]{3,2,1,0:T(8,128)} %copy-done.1), calls=%async_computation.2 | async-start | bytes 4194304 | tf_op jit(solution)/shard_map/all_to_all | solution.py:512
  85.2 5.1 %collective-permute-done.refs_1_ = f32[4,6,16,128]{3,2,1,0:T(8,128)S(1)} collective-permute-done((f32[4,6,16,128]{3,2,1,0:T(8,128)}, f32[4,6,16,128]{3,2,1,0:T(8,128)S(1)}, u32[]{:S(2)}, u32[]{:S(2)}) %collective-permute-start) | collective-permute-done | bytes 196640 | tf_op jit(solution)/shard_map/ppermute | solution.py:523
  92.4 4.1 %collective-permute-done.1.refs_2_ = f32[4,6,16,128]{3,2,1,0:T(8,128)S(1)} collective-permute-done((f32[4,6,16,128]{3,2,1,0:T(8,128)S(1)}, f32[4,6,16,128]{3,2,1,0:T(8,128)S(1)}, u32[]{:S(2)}, u32[]{:S(2)}) %collective-permute-start.1) | collective-permute-done | bytes 196640 | tf_op jit(solution)/shard_map/ppermute | solution.py:523
  96.5 3.0 collective-permute-start.2
  99.5 3.2 collective-permute-done.2.refs_3_
  102.7 3.7 %collective-permute-start.3 = (f32[4,6,16,128]{3,2,1,0:T(8,128)S(1)}, f32[4,6,16,128]{3,2,1,0:T(8,128)S(1)}, u32[]{:S(2)}, u32[]{:S(2)}) collective-permute-start(f32[4,6,16,128]{3,2,1,0:T(8,128)S(1)} %collective-permute-done.2.refs_3_), channel_id=1, source_target_pairs={{0,152},{128,0},{8,128},{136,8},{16,136},{144,16},{24,144},{152,24... | collective-permute-start | bytes 589832 | tf_op jit(solution)/shard_map/ppermute | solution.py:523
  106.4 3.2 %collective-permute-done.3.refs_4_ = f32[4,6,16,128]{3,2,1,0:T(8,128)S(1)} collective-permute-done((f32[4,6,16,128]{3,2,1,0:T(8,128)S(1)}, f32[4,6,16,128]{3,2,1,0:T(8,128)S(1)}, u32[]{:S(2)}, u32[]{:S(2)}) %collective-permute-start.3) | collective-permute-done | bytes 196640 | tf_op jit(solution)/shard_map/ppermute | solution.py:523
  110.5 2.4 shard_map.112.weights
  121.6 3.0 shard_map.113
  125.5 7.5 %all-to-all-start.3 = ((f32[32,64,128]{2,1,0:T(8,128)}), f32[32,64,128]{2,1,0:T(8,128)}, u32[]{:S(2)}, u32[]{:S(2)}) async-start(f32[32,64,128]{2,1,0:T(8,128)} %copy-done.12), calls=%async_computation.3 | async-start | bytes 2097152 | tf_op jit(solution)/shard_map/all_to_all | solution.py:512
  133.0 2.8 shard_map.114.table
  135.9 13.3 %all-to-all-done.3 = f32[32,64,128]{2,1,0:T(8,128)} async-done(((f32[32,64,128]{2,1,0:T(8,128)}), f32[32,64,128]{2,1,0:T(8,128)}, u32[]{:S(2)}, u32[]{:S(2)}) %all-to-all-start.3) | async-done | bytes 1048608 | tf_op jit(solution)/shard_map/all_to_all | solution.py:512
  151.1 6.8 %shard_map.115 = f32[32,2,64,128]{3,2,1,0:T(8,128)S(1)} custom-call(f32[2048,128]{1,0:T(8,128)} %bitcast.6.arrived, f32[2,256,1024]{2,1,0:T(8,128)S(1)} %shard_map.114.table, bf16[2,256,256]{2,1,0:T(8,128)(2,1)S(1)} %copy-done.21, bf16[2,256,256]{2,1,0:T(8,128)(2,1)S(1)} %copy-done.24, f32[2,8,128,128]{3,2,1,0:T(8,128)S(1)} %copy-done, ...), custom_call_target="tpu_custom_call" | custom-call | tf_op jit(solution)/shard_map/pallas_call | solution.py:501
  159.2 5.1 %all-to-all-start.4 = ((f32[32,2,64,128]{3,2,1,0:T(8,128)}), f32[32,2,64,128]{3,2,1,0:T(8,128)S(1)}, u32[]{:S(2)}, u32[]{:S(2)}) async-start(f32[32,2,64,128]{3,2,1,0:T(8,128)} %copy-done.5), calls=%async_computation.4 | async-start | bytes 4194304 | tf_op jit(solution)/shard_map/all_to_all | solution.py:512
  171.8 2.4 shard_map.116.weights
  175.5 16.8 %all-to-all-done.4.moved = f32[32,2,64,128]{3,2,1,0:T(8,128)S(1)} async-done(((f32[32,2,64,128]{3,2,1,0:T(8,128)}), f32[32,2,64,128]{3,2,1,0:T(8,128)S(1)}, u32[]{:S(2)}, u32[]{:S(2)}) %all-to-all-start.4) | async-done | bytes 2097184 | tf_op jit(solution)/shard_map/all_to_all | solution.py:512
  194.9 3.0 shard_map.117
  198.8 6.6 %all-to-all-start.5 = ((f32[32,64,128]{2,1,0:T(8,128)}), f32[32,64,128]{2,1,0:T(8,128)}, u32[]{:S(2)}, u32[]{:S(2)}) async-start(f32[32,64,128]{2,1,0:T(8,128)} %copy-done.13), calls=%async_computation.5 | async-start | bytes 2097152 | tf_op jit(solution)/shard_map/all_to_all | solution.py:512
  205.4 2.8 shard_map.118.table
  208.3 13.4 %all-to-all-done.5 = f32[32,64,128]{2,1,0:T(8,128)} async-done(((f32[32,64,128]{2,1,0:T(8,128)}), f32[32,64,128]{2,1,0:T(8,128)}, u32[]{:S(2)}, u32[]{:S(2)}) %all-to-all-start.5) | async-done | bytes 1048608 | tf_op jit(solution)/shard_map/all_to_all | solution.py:512
  223.6 6.8 %shard_map.119 = f32[32,2,64,128]{3,2,1,0:T(8,128)S(1)} custom-call(f32[2048,128]{1,0:T(8,128)} %bitcast.7.arrived, f32[2,256,1024]{2,1,0:T(8,128)S(1)} %shard_map.118.table, bf16[2,256,256]{2,1,0:T(8,128)(2,1)S(1)} %copy-done.22, bf16[2,256,256]{2,1,0:T(8,128)(2,1)S(1)} %copy-done.25, f32[2,8,128,128]{3,2,1,0:T(8,128)S(1)} %copy-done, ...), custom_call_target="tpu_custom_call" | custom-call | tf_op jit(solution)/shard_map/pallas_call | solution.py:501
  231.8 5.3 %all-to-all-start.6 = ((f32[32,2,64,128]{3,2,1,0:T(8,128)}), f32[32,2,64,128]{3,2,1,0:T(8,128)S(1)}, u32[]{:S(2)}, u32[]{:S(2)}) async-start(f32[32,2,64,128]{3,2,1,0:T(8,128)} %copy-done.2), calls=%async_computation.6 | async-start | bytes 4194304 | tf_op jit(solution)/shard_map/all_to_all | solution.py:512
  240.8 2.4 shard_map.120.weights
  244.6 20.5 %all-to-all-done.6.moved = f32[32,2,64,128]{3,2,1,0:T(8,128)S(1)} async-done(((f32[32,2,64,128]{3,2,1,0:T(8,128)}), f32[32,2,64,128]{3,2,1,0:T(8,128)S(1)}, u32[]{:S(2)}, u32[]{:S(2)}) %all-to-all-start.6) | async-done | bytes 2097184 | tf_op jit(solution)/shard_map/all_to_all | solution.py:512
  266.6 1.9 shard_map.121
  268.5 29.6 %all_to_all.46 = f32[4,2,16,2048]{3,2,1,0:T(8,128)S(1)} all-to-all(f32[4,2,16,2048]{3,2,1,0:T(8,128)S(1)} %shard_map.121), channel_id=1, replica_groups=mesh['zl'=2,'y'=4,'zh'=4,'x'=4,'c'=2] {'zh'}, dimensions={0} | all-to-all | bytes 2097152 | tf_op jit(solution)/shard_map/all_to_all | solution.py:512
  298.1 19.1 %all_to_all.47 = f32[4,2,16,2048]{3,2,1,0:T(8,128)S(1)} all-to-all(f32[4,2,16,2048]{3,2,1,0:T(8,128)S(1)} %all_to_all.46), channel_id=1, replica_groups=mesh['zl'=2,'y'=4,'zh'=4,'x'=4,'c'=2] {'y'}, dimensions={0} | all-to-all | bytes 2097152 | tf_op jit(solution)/shard_map/all_to_all | solution.py:512
  (124 shorter events, 51.2 us)
Async XLA Ops:
  27.1 13.1 %copy-start.52 = (f32[4,616,128]{2,1,0:T(8,128)}, f32[4,616,128]{2,1,0:T(8,128)S(1)}, u32[]{:S(2)}) copy-start(f32[4,616,128]{2,1,0:T(8,128)S(1)} %all_to_all.45) | copy-start | bytes 3784708
  27.1 12.9 %copy-start.53 = (f32[3,2]{0,1:T(2,128)S(1)}, f32[3,2]{0,1:T(2,128)}, u32[]{:S(2)}) copy-start(f32[3,2]{0,1:T(2,128)} %param.14) | copy-start | bytes 76
  28.2 40.4 %copy-start = (f32[2,8,128,128]{3,2,1,0:T(8,128)S(1)}, f32[2,8,128,128]{3,2,1,0:T(8,128)}, u32[]{:S(2)}) copy-start(f32[2,8,128,128]{3,2,1,0:T(8,128)} %constant.41.clone.turns) | copy-start | bytes 3145732
  28.2 40.4 %copy-start.20 = (bf16[2,256,256]{2,1,0:T(8,128)(2,1)S(1)}, bf16[2,256,256]{2,1,0:T(8,128)(2,1)}, u32[]{:S(2)}) copy-start(bf16[2,256,256]{2,1,0:T(8,128)(2,1)} %constant.39.clone.there_matrices) | copy-start | bytes 786436
  28.2 40.4 %copy-start.51 = (f32[2,8,128]{2,1,0:T(8,128)S(1)}, f32[2,8,128]{2,1,0:T(8,128)}, u32[]{:S(2)}) copy-start(f32[2,8,128]{2,1,0:T(8,128)} %constant.42.clone.lane_turn) | copy-start | bytes 24580
  28.2 40.4 %all-to-all-start.1 = ((f32[32,64,128]{2,1,0:T(8,128)}), f32[32,64,128]{2,1,0:T(8,128)}, u32[]{:S(2)}, u32[]{:S(2)}) async-start(f32[32,64,128]{2,1,0:T(8,128)} %bitcast.17), calls=%async_computation.1 | async-start | bytes 2097152 | tf_op jit(solution)/shard_map/all_to_all | solution.py:512
  76.3 1.3 copy-start.1
  77.7 41.4 %copy-start.49 = (f32[2,16,128]{2,1,0:T(8,128)S(1)}, f32[2,16,128]{2,1,0:T(8,128)}, u32[]{:S(2)}) copy-start(f32[2,16,128]{2,1,0:T(8,128)} %constant.38.clone.turns) | copy-start | bytes 49156
  77.7 41.4 %all-to-all-start.2 = ((f32[32,2,64,128]{3,2,1,0:T(8,128)}), f32[32,2,64,128]{3,2,1,0:T(8,128)S(1)}, u32[]{:S(2)}, u32[]{:S(2)}) async-start(f32[32,2,64,128]{3,2,1,0:T(8,128)} %copy-done.1), calls=%async_computation.2 | async-start | bytes 4194304 | tf_op jit(solution)/shard_map/all_to_all | solution.py:512
  83.1 36.0 %copy-start.11 = (bf16[2,256,256]{2,1,0:T(8,128)(2,1)S(1)}, bf16[2,256,256]{2,1,0:T(8,128)(2,1)}, u32[]{:S(2)}) copy-start(bf16[2,256,256]{2,1,0:T(8,128)(2,1)} %constant.37.clone.matrices) | copy-start | bytes 786436
  83.1 7.2 %collective-permute-start = (f32[4,6,16,128]{3,2,1,0:T(8,128)}, f32[4,6,16,128]{3,2,1,0:T(8,128)S(1)}, u32[]{:S(2)}, u32[]{:S(2)}) collective-permute-start(f32[4,6,16,128]{3,2,1,0:T(8,128)} %bitcast.12), channel_id=1, source_target_pairs={{0,152},{128,0},{8,128},{136,8},{16,136},{144,16},{24,144},{152,24... | collective-permute-start | bytes 589832 | tf_op jit(solution)/shard_map/ppermute | solution.py:523
  83.8 8.4 %collective-permute-start.4 = (f32[4,6,16,128]{3,2,1,0:T(8,128)}, f32[4,6,16,128]{3,2,1,0:T(8,128)S(1)}, u32[]{:S(2)}, u32[]{:S(2)}) collective-permute-start(f32[4,6,16,128]{3,2,1,0:T(8,128)} %bitcast.13), channel_id=1, source_target_pairs={{152,0},{0,128},{128,8},{8,136},{136,16},{16,144},{144,24},{24,152... | collective-permute-start | bytes 589832 | tf_op jit(solution)/shard_map/ppermute | solution.py:526
  90.3 6.1 %collective-permute-start.1 = (f32[4,6,16,128]{3,2,1,0:T(8,128)S(1)}, f32[4,6,16,128]{3,2,1,0:T(8,128)S(1)}, u32[]{:S(2)}, u32[]{:S(2)}) collective-permute-start(f32[4,6,16,128]{3,2,1,0:T(8,128)S(1)} %collective-permute-done.refs_1_), channel_id=1, source_target_pairs={{0,152},{128,0},{8,128},{136,8},{16,136},{144,16},{24,144},{152,24... | collective-permute-start | bytes 589832 | tf_op jit(solution)/shard_map/ppermute | solution.py:523
  92.1 7.3 %collective-permute-start.5 = (f32[4,6,16,128]{3,2,1,0:T(8,128)S(1)}, f32[4,6,16,128]{3,2,1,0:T(8,128)S(1)}, u32[]{:S(2)}, u32[]{:S(2)}) collective-permute-start(f32[4,6,16,128]{3,2,1,0:T(8,128)S(1)} %collective-permute-done.4.refs_7_), channel_id=1, source_target_pairs={{152,0},{0,128},{128,8},{8,136},{136,16},{16,144},{144,24},{24,152... | collective-permute-start | bytes 589832 | tf_op jit(solution)/shard_map/ppermute | solution.py:526
  96.5 6.2 %collective-permute-start.2 = (f32[4,6,16,128]{3,2,1,0:T(8,128)S(1)}, f32[4,6,16,128]{3,2,1,0:T(8,128)S(1)}, u32[]{:S(2)}, u32[]{:S(2)}) collective-permute-start(f32[4,6,16,128]{3,2,1,0:T(8,128)S(1)} %collective-permute-done.1.refs_2_), channel_id=1, source_target_pairs={{0,152},{128,0},{8,128},{136,8},{16,136},{144,16},{24,144},{152,24... | collective-permute-start | bytes 589832 | tf_op jit(solution)/shard_map/ppermute | solution.py:523
  99.5 6.9 %collective-permute-start.6 = (f32[4,6,16,128]{3,2,1,0:T(8,128)S(1)}, f32[4,6,16,128]{3,2,1,0:T(8,128)S(1)}, u32[]{:S(2)}, u32[]{:S(2)}) collective-permute-start(f32[4,6,16,128]{3,2,1,0:T(8,128)S(1)} %collective-permute-done.5.refs_6_), channel_id=1, source_target_pairs={{152,0},{0,128},{128,8},{8,136},{136,16},{16,144},{144,24},{24,152... | collective-permute-start | bytes 589832 | tf_op jit(solution)/shard_map/ppermute | solution.py:526
  102.7 6.9 %collective-permute-start.3 = (f32[4,6,16,128]{3,2,1,0:T(8,128)S(1)}, f32[4,6,16,128]{3,2,1,0:T(8,128)S(1)}, u32[]{:S(2)}, u32[]{:S(2)}) collective-permute-start(f32[4,6,16,128]{3,2,1,0:T(8,128)S(1)} %collective-permute-done.2.refs_3_), channel_id=1, source_target_pairs={{0,152},{128,0},{8,128},{136,8},{16,136},{144,16},{24,144},{152,24... | collective-permute-start | bytes 589832 | tf_op jit(solution)/shard_map/ppermute | solution.py:523
  119.1 1.6 copy-start.7
  125.5 23.6 %all-to-all-start.3 = ((f32[32,64,128]{2,1,0:T(8,128)}), f32[32,64,128]{2,1,0:T(8,128)}, u32[]{:S(2)}, u32[]{:S(2)}) async-start(f32[32,64,128]{2,1,0:T(8,128)} %copy-done.12), calls=%async_computation.3 | async-start | bytes 2097152 | tf_op jit(solution)/shard_map/all_to_all | solution.py:512
  157.9 1.3 copy-start.5
  159.2 33.1 %all-to-all-start.4 = ((f32[32,2,64,128]{3,2,1,0:T(8,128)}), f32[32,2,64,128]{3,2,1,0:T(8,128)S(1)}, u32[]{:S(2)}, u32[]{:S(2)}) async-start(f32[32,2,64,128]{3,2,1,0:T(8,128)} %copy-done.5), calls=%async_computation.4 | async-start | bytes 4194304 | tf_op jit(solution)/shard_map/all_to_all | solution.py:512
  174.2 1.3 copy-start.8
  192.3 1.6 copy-start.9
  198.8 22.9 %all-to-all-start.5 = ((f32[32,64,128]{2,1,0:T(8,128)}), f32[32,64,128]{2,1,0:T(8,128)}, u32[]{:S(2)}, u32[]{:S(2)}) async-start(f32[32,64,128]{2,1,0:T(8,128)} %copy-done.13), calls=%async_computation.5 | async-start | bytes 2097152 | tf_op jit(solution)/shard_map/all_to_all | solution.py:512
  230.4 1.3 copy-start.2
  231.8 5.3 %copy-start.16 = (f32[4,96,128]{2,1,0:T(8,128)S(1)}, f32[4,96,128]{2,1,0:T(8,128)}, u32[]{:S(2)}) copy-start(f32[4,96,128]{2,1,0:T(8,128)} %slice.13) | copy-start | bytes 589828
  231.8 5.3 %copy-start.28 = (f32[4,6,16,128]{3,2,1,0:T(8,128)S(1)}, f32[4,6,16,128]{3,2,1,0:T(8,128)}, u32[]{:S(2)}) copy-start(f32[4,6,16,128]{3,2,1,0:T(8,128)} %copy-done.26) | copy-start | bytes 589828
  231.8 5.3 %copy-start.31 = (f32[4,6,16,128]{3,2,1,0:T(8,128)S(1)}, f32[4,6,16,128]{3,2,1,0:T(8,128)}, u32[]{:S(2)}) copy-start(f32[4,6,16,128]{3,2,1,0:T(8,128)} %copy-done.29) | copy-start | bytes 589828
  231.8 5.3 %copy-start.34 = (f32[4,6,16,128]{3,2,1,0:T(8,128)S(1)}, f32[4,6,16,128]{3,2,1,0:T(8,128)}, u32[]{:S(2)}) copy-start(f32[4,6,16,128]{3,2,1,0:T(8,128)} %copy-done.32) | copy-start | bytes 589828
  231.8 33.2 %all-to-all-start.6 = ((f32[32,2,64,128]{3,2,1,0:T(8,128)}), f32[32,2,64,128]{3,2,1,0:T(8,128)S(1)}, u32[]{:S(2)}, u32[]{:S(2)}) async-start(f32[32,2,64,128]{3,2,1,0:T(8,128)} %copy-done.2), calls=%async_computation.6 | async-start | bytes 4194304 | tf_op jit(solution)/shard_map/all_to_all | solution.py:512
  240.8 24.2 %copy-start.19 = (bf16[2,256,256]{2,1,0:T(8,128)(2,1)S(1)}, bf16[2,256,256]{2,1,0:T(8,128)(2,1)}, u32[]{:S(2)}) copy-start(bf16[2,256,256]{2,1,0:T(8,128)(2,1)} %constant.43.clone.back_matrices) | copy-start | bytes 786436
  265.0 1.6 copy-start.4
  (35 other events, 32.0 us)

commit v4 on v3

--- a/solution.py
+++ b/solution.py
@@ -23,8 +23,7 @@
 depth = 3
 ring = 8
 quarter = 16
-cell_start = 8 * rows
-freq_start = cell_start + depth * 2 * quarter
+freq_start = depth * 2 * quarter
 message = freq_start + sub
 
 
@@ -64,21 +63,10 @@
     return split_bf16(np.block([[real, -imag], [imag, real]]))
 
 
-def y_turns():
-    angle = two_pi / length * (np.arange(outer)[:, None] * np.arange(inner)[None, :])
-    return np.cos(angle).astype(np.float32), np.sin(angle).astype(np.float32)
-
-
 def x_turns():
     upper = (np.arange(inner) >= half).astype(np.int64)
     k = 2 * np.arange(outer // 2)[:, None, None] + upper[None, None, :]
     angle = two_pi / length * (k * np.arange(inner)[None, :, None])
-    return np.cos(angle).astype(np.float32), np.sin(angle).astype(np.float32)
-
-
-def lane_turns():
-    upper = (np.arange(inner) >= half).astype(np.float64)
-    angle = two_pi / outer * (np.arange(outer // 2)[:, None] * upper[None, :])
     return np.cos(angle).astype(np.float32), np.sin(angle).astype(np.float32)
 
 
@@ -103,6 +91,18 @@
     for c in sin_fit[-2::-1]:
         sine = sine * square + c
     return cosine, sine * z
+
+
+def fill_y_turns(turns):
+    k = lax.broadcasted_iota(jnp.int32, (outer, inner), 0)
+    b = lax.broadcasted_iota(jnp.int32, (outer, inner), 1)
+    turns[0], turns[1] = cis((k * b).astype(jnp.float32) * (1.0 / length))
+
+
+def fill_lane_turns(turns):
+    a = lax.broadcasted_iota(jnp.int32, (outer // 2, inner), 0)
+    lane = lax.broadcasted_iota(jnp.int32, (outer // 2, inner), 1)
+    turns[0], turns[1] = cis(jnp.where(lane < half, 0, a).astype(jnp.float32) * (1.0 / outer))
 
 
 def times(a, b):
@@ -223,25 +223,29 @@
             write(2 * (k + n) + 1, one[:, inner:])
 
 
-def start_kernel(freqs, wavefield, velocity, matrices, turns, out, spectrum):
+def carve_kernel(place, freqs, velocity, *pieces):
+    for n, piece in enumerate(pieces):
+        first = (place[3] + n) % 4 * quarter
+        for level in range(depth):
+            for t in range(2):
+                at = (2 * level + t) * quarter
+                here = pl.ds(pl.multiple_of(first, quarter), quarter)
+                piece[at : at + quarter, :] = velocity[level, here, t * inner : (t + 1) * inner]
+        piece[freq_start:, :] = jnp.full((sub, inner), freqs[0], jnp.float32)
+
+
+def start_kernel(wavefield, matrices, out, spectrum, turns):
+    fill_y_turns(turns)
+
     def read(here, a):
         columns = slice(a * inner, (a + 1) * inner)
         return wavefield[0, 0, here, columns], wavefield[1, 0, here, columns]
 
     def write(part, value):
         y, x, c = part // 8, part // 2 % 4, part % 2
-        place = (4 * c + x) * rows
-        out[y, place : place + rows, :] = value
+        out[y, 4 * c + x] = value
 
     forward_y(read, write, spectrum, matrices, turns)
-    for y in range(4):
-        for level in range(depth):
-            for t in range(2):
-                place = cell_start + (2 * level + t) * quarter
-                out[y, place : place + quarter, :] = velocity[
-                    level, y * quarter : (y + 1) * quarter, t * inner : (t + 1) * inner
-                ]
-        out[y, freq_start:, :] = jnp.full((sub, inner), freqs[0], jnp.float32)
 
 
 def combine_kernel(
@@ -250,12 +254,13 @@
     weights,
     back_matrices,
     matrices,
-    turns,
     out,
     fields,
     summed,
     spectrum,
+    turns,
 ):
+    fill_y_turns(turns)
     turn_cos, turn_sin = turns[0], turns[1]
     matrix = (back_matrices[0], back_matrices[1])
     for branch in range(2):
@@ -307,27 +312,26 @@
     forward_y(read, write, spectrum, matrices, turns)
 
 
-def weigh_kernel(level, place, freqs, ref_slow, *refs):
+def weigh(level, place, freqs, ref_slow, tiles, weights):
     def full(value):
         return jnp.full((sub, inner), value, jnp.float32)
 
     lower, upper = full(ref_slow[level, 0]), full(ref_slow[level, 1])
-    pace = depth_step * full(freqs[place[0]])
+    pace = depth_step * full(freqs[place[4]])
     inverse_gap = 1.0 / (upper - lower)
     turn = cis(pace * (lower - upper))
 
-    tiles, weights = refs[:ring], refs[ring]
     z = 2 * place[0] + place[1]
     for n in range(ring):
         source = (z + n) % ring
         tile = tiles[n]
 
         def step(c, carry, source=source, tile=tile):
-            from_y = c // 2
-            inside = pl.ds(pl.multiple_of(c % 2 * sub, sub), sub)
+            from_y = (place[3] + 4 - c // 2) % 4
             here = pl.ds(pl.multiple_of(source // 2 * quarter + c % 2 * sub, sub), sub)
             for t in range(2):
-                slowness = 1.0 / tile[from_y, 2 * level + t, inside, :]
+                first = (2 * level + t) * quarter + c % 2 * sub
+                slowness = 1.0 / tile[c // 2, pl.ds(pl.multiple_of(first, sub), sub), :]
                 excess = slowness - lower
                 upper_weight = jnp.clip(excess * inverse_gap, 0.0, 1.0)
                 lower_weight = 1.0 - upper_weight
@@ -350,7 +354,7 @@
     fy = fy * fy
     squares = []
     for branch in range(2):
-        wave = jnp.full((sub, inner), freqs[place[0]]) * jnp.full((sub, inner), ref_slow[level, branch])
+        wave = jnp.full((sub, inner), freqs[place[4]]) * jnp.full((sub, inner), ref_slow[level, branch])
         squares.append(wave * wave)
 
     def at(c, k):
@@ -373,20 +377,23 @@
     return at
 
 
-def propagator_kernel(level, place, freqs, ref_slow, table):
-    at = propagators(level, place, freqs, ref_slow)
-
-    def step(c, carry):
-        here = block_rows(c)
-        second_half = pl.ds(pl.multiple_of(inner + c * sub, sub), sub)
-        for k in range(outer // 2):
-            columns = slice(k * inner, (k + 1) * inner)
-            for branch, factor in enumerate(at(c, k)):
-                table[branch, here, columns] = factor[0]
-                table[branch, second_half, columns] = factor[1]
-        return carry
-
-    lax.fori_loop(0, inner // sub, step, 0)
+def tables_kernel(place, freqs, ref_slow, *refs):
+    tiles, tables, weights = refs[:ring], refs[ring : ring + depth], refs[ring + depth :]
+    for level in range(depth):
+        at = propagators(level, place, freqs, ref_slow)
+
+        def step(c, carry, at=at, table=tables[level]):
+            here = block_rows(c)
+            second_half = pl.ds(pl.multiple_of(inner + c * sub, sub), sub)
+            for k in range(outer // 2):
+                columns = slice(k * inner, (k + 1) * inner)
+                for branch, factor in enumerate(at(c, k)):
+                    table[branch, here, columns] = factor[0]
+                    table[branch, second_half, columns] = factor[1]
+            return carry
+
+        lax.fori_loop(0, inner // sub, step, 0)
+        weigh(level, place, freqs, ref_slow, tiles, weights[level])
 
 
 def slab_rows(a, top, c):
@@ -409,11 +416,12 @@
     there_matrices,
     back_matrices,
     turns,
-    lane_turn,
     out,
     spectrum,
     shifted,
+    lane_turn,
 ):
+    fill_lane_turns(lane_turn)
     lane = lax.broadcasted_iota(jnp.int32, (sub, inner), 1)
     low_lanes = lane < half
     groups = outer // 2
@@ -529,60 +537,65 @@
 
 
 def shards(wavefield, freqs, velocity, ref_slow):
-    zh, zl = lax.axis_index("zh"), lax.axis_index("zl")
-    part = (lax.axis_index("y") * 4 + lax.axis_index("x")) * 2 + lax.axis_index("c")
-    place = jnp.stack([zh, zl, part])
+    zh, zl, y = lax.axis_index("zh"), lax.axis_index("zl"), lax.axis_index("y")
+    part = (y * 4 + lax.axis_index("x")) * 2 + lax.axis_index("c")
+    place = jnp.stack([zh, zl, part, y, (y + 4 - zh) % 4])
 
     fy_matrix = np.stack(forward_y_matrix())
     iy_matrix = np.stack(inverse_y_matrix())
     fx_matrix = np.stack(x_matrix(-1))
     ix_matrix = np.stack(x_matrix(1))
-    turn_y = np.stack(y_turns())
     turn_x = np.stack(x_turns())
-    turn_lane = np.stack(lane_turns())
 
     plane = ("y", "x", "c")
     packed = (parts, rows, inner)
     spectrum_shape = (outer, rows, 2 * inner)
+    y_turns_shape = (2, outer, inner)
     folded_shape = (2 * inner, length // 2)
+
+    pieces = call(carve_kernel, [(message, inner)] * 4, [], (place, freqs), (velocity,))
+    pieces = [
+        lax.ppermute(piece, "y", [(m, (m + n) % 4) for m in range(4)]) if n else piece
+        for n, piece in enumerate(pieces)
+    ]
+    tile = jnp.stack(pieces)
+    tiles = around_z(tile)
+    common = (place, tile[:, freq_start, 0], ref_slow)
     (sent,) = call(
         start_kernel,
-        [(4, message, inner)],
-        [spectrum_shape],
-        (freqs,),
-        (wavefield, velocity, fy_matrix, turn_y),
+        [(4, 8, rows, inner)],
+        [spectrum_shape, y_turns_shape],
+        (),
+        (wavefield, fy_matrix),
     )
-    sent = exchange(sent, ("y",))
-    freqs = sent[:, freq_start, 0]
-    tile = sent[:, cell_start:freq_start].reshape(4, 2 * depth, quarter, inner)
-    arrived = exchange(sent[:, :cell_start].reshape(packed), ("zh", "c", "x"))
-    arrived, tile = lax.optimization_barrier((arrived, tile))
-    tiles = around_z(tile)
-    common = (place, freqs, ref_slow)
+    sent = exchange(sent, ("y",)).reshape(packed)
+    sent, *tiles = lax.optimization_barrier((sent, *tiles))
+    arrived = exchange(sent, ("zh", "c", "x"))
+    tables = call(
+        tables_kernel,
+        [(2, *folded_shape)] * depth + [(4, outer, rows, inner)] * depth,
+        [],
+        common,
+        tiles,
+    )
     for level in range(depth):
         if level:
             arrived = exchange(sent, plane)
-        (table,) = call(
-            functools.partial(propagator_kernel, level), [(2, *folded_shape)], [], common, ()
-        )
         (shifted,) = call(
             functools.partial(shift_kernel, plane_rows if level else slab_rows),
             [(parts, 2, rows, inner)],
-            [folded_shape, (2, *folded_shape)],
+            [folded_shape, (2, *folded_shape), (2, outer // 2, inner)],
             (),
-            (arrived.reshape(length, inner), table, fx_matrix, ix_matrix, turn_x, turn_lane),
+            (arrived.reshape(length, inner), tables[level], fx_matrix, ix_matrix, turn_x),
         )
         moved = exchange(shifted, plane)
-        (weights,) = call(
-            functools.partial(weigh_kernel, level), [(4, outer, rows, inner)], [], common, tiles
-        )
         last = level == depth - 1
         (sent,) = call(
             functools.partial(combine_kernel, last),
             [(4, 2, quarter, length) if last else packed],
-            [(2, *spectrum_shape), (2, outer, rows, inner), spectrum_shape],
+            [(2, *spectrum_shape), (2, outer, rows, inner), spectrum_shape, y_turns_shape],
             (),
-            (moved, weights, iy_matrix, fy_matrix, turn_y),
+            (moved, tables[depth + level], iy_matrix, fy_matrix),
         )
     back = exchange(exchange(sent, ("zh",)), ("y",))
     return back.transpose(1, 0, 2, 3).reshape(2, 1, rows, length)

time: 321 us -> 302 us (0.941)
  blocking collectives: 70.3 us -> 188 us
  waiting for transfers between devices: 103 us -> 16.8 us
  local copies, waits for them, and re-layouts: 46 us -> 20.8 us
  starting transfers between devices: 52.5 us -> 31.9 us
  Pallas kernels: 44.9 us -> 40.1 us
    all_to_all x3 -> x7, blocking collectives: 70.3 us -> 188 us  [exchange(): return lax.all_to_all(values, axes, split_axis=0, concat_axis=0, tiled=True)]
    all_to_all x6 -> x2, waiting for transfers between devices: 87.8 us -> 3.87 us  [exchange(): return lax.all_to_all(values, axes, split_axis=0, concat_axis=0, tiled=True)]
    all_to_all x6 -> x2, starting transfers between devices: 41.7 us -> 10.3 us  [exchange(): return lax.all_to_all(values, axes, split_axis=0, concat_axis=0, tiled=True)]
    unnamed x109 -> x59, local copies, waits for them, and re-layouts: 42.1 us -> 19.5 us
    ppermute x4, waiting for transfers between devices: 15.6 us -> 0.01 us  [around_z(): above = lax.ppermute(above, axes, down)]
    ppermute x3, waiting for transfers between devices: 0.01 us -> 10.1 us  [around_z(): below = lax.ppermute(below, axes, up)]
    ppermute x4, starting transfers between devices: 9.19 us -> 15.6 us  [around_z(): above = lax.ppermute(above, axes, down)]
    ppermute x0 -> x3, starting transfers between devices: none -> 5.9 us  [shards(): lax.ppermute(piece, 'y', [(m, (m + n) % 4) for m in range(4)])]
  transfers between devices with their start and end apart: 13 -> 12, of which waited for: 9 -> 6; matrix products, arithmetic and copies ran while one was open for 1% -> 0% of each run, Pallas kernels for 5% -> 5%
where the time goes in v4:
time: 302 us; the launch traced here: 299 us
  blocking collectives  188 us (62%)
  Pallas kernels  40.1 us (13%)
  starting transfers between devices  31.9 us (11%)
  local copies, waits for them, and re-layouts  20.8 us (7%)
  waiting for transfers between devices  16.8 us (6%)
    all_to_all x7, blocking collectives, exchange(): return lax.all_to_all(values, axes, split_axis=0, concat_axis=0, tiled=True)  188 us
    pallas_call x9, Pallas kernels, call(): pl.pallas_call(kernel, out_shape=[jax.ShapeDtypeStruct(s, jnp.float32) fo...  40.1 us
    unnamed x59, local copies, waits for them, and re-layouts  19.5 us
    ppermute x4, starting transfers between devices, around_z(): above = lax.ppermute(above, axes, down)  15.6 us
    all_to_all x2, starting transfers between devices, exchange(): return lax.all_to_all(values, axes, split_axis=0, concat_axis=0, tiled=True)  10.3 us
    ppermute x3, waiting for transfers between devices, around_z(): below = lax.ppermute(below, axes, up)  10.1 us
  transfers between devices with their start and end apart: 12, of which 6 were waited for; matrix products, arithmetic and copies ran while one was open for 0% of the time, Pallas kernels for 5%

profile of v4, /device:TPU:2, one launch (start us, length us, event | category | flops | bytes accessed | tf_op | source)
XLA Modules:
  0.0 298.5 jit_solution(12227108754965090067)
XLA Ops:
  2.2 1.7 collective-permute-start
  3.9 2.9 collective-permute-start.1
  8.2 1.4 collective-permute-done.1
  9.5 1.4 collective-permute-done.2
  11.0 5.9 %collective-permute-start.3 = (f32[4,104,128]{2,1,0:T(8,128)S(1)}, f32[4,104,128]{2,1,0:T(8,128)S(1)}, u32[]{:S(2)}, u32[]{:S(2)}) collective-permute-start(f32[4,104,128]{2,1,0:T(8,128)S(1)} %pad_maximum_fusion.refs_0_), channel_id=1, source_target_pairs={{0,152},{128,0},{8,128},{136,8},{16,136},{144,16},{24,144},{152,24... | collective-permute-start | bytes 638984 | tf_op jit(solution)/shard_map/ppermute | solution.py:531
  19.1 2.0 shard_map.91
  21.0 4.4 %all-to-all-start = ((f32[4,8,64,128]{3,2,1,0:T(8,128)}), f32[4,8,64,128]{3,2,1,0:T(8,128)}, u32[]{:S(2)}, u32[]{:S(2)}) async-start(f32[4,8,64,128]{3,2,1,0:T(8,128)} %shard_map.91), calls=%async_computation | async-start | bytes 2097152 | tf_op jit(solution)/shard_map/all_to_all | solution.py:520
  25.6 3.2 %collective-permute-start.4 = (f32[4,104,128]{2,1,0:T(8,128)S(1)}, f32[4,104,128]{2,1,0:T(8,128)S(1)}, u32[]{:S(2)}, u32[]{:S(2)}) collective-permute-start(f32[4,104,128]{2,1,0:T(8,128)S(1)} %collective-permute-done.3.refs_1_), channel_id=1, source_target_pairs={{0,152},{128,0},{8,128},{136,8},{16,136},{144,16},{24,144},{152,24... | collective-permute-start | bytes 638984 | tf_op jit(solution)/shard_map/ppermute | solution.py:531
  28.8 3.8 %collective-permute-done.7.refs_7_ = f32[4,104,128]{2,1,0:T(8,128)S(1)} collective-permute-done((f32[4,104,128]{2,1,0:T(8,128)S(1)}, f32[4,104,128]{2,1,0:T(8,128)S(1)}, u32[]{:S(2)}, u32[]{:S(2)}) %collective-permute-start.7) | collective-permute-done | bytes 213024 | tf_op jit(solution)/shard_map/ppermute | solution.py:534
  32.6 3.2 %collective-permute-start.5 = (f32[4,104,128]{2,1,0:T(8,128)S(1)}, f32[4,104,128]{2,1,0:T(8,128)S(1)}, u32[]{:S(2)}, u32[]{:S(2)}) collective-permute-start(f32[4,104,128]{2,1,0:T(8,128)S(1)} %collective-permute-done.4.refs_2_), channel_id=1, source_target_pairs={{0,152},{128,0},{8,128},{136,8},{16,136},{144,16},{24,144},{152,24... | collective-permute-start | bytes 638984 | tf_op jit(solution)/shard_map/ppermute | solution.py:531
  35.8 3.8 %collective-permute-done.8.refs_6_ = f32[4,104,128]{2,1,0:T(8,128)S(1)} collective-permute-done((f32[4,104,128]{2,1,0:T(8,128)S(1)}, f32[4,104,128]{2,1,0:T(8,128)S(1)}, u32[]{:S(2)}, u32[]{:S(2)}) %collective-permute-start.8) | collective-permute-done | bytes 213024 | tf_op jit(solution)/shard_map/ppermute | solution.py:534
  40.3 3.2 %collective-permute-start.6 = (f32[4,104,128]{2,1,0:T(8,128)S(1)}, f32[4,104,128]{2,1,0:T(8,128)S(1)}, u32[]{:S(2)}, u32[]{:S(2)}) collective-permute-start(f32[4,104,128]{2,1,0:T(8,128)S(1)} %collective-permute-done.5.refs_3_), channel_id=1, source_target_pairs={{0,152},{128,0},{8,128},{136,8},{16,136},{144,16},{24,144},{152,24... | collective-permute-start | bytes 638984 | tf_op jit(solution)/shard_map/ppermute | solution.py:531
  44.3 2.5 collective-permute-done.9.refs_5_
  48.1 5.9 %all-to-all-start.1 = ((f32[32,64,128]{2,1,0:T(8,128)}), f32[32,64,128]{2,1,0:T(8,128)S(1)}, u32[]{:S(2)}, u32[]{:S(2)}) async-start(f32[32,64,128]{2,1,0:T(8,128)} %bitcast), calls=%async_computation.1 | async-start | bytes 2097152 | tf_op jit(solution)/shard_map/all_to_all | solution.py:520
  57.9 12.9 %shard_map.93 = (f32[2,256,1024]{2,1,0:T(8,128)S(1)}, f32[2,256,1024]{2,1,0:T(8,128)S(1)}, f32[2,256,1024]{2,1,0:T(8,128)S(1)}, f32[4,16,64,128]{3,2,1,0:T(8,128...) custom-call(s32[5]{0:T(128)S(1)} %stack.38.place, f32[4]{0:T(128)S(1)} %slice_reduce_fusion.freqs, ...), custom_call_target="tpu_custom_call" | custom-call | tf_op jit(solution)/shard_map/pallas_call | solution.py:509
  76.3 1.4 copy-done.14
  77.7 1.4 copy-done.16
  79.1 3.9 %all-to-all-done.1 = f32[32,64,128]{2,1,0:T(8,128)S(1)} async-done(((f32[32,64,128]{2,1,0:T(8,128)}), f32[32,64,128]{2,1,0:T(8,128)S(1)}, u32[]{:S(2)}, u32[]{:S(2)}) %all-to-all-start.1) | async-done | bytes 1048608 | tf_op jit(solution)/shard_map/all_to_all | solution.py:520
  82.9 1.6 copy-done.11
  84.5 5.6 %shard_map.94 = f32[32,2,64,128]{3,2,1,0:T(8,128)S(1)} custom-call(f32[2048,128]{1,0:T(8,128)S(1)} %bitcast.17, f32[2,256,1024]{2,1,0:T(8,128)S(1)} %copy-done.11, bf16[2,256,256]{2,1,0:T(8,128)(2,1)S(1)} %copy-done.5, bf16[2,256,256]{2,1,0:T(8,128)(2,1)S(1)} %copy-done.4, f32[2,8,128,128]{3,2,1,0:T(8,128)S(1)} %copy-done), custom_call_target="tpu_custom_call" | custom-call | tf_op jit(solution)/shard_map/pallas_call | solution.py:509
  90.1 35.4 %all_to_all.45.moved = f32[32,2,64,128]{3,2,1,0:T(8,128)S(1)} all-to-all(f32[32,2,64,128]{3,2,1,0:T(8,128)S(1)} %shard_map.94), channel_id=1, replica_groups=mesh['zl'=2,'y'=4,'zh'=4,'x'=4,'c'=2] {'y','x','c'}, dimensions={0} | all-to-all | bytes 4194304 | tf_op jit(solution)/shard_map/all_to_all | solution.py:520
  125.5 3.0 shard_map.95
  128.5 20.8 %all_to_all.46 = f32[32,64,128]{2,1,0:T(8,128)S(1)} all-to-all(f32[32,64,128]{2,1,0:T(8,128)S(1)} %shard_map.95), channel_id=1, replica_groups=mesh['zl'=2,'y'=4,'zh'=4,'x'=4,'c'=2] {'y','x','c'}, dimensions={0} | all-to-all | bytes 2097152 | tf_op jit(solution)/shard_map/all_to_all | solution.py:520
  149.3 5.6 %shard_map.96 = f32[32,2,64,128]{3,2,1,0:T(8,128)S(1)} custom-call(f32[2048,128]{1,0:T(8,128)S(1)} %bitcast.19, f32[2,256,1024]{2,1,0:T(8,128)S(1)} %copy-done.9, bf16[2,256,256]{2,1,0:T(8,128)(2,1)S(1)} %copy-done.5, bf16[2,256,256]{2,1,0:T(8,128)(2,1)S(1)} %copy-done.4, f32[2,8,128,128]{3,2,1,0:T(8,128)S(1)} %copy-done), custom_call_target="tpu_custom_call" | custom-call | tf_op jit(solution)/shard_map/pallas_call | solution.py:509
  155.0 32.1 %all_to_all.47.moved = f32[32,2,64,128]{3,2,1,0:T(8,128)S(1)} all-to-all(f32[32,2,64,128]{3,2,1,0:T(8,128)S(1)} %shard_map.96), channel_id=1, replica_groups=mesh['zl'=2,'y'=4,'zh'=4,'x'=4,'c'=2] {'y','x','c'}, dimensions={0} | all-to-all | bytes 4194304 | tf_op jit(solution)/shard_map/all_to_all | solution.py:520
  187.0 3.0 shard_map.97
  190.0 20.8 %all_to_all.48 = f32[32,64,128]{2,1,0:T(8,128)S(1)} all-to-all(f32[32,64,128]{2,1,0:T(8,128)S(1)} %shard_map.97), channel_id=1, replica_groups=mesh['zl'=2,'y'=4,'zh'=4,'x'=4,'c'=2] {'y','x','c'}, dimensions={0} | all-to-all | bytes 2097152 | tf_op jit(solution)/shard_map/all_to_all | solution.py:520
  210.8 5.6 %shard_map.98 = f32[32,2,64,128]{3,2,1,0:T(8,128)S(1)} custom-call(f32[2048,128]{1,0:T(8,128)S(1)} %bitcast.18, f32[2,256,1024]{2,1,0:T(8,128)S(1)} %copy-done.7, bf16[2,256,256]{2,1,0:T(8,128)(2,1)S(1)} %copy-done.5, bf16[2,256,256]{2,1,0:T(8,128)(2,1)S(1)} %copy-done.4, f32[2,8,128,128]{3,2,1,0:T(8,128)S(1)} %copy-done), custom_call_target="tpu_custom_call" | custom-call | tf_op jit(solution)/shard_map/pallas_call | solution.py:509
  216.5 32.1 %all_to_all.49.moved = f32[32,2,64,128]{3,2,1,0:T(8,128)S(1)} all-to-all(f32[32,2,64,128]{3,2,1,0:T(8,128)S(1)} %shard_map.98), channel_id=1, replica_groups=mesh['zl'=2,'y'=4,'zh'=4,'x'=4,'c'=2] {'y','x','c'}, dimensions={0} | all-to-all | bytes 4194304 | tf_op jit(solution)/shard_map/all_to_all | solution.py:520
  248.5 1.9 shard_map.99
  250.5 28.3 %all_to_all.50 = f32[4,2,16,2048]{3,2,1,0:T(8,128)S(1)} all-to-all(f32[4,2,16,2048]{3,2,1,0:T(8,128)S(1)} %shard_map.99), channel_id=1, replica_groups=mesh['zl'=2,'y'=4,'zh'=4,'x'=4,'c'=2] {'zh'}, dimensions={0} | all-to-all | bytes 2097152 | tf_op jit(solution)/shard_map/all_to_all | solution.py:520
  278.8 18.6 %all_to_all.51 = f32[4,2,16,2048]{3,2,1,0:T(8,128)S(1)} all-to-all(f32[4,2,16,2048]{3,2,1,0:T(8,128)S(1)} %all_to_all.50), channel_id=1, replica_groups=mesh['zl'=2,'y'=4,'zh'=4,'x'=4,'c'=2] {'y'}, dimensions={0} | all-to-all | bytes 2097152 | tf_op jit(solution)/shard_map/all_to_all | solution.py:520
  (71 shorter events, 18.4 us)
Async XLA Ops:
  2.2 5.9 %collective-permute-start = (f32[104,128]{1,0:T(8,128)S(1)}, f32[104,128]{1,0:T(8,128)S(1)}, u32[]{:S(2)}, u32[]{:S(2)}) collective-permute-start(f32[104,128]{1,0:T(8,128)S(1)} %get-tuple-element.25), channel_id=1, source_target_pairs={{0,32},{32,64},{64,96},{96,0},{1,33},{33,65},{65,97},{97,1},{2,34}... | collective-permute-start | bytes 159752 | tf_op jit(solution)/shard_map/ppermute | solution.py:558
  3.9 5.6 %collective-permute-start.1 = (f32[104,128]{1,0:T(8,128)S(1)}, f32[104,128]{1,0:T(8,128)S(1)}, u32[]{:S(2)}, u32[]{:S(2)}) collective-permute-start(f32[104,128]{1,0:T(8,128)S(1)} %get-tuple-element.26), channel_id=1, source_target_pairs={{0,64},{32,96},{64,0},{96,32},{1,65},{33,97},{65,1},{97,33},{2,66}... | collective-permute-start | bytes 159752 | tf_op jit(solution)/shard_map/ppermute | solution.py:558
  6.8 4.1 %collective-permute-start.2 = (f32[104,128]{1,0:T(8,128)S(1)}, f32[104,128]{1,0:T(8,128)S(1)}, u32[]{:S(2)}, u32[]{:S(2)}) collective-permute-start(f32[104,128]{1,0:T(8,128)S(1)} %get-tuple-element.27), channel_id=1, source_target_pairs={{0,96},{32,0},{64,32},{96,64},{1,97},{33,1},{65,33},{97,65},{2,98}... | collective-permute-start | bytes 159752 | tf_op jit(solution)/shard_map/ppermute | solution.py:558
  11.0 14.6 %collective-permute-start.3 = (f32[4,104,128]{2,1,0:T(8,128)S(1)}, f32[4,104,128]{2,1,0:T(8,128)S(1)}, u32[]{:S(2)}, u32[]{:S(2)}) collective-permute-start(f32[4,104,128]{2,1,0:T(8,128)S(1)} %pad_maximum_fusion.refs_0_), channel_id=1, source_target_pairs={{0,152},{128,0},{8,128},{136,8},{16,136},{144,16},{24,144},{152,24... | collective-permute-start | bytes 638984 | tf_op jit(solution)/shard_map/ppermute | solution.py:531
  16.9 0.9 copy-start.1
  17.8 1.2 copy-start.18
  21.0 33.0 %copy-start.28 = (f32[3,2]{0,1:T(2,128)S(1)}, f32[3,2]{0,1:T(2,128)}, u32[]{:S(2)}) copy-start(f32[3,2]{0,1:T(2,128)} %param.12) | copy-start | bytes 76
  21.0 26.4 %all-to-all-start = ((f32[4,8,64,128]{3,2,1,0:T(8,128)}), f32[4,8,64,128]{3,2,1,0:T(8,128)}, u32[]{:S(2)}, u32[]{:S(2)}) async-start(f32[4,8,64,128]{3,2,1,0:T(8,128)} %shard_map.91), calls=%async_computation | async-start | bytes 2097152 | tf_op jit(solution)/shard_map/all_to_all | solution.py:520
  25.4 57.5 %copy-start = (f32[2,8,128,128]{3,2,1,0:T(8,128)S(1)}, f32[2,8,128,128]{3,2,1,0:T(8,128)}, u32[]{:S(2)}) copy-start(f32[2,8,128,128]{3,2,1,0:T(8,128)} %constant.47.clone.turns) | copy-start | bytes 3145732
  25.4 57.5 %copy-start.4 = (bf16[2,256,256]{2,1,0:T(8,128)(2,1)S(1)}, bf16[2,256,256]{2,1,0:T(8,128)(2,1)}, u32[]{:S(2)}) copy-start(bf16[2,256,256]{2,1,0:T(8,128)(2,1)} %constant.46.clone.back_matrices) | copy-start | bytes 786436
  25.4 57.5 %copy-start.5 = (bf16[2,256,256]{2,1,0:T(8,128)(2,1)S(1)}, bf16[2,256,256]{2,1,0:T(8,128)(2,1)}, u32[]{:S(2)}) copy-start(bf16[2,256,256]{2,1,0:T(8,128)(2,1)} %constant.45.clone.there_matrices) | copy-start | bytes 786436
  25.5 7.1 %collective-permute-start.7 = (f32[4,104,128]{2,1,0:T(8,128)S(1)}, f32[4,104,128]{2,1,0:T(8,128)S(1)}, u32[]{:S(2)}, u32[]{:S(2)}) collective-permute-start(f32[4,104,128]{2,1,0:T(8,128)S(1)} %pad_maximum_fusion.refs_0_), channel_id=1, source_target_pairs={{152,0},{0,128},{128,8},{8,136},{136,16},{16,144},{144,24},{24,152... | collective-permute-start | bytes 638984 | tf_op jit(solution)/shard_map/ppermute | solution.py:534
  25.6 7.0 %collective-permute-start.4 = (f32[4,104,128]{2,1,0:T(8,128)S(1)}, f32[4,104,128]{2,1,0:T(8,128)S(1)}, u32[]{:S(2)}, u32[]{:S(2)}) collective-permute-start(f32[4,104,128]{2,1,0:T(8,128)S(1)} %collective-permute-done.3.refs_1_), channel_id=1, source_target_pairs={{0,152},{128,0},{8,128},{136,8},{16,136},{144,16},{24,144},{152,24... | collective-permute-start | bytes 638984 | tf_op jit(solution)/shard_map/ppermute | solution.py:531
  32.6 7.1 %collective-permute-start.8 = (f32[4,104,128]{2,1,0:T(8,128)S(1)}, f32[4,104,128]{2,1,0:T(8,128)S(1)}, u32[]{:S(2)}, u32[]{:S(2)}) collective-permute-start(f32[4,104,128]{2,1,0:T(8,128)S(1)} %collective-permute-done.7.refs_7_), channel_id=1, source_target_pairs={{152,0},{0,128},{128,8},{8,136},{136,16},{16,144},{144,24},{24,152... | collective-permute-start | bytes 638984 | tf_op jit(solution)/shard_map/ppermute | solution.py:534
  32.6 7.7 %collective-permute-start.5 = (f32[4,104,128]{2,1,0:T(8,128)S(1)}, f32[4,104,128]{2,1,0:T(8,128)S(1)}, u32[]{:S(2)}, u32[]{:S(2)}) collective-permute-start(f32[4,104,128]{2,1,0:T(8,128)S(1)} %collective-permute-done.4.refs_2_), channel_id=1, source_target_pairs={{0,152},{128,0},{8,128},{136,8},{16,136},{144,16},{24,144},{152,24... | collective-permute-start | bytes 638984 | tf_op jit(solution)/shard_map/ppermute | solution.py:531
  39.7 7.1 %collective-permute-start.9 = (f32[4,104,128]{2,1,0:T(8,128)S(1)}, f32[4,104,128]{2,1,0:T(8,128)S(1)}, u32[]{:S(2)}, u32[]{:S(2)}) collective-permute-start(f32[4,104,128]{2,1,0:T(8,128)S(1)} %collective-permute-done.8.refs_6_), channel_id=1, source_target_pairs={{152,0},{0,128},{128,8},{8,136},{136,16},{16,144},{144,24},{24,152... | collective-permute-start | bytes 638984 | tf_op jit(solution)/shard_map/ppermute | solution.py:534
  40.3 7.1 %collective-permute-start.6 = (f32[4,104,128]{2,1,0:T(8,128)S(1)}, f32[4,104,128]{2,1,0:T(8,128)S(1)}, u32[]{:S(2)}, u32[]{:S(2)}) collective-permute-start(f32[4,104,128]{2,1,0:T(8,128)S(1)} %collective-permute-done.5.refs_3_), channel_id=1, source_target_pairs={{0,152},{128,0},{8,128},{136,8},{16,136},{144,16},{24,144},{152,24... | collective-permute-start | bytes 638984 | tf_op jit(solution)/shard_map/ppermute | solution.py:531
  48.1 34.8 %all-to-all-start.1 = ((f32[32,64,128]{2,1,0:T(8,128)}), f32[32,64,128]{2,1,0:T(8,128)S(1)}, u32[]{:S(2)}, u32[]{:S(2)}) async-start(f32[32,64,128]{2,1,0:T(8,128)} %bitcast), calls=%async_computation.1 | async-start | bytes 2097152 | tf_op jit(solution)/shard_map/all_to_all | solution.py:520
  70.8 1.4 copy-start.6
  72.2 1.4 copy-start.8
  73.6 1.4 copy-start.10
  74.9 1.3 copy-start.12
  76.3 1.4 copy-start.14
  77.7 1.4 copy-start.16
  82.9 1.6 copy-start.11
  90.1 35.4 %copy-start.2 = (bf16[2,256,256]{2,1,0:T(8,128)(2,1)S(1)}, bf16[2,256,256]{2,1,0:T(8,128)(2,1)}, u32[]{:S(2)}) copy-start(bf16[2,256,256]{2,1,0:T(8,128)(2,1)} %constant.44.clone.matrices) | copy-start | bytes 786436
  90.1 35.4 %copy-start.3 = (bf16[2,256,256]{2,1,0:T(8,128)(2,1)S(1)}, bf16[2,256,256]{2,1,0:T(8,128)(2,1)}, u32[]{:S(2)}) copy-start(bf16[2,256,256]{2,1,0:T(8,128)(2,1)} %constant.48.clone.back_matrices) | copy-start | bytes 786436
  90.1 35.4 %copy-start.17 = (f32[4,16,64,128]{3,2,1,0:T(8,128)S(1)}, f32[4,16,64,128]{3,2,1,0:T(8,128)}, u32[]{:S(2)}) copy-start(f32[4,16,64,128]{3,2,1,0:T(8,128)} %copy-done.16) | copy-start | bytes 6291460
  128.5 20.8 %copy-start.9 = (f32[2,256,1024]{2,1,0:T(8,128)S(1)}, f32[2,256,1024]{2,1,0:T(8,128)}, u32[]{:S(2)}) copy-start(f32[2,256,1024]{2,1,0:T(8,128)} %copy-done.8) | copy-start | bytes 6291460
  155.0 32.1 %copy-start.15 = (f32[4,16,64,128]{3,2,1,0:T(8,128)S(1)}, f32[4,16,64,128]{3,2,1,0:T(8,128)}, u32[]{:S(2)}) copy-start(f32[4,16,64,128]{3,2,1,0:T(8,128)} %copy-done.14) | copy-start | bytes 6291460
  190.0 20.8 %copy-start.7 = (f32[2,256,1024]{2,1,0:T(8,128)S(1)}, f32[2,256,1024]{2,1,0:T(8,128)}, u32[]{:S(2)}) copy-start(f32[2,256,1024]{2,1,0:T(8,128)} %copy-done.6) | copy-start | bytes 6291460
  216.5 32.1 %copy-start.13 = (f32[4,16,64,128]{3,2,1,0:T(8,128)S(1)}, f32[4,16,64,128]{3,2,1,0:T(8,128)}, u32[]{:S(2)}) copy-start(f32[4,16,64,128]{3,2,1,0:T(8,128)} %copy-done.12) | copy-start | bytes 6291460
  (9 other events, 7.4 us)

commit v5 on v4

--- a/solution.py
+++ b/solution.py
@@ -23,7 +23,9 @@
 depth = 3
 ring = 8
 quarter = 16
-freq_start = depth * 2 * quarter
+level_rows = 2 * quarter
+cell_start = 8 * rows
+freq_start = cell_start + depth * level_rows
 message = freq_start + sub
 
 
@@ -223,18 +225,7 @@
             write(2 * (k + n) + 1, one[:, inner:])
 
 
-def carve_kernel(place, freqs, velocity, *pieces):
-    for n, piece in enumerate(pieces):
-        first = (place[3] + n) % 4 * quarter
-        for level in range(depth):
-            for t in range(2):
-                at = (2 * level + t) * quarter
-                here = pl.ds(pl.multiple_of(first, quarter), quarter)
-                piece[at : at + quarter, :] = velocity[level, here, t * inner : (t + 1) * inner]
-        piece[freq_start:, :] = jnp.full((sub, inner), freqs[0], jnp.float32)
-
-
-def start_kernel(wavefield, matrices, out, spectrum, turns):
+def start_kernel(freqs, wavefield, velocity, matrices, out, spectrum, turns):
     fill_y_turns(turns)
 
     def read(here, a):
@@ -243,9 +234,18 @@
 
     def write(part, value):
         y, x, c = part // 8, part // 2 % 4, part % 2
-        out[y, 4 * c + x] = value
+        place = (4 * c + x) * rows
+        out[y, place : place + rows, :] = value
 
     forward_y(read, write, spectrum, matrices, turns)
+    for y in range(4):
+        for level in range(depth):
+            for t in range(2):
+                place = cell_start + (2 * level + t) * quarter
+                out[y, place : place + quarter, :] = velocity[
+                    level, y * quarter : (y + 1) * quarter, t * inner : (t + 1) * inner
+                ]
+        out[y, freq_start:, :] = jnp.full((sub, inner), freqs[0], jnp.float32)
 
 
 def combine_kernel(
@@ -312,12 +312,12 @@
     forward_y(read, write, spectrum, matrices, turns)
 
 
-def weigh(level, place, freqs, ref_slow, tiles, weights):
+def weigh(level, first_level, place, freqs, ref_slow, tiles, weights):
     def full(value):
         return jnp.full((sub, inner), value, jnp.float32)
 
     lower, upper = full(ref_slow[level, 0]), full(ref_slow[level, 1])
-    pace = depth_step * full(freqs[place[4]])
+    pace = depth_step * full(freqs[place[0]])
     inverse_gap = 1.0 / (upper - lower)
     turn = cis(pace * (lower - upper))
 
@@ -327,11 +327,11 @@
         tile = tiles[n]
 
         def step(c, carry, source=source, tile=tile):
-            from_y = (place[3] + 4 - c // 2) % 4
+            from_y = c // 2
             here = pl.ds(pl.multiple_of(source // 2 * quarter + c % 2 * sub, sub), sub)
             for t in range(2):
-                first = (2 * level + t) * quarter + c % 2 * sub
-                slowness = 1.0 / tile[c // 2, pl.ds(pl.multiple_of(first, sub), sub), :]
+                first = (2 * (level - first_level) + t) * quarter + c % 2 * sub
+                slowness = 1.0 / tile[from_y, pl.ds(pl.multiple_of(first, sub), sub), :]
                 excess = slowness - lower
                 upper_weight = jnp.clip(excess * inverse_gap, 0.0, 1.0)
                 lower_weight = 1.0 - upper_weight
@@ -354,7 +354,7 @@
     fy = fy * fy
     squares = []
     for branch in range(2):
-        wave = jnp.full((sub, inner), freqs[place[4]]) * jnp.full((sub, inner), ref_slow[level, branch])
+        wave = jnp.full((sub, inner), freqs[place[0]]) * jnp.full((sub, inner), ref_slow[level, branch])
         squares.append(wave * wave)
 
     def at(c, k):
@@ -377,12 +377,11 @@
     return at
 
 
-def tables_kernel(place, freqs, ref_slow, *refs):
-    tiles, tables, weights = refs[:ring], refs[ring : ring + depth], refs[ring + depth :]
-    for level in range(depth):
+def propagator_kernel(place, freqs, ref_slow, *tables):
+    for level, table in enumerate(tables):
         at = propagators(level, place, freqs, ref_slow)
 
-        def step(c, carry, at=at, table=tables[level]):
+        def step(c, carry, at=at, table=table):
             here = block_rows(c)
             second_half = pl.ds(pl.multiple_of(inner + c * sub, sub), sub)
             for k in range(outer // 2):
@@ -393,7 +392,12 @@
             return carry
 
         lax.fori_loop(0, inner // sub, step, 0)
-        weigh(level, place, freqs, ref_slow, tiles, weights[level])
+
+
+def weigh_kernel(first_level, place, freqs, ref_slow, *refs):
+    tiles = refs[:ring]
+    for n, weights in enumerate(refs[ring:]):
+        weigh(first_level + n, first_level, place, freqs, ref_slow, tiles, weights)
 
 
 def slab_rows(a, top, c):
@@ -512,7 +516,7 @@
         in_specs=[smem] * len(scalars) + [vmem] * len(operands),
         out_specs=[vmem] * len(shapes),
         scratch_shapes=[pltpu.VMEM(s, jnp.float32) for s in scratch],
-        compiler_params=pltpu.CompilerParams(vmem_limit_bytes=28 * 1024 * 1024),
+        compiler_params=pltpu.CompilerParams(vmem_limit_bytes=12 * 1024 * 1024),
     )(*scalars, *operands)
 
 
@@ -537,9 +541,9 @@
 
 
 def shards(wavefield, freqs, velocity, ref_slow):
-    zh, zl, y = lax.axis_index("zh"), lax.axis_index("zl"), lax.axis_index("y")
-    part = (y * 4 + lax.axis_index("x")) * 2 + lax.axis_index("c")
-    place = jnp.stack([zh, zl, part, y, (y + 4 - zh) % 4])
+    zh, zl = lax.axis_index("zh"), lax.axis_index("zl")
+    part = (lax.axis_index("y") * 4 + lax.axis_index("x")) * 2 + lax.axis_index("c")
+    place = jnp.stack([zh, zl, part])
 
     fy_matrix = np.stack(forward_y_matrix())
     iy_matrix = np.stack(inverse_y_matrix())
@@ -553,34 +557,40 @@
     y_turns_shape = (2, outer, inner)
     folded_shape = (2 * inner, length // 2)
 
-    pieces = call(carve_kernel, [(message, inner)] * 4, [], (place, freqs), (velocity,))
-    pieces = [
-        lax.ppermute(piece, "y", [(m, (m + n) % 4) for m in range(4)]) if n else piece
-        for n, piece in enumerate(pieces)
-    ]
-    tile = jnp.stack(pieces)
-    tiles = around_z(tile)
-    common = (place, tile[:, freq_start, 0], ref_slow)
     (sent,) = call(
         start_kernel,
-        [(4, 8, rows, inner)],
+        [(4, message, inner)],
         [spectrum_shape, y_turns_shape],
-        (),
-        (wavefield, fy_matrix),
+        (freqs,),
+        (wavefield, velocity, fy_matrix),
     )
-    sent = exchange(sent, ("y",)).reshape(packed)
-    sent, *tiles = lax.optimization_barrier((sent, *tiles))
-    arrived = exchange(sent, ("zh", "c", "x"))
-    tables = call(
-        tables_kernel,
-        [(2, *folded_shape)] * depth + [(4, outer, rows, inner)] * depth,
-        [],
-        common,
-        tiles,
-    )
+    sent = exchange(sent, ("y",))
+    sent, cells = lax.optimization_barrier((sent[:, :cell_start], sent[:, cell_start:]))
+    common = (place, cells[:, -1, 0], ref_slow)
+    first_tile = cells[:, :level_rows]
+    later_tile = cells[:, level_rows : depth * level_rows]
+    arrived = exchange(sent.reshape(packed), ("zh", "c", "x"))
+    tables = call(propagator_kernel, [(2, *folded_shape)] * depth, [], common, ())
+    weights = []
     for level in range(depth):
         if level:
             arrived = exchange(sent, plane)
+        if level == 0:
+            arrived, first_tile, later_tile = lax.optimization_barrier(
+                (arrived, first_tile, later_tile)
+            )
+            tiles = around_z(first_tile)
+        if level == 1:
+            arrived, later_tile = lax.optimization_barrier((arrived, later_tile))
+            tiles = around_z(later_tile)
+        if level < 2:
+            weights += call(
+                functools.partial(weigh_kernel, level),
+                [(4, outer, rows, inner)] * (depth - 1 if level else 1),
+                [],
+                common,
+                tiles,
+            )
         (shifted,) = call(
             functools.partial(shift_kernel, plane_rows if level else slab_rows),
             [(parts, 2, rows, inner)],
@@ -595,7 +605,7 @@
             [(4, 2, quarter, length) if last else packed],
             [(2, *spectrum_shape), (2, outer, rows, inner), spectrum_shape, y_turns_shape],
             (),
-            (moved, tables[depth + level], iy_matrix, fy_matrix),
+            (moved, weights[level], iy_matrix, fy_matrix),
         )
     back = exchange(exchange(sent, ("zh",)), ("y",))
     return back.transpose(1, 0, 2, 3).reshape(2, 1, rows, length)

time: 302 us -> 299 us (0.990)
  blocking collectives: 188 us -> 147 us
  waiting for transfers between devices: 16.8 us -> 40.2 us
  starting transfers between devices: 31.9 us -> 44.3 us
    all_to_all x7 -> x6, blocking collectives: 188 us -> 147 us  [exchange(): return lax.all_to_all(values, axes, split_axis=0, concat_axis=0, tiled=True)]
    ppermute x4 -> x8, waiting for transfers between devices: 0.01 us -> 19.6 us  [around_z(): above = lax.ppermute(above, axes, down)]
    all_to_all x2 -> x3, waiting for transfers between devices: 3.87 us -> 20.6 us  [exchange(): return lax.all_to_all(values, axes, split_axis=0, concat_axis=0, tiled=True)]
    all_to_all x2 -> x3, starting transfers between devices: 10.3 us -> 22.3 us  [exchange(): return lax.all_to_all(values, axes, split_axis=0, concat_axis=0, tiled=True)]
    ppermute x3 -> x6, waiting for transfers between devices: 10.1 us -> 0.02 us  [around_z(): below = lax.ppermute(below, axes, up)]
    ppermute x3 -> x0, starting transfers between devices: 5.9 us -> none  [shards(): lax.ppermute(piece, 'y', [(m, (m + n) % 4) for m in range(4)])]
    ppermute x3 -> x6, starting transfers between devices: 0.09 us -> 3.4 us  [around_z(): below = lax.ppermute(below, axes, up)]
    ppermute x4 -> x8, starting transfers between devices: 15.6 us -> 18.6 us  [around_z(): above = lax.ppermute(above, axes, down)]
  transfers between devices with their start and end apart: 12 -> 17, of which waited for: 6 -> 10; matrix products, arithmetic and copies ran while one was open for 0% -> 0% of each run, Pallas kernels for 5% -> 5%
where the time goes in v5:
time: 299 us; the launch traced here: 297 us
  blocking collectives  147 us (49%)
  starting transfers between devices  44.3 us (15%)
  Pallas kernels  42.5 us (14%)
  waiting for transfers between devices  40.2 us (13%)
  local copies, waits for them, and re-layouts  21.8 us (7%)
    all_to_all x6, blocking collectives, exchange(): return lax.all_to_all(values, axes, split_axis=0, concat_axis=0, tiled=True)  147 us
    pallas_call x10, Pallas kernels, call(): pl.pallas_call(kernel, out_shape=[jax.ShapeDtypeStruct(s, jnp.float32) fo...  42.5 us
    all_to_all x3, starting transfers between devices, exchange(): return lax.all_to_all(values, axes, split_axis=0, concat_axis=0, tiled=True)  22.3 us
    all_to_all x3, waiting for transfers between devices, exchange(): return lax.all_to_all(values, axes, split_axis=0, concat_axis=0, tiled=True)  20.6 us
    ppermute x8, waiting for transfers between devices, around_z(): above = lax.ppermute(above, axes, down)  19.6 us
    unnamed x57, local copies, waits for them, and re-layouts  18.9 us
    ppermute x8, starting transfers between devices, around_z(): above = lax.ppermute(above, axes, down)  18.6 us
  transfers between devices with their start and end apart: 17, of which 10 were waited for; matrix products, arithmetic and copies ran while one was open for 0% of the time, Pallas kernels for 5%

profile of v5, /device:TPU:2, one launch (start us, length us, event | category | flops | bytes accessed | tf_op | source)
XLA Modules:
  0.0 296.8 jit_solution(16597582767405260106)
XLA Ops:
  4.8 21.7 %all_to_all.45 = f32[4,616,128]{2,1,0:T(8,128)S(1)} all-to-all(f32[4,616,128]{2,1,0:T(8,128)S(1)} %shard_map.91), channel_id=1, replica_groups=mesh['zl'=2,'y'=4,'zh'=4,'x'=4,'c'=2] {'y'}, dimensions={0} | all-to-all | bytes 2523136 | tf_op jit(solution)/shard_map/all_to_all | solution.py:524
  27.5 11.6 %all-to-all-start.1 = ((f32[32,64,128]{2,1,0:T(8,128)}), f32[32,64,128]{2,1,0:T(8,128)S(1)}, u32[]{:S(2)}, u32[]{:S(2)}) async-start(f32[32,64,128]{2,1,0:T(8,128)} %bitcast.14), calls=%async_computation.1 | async-start | bytes 2097152 | tf_op jit(solution)/shard_map/all_to_all | solution.py:524
  40.0 7.5 %shard_map.92 = (f32[2,256,1024]{2,1,0:T(8,128)S(1)}, f32[2,256,1024]{2,1,0:T(8,128)S(1)}, f32[2,256,1024]{2,1,0:T(8,128)S(1)}) custom-call(s32[3]{0:T(128)S(1)} %pad_add_fusion.place, f32[4]{0:T(128)S(1)} %slice_reduce_fusion.freqs, f32[3,2]{1,0:T(4,128)S(1)} %copy.13.ref_slow), custom_call_target="tpu_custom_call" | custom-call | tf_op jit(solution)/shard_map/pallas_call | solution.py:513
  51.6 16.0 %all-to-all-done.1 = f32[32,64,128]{2,1,0:T(8,128)S(1)} async-done(((f32[32,64,128]{2,1,0:T(8,128)}), f32[32,64,128]{2,1,0:T(8,128)S(1)}, u32[]{:S(2)}, u32[]{:S(2)}) %all-to-all-start.1) | async-done | bytes 1048608 | tf_op jit(solution)/shard_map/all_to_all | solution.py:524
  69.3 7.0 %shard_map.93 = f32[32,2,64,128]{3,2,1,0:T(8,128)} custom-call(f32[2048,128]{1,0:T(8,128)S(1)} %bitcast.11, f32[2,256,1024]{2,1,0:T(8,128)S(1)} %copy-done.19, bf16[2,256,256]{2,1,0:T(8,128)(2,1)S(1)} %copy-done.8, bf16[2,256,256]{2,1,0:T(8,128)(2,1)S(1)} %copy-done.11, f32[2,8,128,128]{3,2,1,0:T(8,128)S(1)} %copy-done), custom_call_target="tpu_custom_call" | custom-call | tf_op jit(solution)/shard_map/pallas_call | solution.py:513
  76.2 5.5 %all-to-all-start.2 = ((f32[32,2,64,128]{3,2,1,0:T(8,128)}), f32[32,2,64,128]{3,2,1,0:T(8,128)S(1)}, u32[]{:S(2)}, u32[]{:S(2)}) async-start(f32[32,2,64,128]{3,2,1,0:T(8,128)} %shard_map.93), calls=%async_computation.2 | async-start | bytes 4194304 | tf_op jit(solution)/shard_map/all_to_all | solution.py:524
  83.9 2.4 collective-permute-done.refs_1_
  88.4 2.2 collective-permute-done.1.refs_2_
  90.6 2.6 collective-permute-start.2
  95.1 3.6 %collective-permute-start.3 = (f32[4,32,128]{2,1,0:T(8,128)S(1)}, f32[4,32,128]{2,1,0:T(8,128)S(1)}, u32[]{:S(2)}, u32[]{:S(2)}) collective-permute-start(f32[4,32,128]{2,1,0:T(8,128)S(1)} %collective-permute-done.2.refs_3_), channel_id=1, source_target_pairs={{0,152},{128,0},{8,128},{136,8},{16,136},{144,16},{24,144},{152,24... | collective-permute-start | bytes 196616 | tf_op jit(solution)/shard_map/ppermute | solution.py:535
  98.7 1.9 collective-permute-done.3.refs_4_
  101.4 2.3 shard_map.94.weights
  105.1 4.5 %all-to-all-done.2.moved = f32[32,2,64,128]{3,2,1,0:T(8,128)S(1)} async-done(((f32[32,2,64,128]{3,2,1,0:T(8,128)}), f32[32,2,64,128]{3,2,1,0:T(8,128)S(1)}, u32[]{:S(2)}, u32[]{:S(2)}) %all-to-all-start.2) | async-done | bytes 2097184 | tf_op jit(solution)/shard_map/all_to_all | solution.py:524
  112.2 3.0 %shard_map.95 = f32[32,64,128]{2,1,0:T(8,128)S(1)} custom-call(f32[32,2,64,128]{3,2,1,0:T(8,128)S(1)} %all-to-all-done.2.moved, f32[4,16,64,128]{3,2,1,0:T(8,128)S(1)} %copy-done.2, bf16[2,256,256]{2,1,0:T(8,128)(2,1)S(1)} %copy-done.5, bf16[2,256,256]{2,1,0:T(8,128)(2,1)S(1)} %copy-done.4), custom_call_target="tpu_custom_call" | custom-call | tf_op jit(solution)/shard_map/pallas_call | solution.py:513
  115.3 21.4 %all_to_all.46 = f32[32,64,128]{2,1,0:T(8,128)S(1)} all-to-all(f32[32,64,128]{2,1,0:T(8,128)S(1)} %shard_map.95), channel_id=1, replica_groups=mesh['zl'=2,'y'=4,'zh'=4,'x'=4,'c'=2] {'y','x','c'}, dimensions={0} | all-to-all | bytes 2097152 | tf_op jit(solution)/shard_map/all_to_all | solution.py:524
  136.6 7.0 %shard_map.96 = f32[32,2,64,128]{3,2,1,0:T(8,128)} custom-call(f32[2048,128]{1,0:T(8,128)S(1)} %bitcast.13, f32[2,256,1024]{2,1,0:T(8,128)S(1)} %copy-done.17, bf16[2,256,256]{2,1,0:T(8,128)(2,1)S(1)} %copy-done.9, bf16[2,256,256]{2,1,0:T(8,128)(2,1)S(1)} %copy-done.12, f32[2,8,128,128]{3,2,1,0:T(8,128)S(1)} %copy-done), custom_call_target="tpu_custom_call" | custom-call | tf_op jit(solution)/shard_map/pallas_call | solution.py:513
  143.7 5.1 %all-to-all-start.4 = ((f32[32,2,64,128]{3,2,1,0:T(8,128)}), f32[32,2,64,128]{3,2,1,0:T(8,128)S(1)}, u32[]{:S(2)}, u32[]{:S(2)}) async-start(f32[32,2,64,128]{3,2,1,0:T(8,128)} %shard_map.96), calls=%async_computation.4 | async-start | bytes 4194304 | tf_op jit(solution)/shard_map/all_to_all | solution.py:524
  150.9 3.5 %collective-permute-done.7.refs_1_ = f32[4,64,128]{2,1,0:T(8,128)S(1)} collective-permute-done((f32[4,64,128]{2,1,0:T(8,128)S(1)}, f32[4,64,128]{2,1,0:T(8,128)S(1)}, u32[]{:S(2)}, u32[]{:S(2)}) %collective-permute-start.7) | collective-permute-done | bytes 131104 | tf_op jit(solution)/shard_map/ppermute | solution.py:535
  154.4 2.4 collective-permute-start.8
  156.8 2.6 collective-permute-done.8.refs_2_
  159.4 3.6 %collective-permute-start.9 = (f32[4,64,128]{2,1,0:T(8,128)S(1)}, f32[4,64,128]{2,1,0:T(8,128)S(1)}, u32[]{:S(2)}, u32[]{:S(2)}) collective-permute-start(f32[4,64,128]{2,1,0:T(8,128)S(1)} %collective-permute-done.8.refs_2_), channel_id=1, source_target_pairs={{0,152},{128,0},{8,128},{136,8},{16,136},{144,16},{24,144},{152,24... | collective-permute-start | bytes 393224 | tf_op jit(solution)/shard_map/ppermute | solution.py:535
  163.0 2.5 collective-permute-done.9.refs_3_
  165.5 3.7 %collective-permute-start.10 = (f32[4,64,128]{2,1,0:T(8,128)S(1)}, f32[4,64,128]{2,1,0:T(8,128)S(1)}, u32[]{:S(2)}, u32[]{:S(2)}) collective-permute-start(f32[4,64,128]{2,1,0:T(8,128)S(1)} %collective-permute-done.9.refs_3_), channel_id=1, source_target_pairs={{0,152},{128,0},{8,128},{136,8},{16,136},{144,16},{24,144},{152,24... | collective-permute-start | bytes 393224 | tf_op jit(solution)/shard_map/ppermute | solution.py:535
  169.2 2.5 collective-permute-done.10.refs_4_
  171.7 4.0 %shard_map.97 = (f32[4,16,64,128]{3,2,1,0:T(8,128)S(1)}, f32[4,16,64,128]{3,2,1,0:T(8,128)S(1)}) custom-call(s32[3]{0:T(128)S(1)} %pad_add_fusion.place, f32[4]{0:T(128)S(1)} %slice_reduce_fusion.freqs, f32[3,2]{1,0:T(4,128)S(1)} %copy.13.ref_slow, f32[4,64,128]{2,1,0:T(8,128)S(1)} %slice.18.refs_0_, f32[4,64,128]{2,1,0:T(8,128)S(1)} %collective-permute-done.7.refs_1_, ...), custom_call_target="tpu_custom_call" | custom-call | tf_op jit(solution)/shard_map/pallas_call | solution.py:513
  181.0 3.0 %shard_map.98 = f32[32,64,128]{2,1,0:T(8,128)S(1)} custom-call(f32[32,2,64,128]{3,2,1,0:T(8,128)S(1)} %all-to-all-done.4.moved, f32[4,16,64,128]{3,2,1,0:T(8,128)S(1)} %copy-done.23, bf16[2,256,256]{2,1,0:T(8,128)(2,1)S(1)} %copy-done.6, bf16[2,256,256]{2,1,0:T(8,128)(2,1)S(1)} %copy-done.4), custom_call_target="tpu_custom_call" | custom-call | tf_op jit(solution)/shard_map/pallas_call | solution.py:513
  184.1 23.5 %all_to_all.47 = f32[32,64,128]{2,1,0:T(8,128)S(1)} all-to-all(f32[32,64,128]{2,1,0:T(8,128)S(1)} %shard_map.98), channel_id=1, replica_groups=mesh['zl'=2,'y'=4,'zh'=4,'x'=4,'c'=2] {'y','x','c'}, dimensions={0} | all-to-all | bytes 2097152 | tf_op jit(solution)/shard_map/all_to_all | solution.py:524
  207.6 5.7 %shard_map.99 = f32[32,2,64,128]{3,2,1,0:T(8,128)S(1)} custom-call(f32[2048,128]{1,0:T(8,128)S(1)} %bitcast.12, f32[2,256,1024]{2,1,0:T(8,128)S(1)} %copy-done.15, bf16[2,256,256]{2,1,0:T(8,128)(2,1)S(1)} %copy-done.10, bf16[2,256,256]{2,1,0:T(8,128)(2,1)S(1)} %copy-done.13, f32[2,8,128,128]{3,2,1,0:T(8,128)S(1)} %copy-done), custom_call_target="tpu_custom_call" | custom-call | tf_op jit(solution)/shard_map/pallas_call | solution.py:513
  213.3 32.1 %all_to_all.48.moved = f32[32,2,64,128]{3,2,1,0:T(8,128)S(1)} all-to-all(f32[32,2,64,128]{3,2,1,0:T(8,128)S(1)} %shard_map.99), channel_id=1, replica_groups=mesh['zl'=2,'y'=4,'zh'=4,'x'=4,'c'=2] {'y','x','c'}, dimensions={0} | all-to-all | bytes 4194304 | tf_op jit(solution)/shard_map/all_to_all | solution.py:524
  245.4 2.0 shard_map.100
  247.4 30.0 %all_to_all.49 = f32[4,2,16,2048]{3,2,1,0:T(8,128)S(1)} all-to-all(f32[4,2,16,2048]{3,2,1,0:T(8,128)S(1)} %shard_map.100), channel_id=1, replica_groups=mesh['zl'=2,'y'=4,'zh'=4,'x'=4,'c'=2] {'zh'}, dimensions={0} | all-to-all | bytes 2097152 | tf_op jit(solution)/shard_map/all_to_all | solution.py:524
  277.4 18.3 %all_to_all.50 = f32[4,2,16,2048]{3,2,1,0:T(8,128)S(1)} all-to-all(f32[4,2,16,2048]{3,2,1,0:T(8,128)S(1)} %all_to_all.49), channel_id=1, replica_groups=mesh['zl'=2,'y'=4,'zh'=4,'x'=4,'c'=2] {'y'}, dimensions={0} | all-to-all | bytes 2097152 | tf_op jit(solution)/shard_map/all_to_all | solution.py:524
  (82 shorter events, 31.0 us)
Async XLA Ops:
  26.4 12.7 %copy-start.27 = (f32[3,2]{0,1:T(2,128)S(1)}, f32[3,2]{0,1:T(2,128)}, u32[]{:S(2)}) copy-start(f32[3,2]{0,1:T(2,128)} %param.12) | copy-start | bytes 76
  26.4 41.2 %copy-start = (f32[2,8,128,128]{3,2,1,0:T(8,128)S(1)}, f32[2,8,128,128]{3,2,1,0:T(8,128)}, u32[]{:S(2)}) copy-start(f32[2,8,128,128]{3,2,1,0:T(8,128)} %constant.36.clone.turns) | copy-start | bytes 3145732
  26.4 41.2 %copy-start.8 = (bf16[2,256,256]{2,1,0:T(8,128)(2,1)S(1)}, bf16[2,256,256]{2,1,0:T(8,128)(2,1)}, u32[]{:S(2)}) copy-start(bf16[2,256,256]{2,1,0:T(8,128)(2,1)} %constant.34.clone.there_matrices) | copy-start | bytes 786436
  26.4 41.2 %copy-start.11 = (bf16[2,256,256]{2,1,0:T(8,128)(2,1)S(1)}, bf16[2,256,256]{2,1,0:T(8,128)(2,1)}, u32[]{:S(2)}) copy-start(bf16[2,256,256]{2,1,0:T(8,128)(2,1)} %constant.35.clone.back_matrices) | copy-start | bytes 786436
  27.5 40.2 %all-to-all-start.1 = ((f32[32,64,128]{2,1,0:T(8,128)}), f32[32,64,128]{2,1,0:T(8,128)S(1)}, u32[]{:S(2)}, u32[]{:S(2)}) async-start(f32[32,64,128]{2,1,0:T(8,128)} %bitcast.14), calls=%async_computation.1 | async-start | bytes 2097152 | tf_op jit(solution)/shard_map/all_to_all | solution.py:524
  67.7 1.6 copy-start.19
  76.2 33.4 %all-to-all-start.2 = ((f32[32,2,64,128]{3,2,1,0:T(8,128)}), f32[32,2,64,128]{3,2,1,0:T(8,128)S(1)}, u32[]{:S(2)}, u32[]{:S(2)}) async-start(f32[32,2,64,128]{3,2,1,0:T(8,128)} %shard_map.93), calls=%async_computation.2 | async-start | bytes 4194304 | tf_op jit(solution)/shard_map/all_to_all | solution.py:524
  81.8 27.9 %copy-start.4 = (bf16[2,256,256]{2,1,0:T(8,128)(2,1)S(1)}, bf16[2,256,256]{2,1,0:T(8,128)(2,1)}, u32[]{:S(2)}) copy-start(bf16[2,256,256]{2,1,0:T(8,128)(2,1)} %constant.33.clone.matrices) | copy-start | bytes 786436
  81.8 4.6 %collective-permute-start = (f32[4,32,128]{2,1,0:T(8,128)}, f32[4,32,128]{2,1,0:T(8,128)S(1)}, u32[]{:S(2)}, u32[]{:S(2)}) collective-permute-start(f32[4,32,128]{2,1,0:T(8,128)} %slice.17.refs_0_), channel_id=1, source_target_pairs={{0,152},{128,0},{8,128},{136,8},{16,136},{144,16},{24,144},{152,24... | collective-permute-start | bytes 196616 | tf_op jit(solution)/shard_map/ppermute | solution.py:535
  82.0 5.7 %collective-permute-start.4 = (f32[4,32,128]{2,1,0:T(8,128)}, f32[4,32,128]{2,1,0:T(8,128)S(1)}, u32[]{:S(2)}, u32[]{:S(2)}) collective-permute-start(f32[4,32,128]{2,1,0:T(8,128)} %slice.17.refs_0_), channel_id=1, source_target_pairs={{152,0},{0,128},{128,8},{8,136},{136,16},{16,144},{144,24},{24,152... | collective-permute-start | bytes 196616 | tf_op jit(solution)/shard_map/ppermute | solution.py:538
  86.3 4.3 %collective-permute-start.1 = (f32[4,32,128]{2,1,0:T(8,128)S(1)}, f32[4,32,128]{2,1,0:T(8,128)S(1)}, u32[]{:S(2)}, u32[]{:S(2)}) collective-permute-start(f32[4,32,128]{2,1,0:T(8,128)S(1)} %collective-permute-done.refs_1_), channel_id=1, source_target_pairs={{0,152},{128,0},{8,128},{136,8},{16,136},{144,16},{24,144},{152,24... | collective-permute-start | bytes 196616 | tf_op jit(solution)/shard_map/ppermute | solution.py:535
  87.7 5.5 %collective-permute-start.5 = (f32[4,32,128]{2,1,0:T(8,128)S(1)}, f32[4,32,128]{2,1,0:T(8,128)S(1)}, u32[]{:S(2)}, u32[]{:S(2)}) collective-permute-start(f32[4,32,128]{2,1,0:T(8,128)S(1)} %collective-permute-done.4.refs_7_), channel_id=1, source_target_pairs={{152,0},{0,128},{128,8},{8,136},{136,16},{16,144},{144,24},{24,152... | collective-permute-start | bytes 196616 | tf_op jit(solution)/shard_map/ppermute | solution.py:538
  90.6 4.5 %collective-permute-start.2 = (f32[4,32,128]{2,1,0:T(8,128)S(1)}, f32[4,32,128]{2,1,0:T(8,128)S(1)}, u32[]{:S(2)}, u32[]{:S(2)}) collective-permute-start(f32[4,32,128]{2,1,0:T(8,128)S(1)} %collective-permute-done.1.refs_2_), channel_id=1, source_target_pairs={{0,152},{128,0},{8,128},{136,8},{16,136},{144,16},{24,144},{152,24... | collective-permute-start | bytes 196616 | tf_op jit(solution)/shard_map/ppermute | solution.py:535
  93.2 5.5 %collective-permute-start.6 = (f32[4,32,128]{2,1,0:T(8,128)S(1)}, f32[4,32,128]{2,1,0:T(8,128)S(1)}, u32[]{:S(2)}, u32[]{:S(2)}) collective-permute-start(f32[4,32,128]{2,1,0:T(8,128)S(1)} %collective-permute-done.5.refs_6_), channel_id=1, source_target_pairs={{152,0},{0,128},{128,8},{8,136},{136,16},{16,144},{144,24},{24,152... | collective-permute-start | bytes 196616 | tf_op jit(solution)/shard_map/ppermute | solution.py:538
  95.1 5.5 %collective-permute-start.3 = (f32[4,32,128]{2,1,0:T(8,128)S(1)}, f32[4,32,128]{2,1,0:T(8,128)S(1)}, u32[]{:S(2)}, u32[]{:S(2)}) collective-permute-start(f32[4,32,128]{2,1,0:T(8,128)S(1)} %collective-permute-done.2.refs_3_), channel_id=1, source_target_pairs={{0,152},{128,0},{8,128},{136,8},{16,136},{144,16},{24,144},{152,24... | collective-permute-start | bytes 196616 | tf_op jit(solution)/shard_map/ppermute | solution.py:535
  109.7 1.6 copy-start.2
  112.2 24.4 %copy-start.17 = (f32[2,256,1024]{2,1,0:T(8,128)S(1)}, f32[2,256,1024]{2,1,0:T(8,128)}, u32[]{:S(2)}) copy-start(f32[2,256,1024]{2,1,0:T(8,128)} %copy-done.16) | copy-start | bytes 6291460
  115.2 21.4 %copy-start.9 = (bf16[2,256,256]{2,1,0:T(8,128)(2,1)S(1)}, bf16[2,256,256]{2,1,0:T(8,128)(2,1)}, u32[]{:S(2)}) copy-start(bf16[2,256,256]{2,1,0:T(8,128)(2,1)} %constant.34.clone.there_matrices) | copy-start | bytes 786436
  115.3 21.4 %copy-start.12 = (bf16[2,256,256]{2,1,0:T(8,128)(2,1)S(1)}, bf16[2,256,256]{2,1,0:T(8,128)(2,1)}, u32[]{:S(2)}) copy-start(bf16[2,256,256]{2,1,0:T(8,128)(2,1)} %constant.35.clone.back_matrices) | copy-start | bytes 786436
  143.7 34.8 %all-to-all-start.4 = ((f32[32,2,64,128]{3,2,1,0:T(8,128)}), f32[32,2,64,128]{3,2,1,0:T(8,128)S(1)}, u32[]{:S(2)}, u32[]{:S(2)}) async-start(f32[32,2,64,128]{3,2,1,0:T(8,128)} %shard_map.96), calls=%async_computation.4 | async-start | bytes 4194304 | tf_op jit(solution)/shard_map/all_to_all | solution.py:524
  148.8 5.6 %collective-permute-start.7 = (f32[4,64,128]{2,1,0:T(8,128)S(1)}, f32[4,64,128]{2,1,0:T(8,128)S(1)}, u32[]{:S(2)}, u32[]{:S(2)}) collective-permute-start(f32[4,64,128]{2,1,0:T(8,128)S(1)} %slice.18.refs_0_), channel_id=1, source_target_pairs={{0,152},{128,0},{8,128},{136,8},{16,136},{144,16},{24,144},{152,24... | collective-permute-start | bytes 393224 | tf_op jit(solution)/shard_map/ppermute | solution.py:535
  150.1 6.8 %collective-permute-start.11 = (f32[4,64,128]{2,1,0:T(8,128)S(1)}, f32[4,64,128]{2,1,0:T(8,128)S(1)}, u32[]{:S(2)}, u32[]{:S(2)}) collective-permute-start(f32[4,64,128]{2,1,0:T(8,128)S(1)} %slice.18.refs_0_), channel_id=1, source_target_pairs={{152,0},{0,128},{128,8},{8,136},{136,16},{16,144},{144,24},{24,152... | collective-permute-start | bytes 393224 | tf_op jit(solution)/shard_map/ppermute | solution.py:538
  154.4 5.0 %collective-permute-start.8 = (f32[4,64,128]{2,1,0:T(8,128)S(1)}, f32[4,64,128]{2,1,0:T(8,128)S(1)}, u32[]{:S(2)}, u32[]{:S(2)}) collective-permute-start(f32[4,64,128]{2,1,0:T(8,128)S(1)} %collective-permute-done.7.refs_1_), channel_id=1, source_target_pairs={{0,152},{128,0},{8,128},{136,8},{16,136},{144,16},{24,144},{152,24... | collective-permute-start | bytes 393224 | tf_op jit(solution)/shard_map/ppermute | solution.py:535
  156.8 6.2 %collective-permute-start.12 = (f32[4,64,128]{2,1,0:T(8,128)S(1)}, f32[4,64,128]{2,1,0:T(8,128)S(1)}, u32[]{:S(2)}, u32[]{:S(2)}) collective-permute-start(f32[4,64,128]{2,1,0:T(8,128)S(1)} %collective-permute-done.11.refs_7_), channel_id=1, source_target_pairs={{152,0},{0,128},{128,8},{8,136},{136,16},{16,144},{144,24},{24,152... | collective-permute-start | bytes 393224 | tf_op jit(solution)/shard_map/ppermute | solution.py:538
  159.4 6.1 %collective-permute-start.9 = (f32[4,64,128]{2,1,0:T(8,128)S(1)}, f32[4,64,128]{2,1,0:T(8,128)S(1)}, u32[]{:S(2)}, u32[]{:S(2)}) collective-permute-start(f32[4,64,128]{2,1,0:T(8,128)S(1)} %collective-permute-done.8.refs_2_), channel_id=1, source_target_pairs={{0,152},{128,0},{8,128},{136,8},{16,136},{144,16},{24,144},{152,24... | collective-permute-start | bytes 393224 | tf_op jit(solution)/shard_map/ppermute | solution.py:535
  163.0 6.2 %collective-permute-start.13 = (f32[4,64,128]{2,1,0:T(8,128)S(1)}, f32[4,64,128]{2,1,0:T(8,128)S(1)}, u32[]{:S(2)}, u32[]{:S(2)}) collective-permute-start(f32[4,64,128]{2,1,0:T(8,128)S(1)} %collective-permute-done.12.refs_6_), channel_id=1, source_target_pairs={{152,0},{0,128},{128,8},{8,136},{136,16},{16,144},{144,24},{24,152... | collective-permute-start | bytes 393224 | tf_op jit(solution)/shard_map/ppermute | solution.py:538
  165.5 6.2 %collective-permute-start.10 = (f32[4,64,128]{2,1,0:T(8,128)S(1)}, f32[4,64,128]{2,1,0:T(8,128)S(1)}, u32[]{:S(2)}, u32[]{:S(2)}) collective-permute-start(f32[4,64,128]{2,1,0:T(8,128)S(1)} %collective-permute-done.9.refs_3_), channel_id=1, source_target_pairs={{0,152},{128,0},{8,128},{136,8},{16,136},{144,16},{24,144},{152,24... | collective-permute-start | bytes 393224 | tf_op jit(solution)/shard_map/ppermute | solution.py:535
  181.0 26.6 %copy-start.15 = (f32[2,256,1024]{2,1,0:T(8,128)S(1)}, f32[2,256,1024]{2,1,0:T(8,128)}, u32[]{:S(2)}) copy-start(f32[2,256,1024]{2,1,0:T(8,128)} %copy-done.14) | copy-start | bytes 6291460
  184.1 23.6 %copy-start.10 = (bf16[2,256,256]{2,1,0:T(8,128)(2,1)S(1)}, bf16[2,256,256]{2,1,0:T(8,128)(2,1)}, u32[]{:S(2)}) copy-start(bf16[2,256,256]{2,1,0:T(8,128)(2,1)} %constant.34.clone.there_matrices) | copy-start | bytes 786436
  184.1 23.6 %copy-start.13 = (bf16[2,256,256]{2,1,0:T(8,128)(2,1)S(1)}, bf16[2,256,256]{2,1,0:T(8,128)(2,1)}, u32[]{:S(2)}) copy-start(bf16[2,256,256]{2,1,0:T(8,128)(2,1)} %constant.35.clone.back_matrices) | copy-start | bytes 786436
  213.3 32.1 %copy-start.7 = (bf16[2,256,256]{2,1,0:T(8,128)(2,1)S(1)}, bf16[2,256,256]{2,1,0:T(8,128)(2,1)}, u32[]{:S(2)}) copy-start(bf16[2,256,256]{2,1,0:T(8,128)(2,1)} %constant.37.clone.back_matrices) | copy-start | bytes 786436
  213.3 32.1 %copy-start.21 = (f32[4,16,64,128]{3,2,1,0:T(8,128)S(1)}, f32[4,16,64,128]{3,2,1,0:T(8,128)}, u32[]{:S(2)}) copy-start(f32[4,16,64,128]{3,2,1,0:T(8,128)} %copy-done.20) | copy-start | bytes 6291460
  (13 other events, 15.6 us)

commit v6 on v5

--- a/solution.py
+++ b/solution.py
@@ -190,7 +190,9 @@
 
 def mix(a, b):
     (a_high, a_low), (b_high, b_low) = a, b
-    return product(a_high, b_high) + (product(a_high, b_low) + product(a_low, b_high))
+    left = jnp.concatenate([a_high, a_high, a_low], axis=1)
+    right = jnp.concatenate([b_high, b_low, b_high], axis=0)
+    return product(left, right)
 
 
 def folded(number):
@@ -455,7 +457,7 @@
         return carry
 
     for top in range(2):
-        lax.fori_loop(0, half // sub, functools.partial(there, top), 0)
+        lax.fori_loop(0, half // sub, functools.partial(there, top), 0, unroll=half // sub)
     matrix = (there_matrices[0], there_matrices[1])
     for n in range(4):
         columns = slice(n * 2 * inner, (n + 1) * 2 * inner)
@@ -504,7 +506,7 @@
                         out[chunk, branch, pl.ds(pl.multiple_of(row, sub), sub), :] = result
             return carry
 
-        lax.fori_loop(0, half // sub, back, 0)
+        lax.fori_loop(0, half // sub, back, 0, unroll=half // sub)
 
 
 def call(kernel, shapes, scratch, scalars, operands):
@@ -524,19 +526,16 @@
     return lax.all_to_all(values, axes, split_axis=0, concat_axis=0, tiled=True)
 
 
-def around_z(tile):
+def around_z(tiles, first, last):
     axes = ("zl", "zh")
     index = [n % 2 * 4 + n // 2 for n in range(ring)]
     down = [(index[n], index[n - 1]) for n in range(ring)]
     up = [(index[n - 1], index[n]) for n in range(ring)]
-    tiles = [tile] + [None] * (ring - 1)
-    above = below = tile
-    for n in range(1, 5):
-        above = lax.ppermute(above, axes, down)
-        tiles[n] = above
-        if n < 4:
-            below = lax.ppermute(below, axes, up)
-            tiles[ring - n] = below
+    tiles = dict(tiles)
+    for n in range(first, last):
+        tiles[n] = lax.ppermute(tiles[n - 1], axes, down)
+        if n < ring // 2:
+            tiles[ring - n] = lax.ppermute(tiles[(ring + 1 - n) % ring], axes, up)
     return tiles
 
 
@@ -573,23 +572,25 @@
     tables = call(propagator_kernel, [(2, *folded_shape)] * depth, [], common, ())
     weights = []
     for level in range(depth):
-        if level:
-            arrived = exchange(sent, plane)
         if level == 0:
             arrived, first_tile, later_tile = lax.optimization_barrier(
                 (arrived, first_tile, later_tile)
             )
-            tiles = around_z(first_tile)
-        if level == 1:
-            arrived, later_tile = lax.optimization_barrier((arrived, later_tile))
-            tiles = around_z(later_tile)
+            tiles = around_z({0: first_tile}, 1, 5)
+        elif level == 1:
+            sent, later_tile = lax.optimization_barrier((sent, later_tile))
+            tiles = around_z({0: later_tile}, 1, 3)
+            arrived, tiles = lax.optimization_barrier((exchange(sent, plane), tiles))
+            tiles = around_z(tiles, 3, 5)
+        else:
+            arrived = exchange(sent, plane)
         if level < 2:
             weights += call(
                 functools.partial(weigh_kernel, level),
                 [(4, outer, rows, inner)] * (depth - 1 if level else 1),
                 [],
                 common,
-                tiles,
+                [tiles[n] for n in range(ring)],
             )
         (shifted,) = call(
             functools.partial(shift_kernel, plane_rows if level else slab_rows),

time: 299 us -> 291 us (0.973)
  blocking collectives: 147 us -> 124 us
  waiting for transfers between devices: 40.2 us -> 53 us
  local copies, waits for them, and re-layouts: 21.8 us -> 29 us
  Pallas kernels: 42.5 us -> 35.6 us
  starting transfers between devices: 44.3 us -> 47.4 us
    all_to_all x6 -> x5, blocking collectives: 147 us -> 124 us  [exchange(): return lax.all_to_all(values, axes, split_axis=0, concat_axis=0, tiled=True)]
    all_to_all x3 -> x4, waiting for transfers between devices: 20.6 us -> 28.8 us  [exchange(): return lax.all_to_all(values, axes, split_axis=0, concat_axis=0, tiled=True)]
    unnamed x57 -> x71, local copies, waits for them, and re-layouts: 18.9 us -> 26.2 us
    pallas_call x10, Pallas kernels: 42.5 us -> 35.6 us  [call(): pl.pallas_call(kernel, out_shape=[jax.ShapeDtypeStruct(s, jnp.float32) fo...]
    all_to_all x3 -> x4, starting transfers between devices: 22.3 us -> 28.8 us  [exchange(): return lax.all_to_all(values, axes, split_axis=0, concat_axis=0, tiled=True)]
    ppermute x14, waiting for transfers between devices: 19.6 us -> 24.2 us  [the longest x8 20.7 us: around_z(): tiles[n] = lax.ppermute(tiles[n - 1], axes, down)]
    ppermute x14, starting transfers between devices: 22 us -> 18.6 us  [the longest x8 13.9 us: around_z(): tiles[n] = lax.ppermute(tiles[n - 1], axes, down)]
  transfers between devices with their start and end apart: 17 -> 18, of which waited for: 10 -> 13; matrix products, arithmetic and copies ran while one was open for 0% -> 0% of each run, Pallas kernels for 5% -> 5%
where the time goes in v6:
time: 291 us; the launch traced here: 290 us
  blocking collectives  124 us (43%)
  waiting for transfers between devices  53 us (18%)
  starting transfers between devices  47.4 us (16%)
  Pallas kernels  35.6 us (12%)
  local copies, waits for them, and re-layouts  29 us (10%)
    all_to_all x5, blocking collectives, exchange(): return lax.all_to_all(values, axes, split_axis=0, concat_axis=0, tiled=True)  124 us
    pallas_call x10, Pallas kernels, call(): pl.pallas_call(kernel, out_shape=[jax.ShapeDtypeStruct(s, jnp.float32) fo...  35.6 us
    all_to_all x4, starting transfers between devices, exchange(): return lax.all_to_all(values, axes, split_axis=0, concat_axis=0, tiled=True)  28.8 us
    all_to_all x4, waiting for transfers between devices, exchange(): return lax.all_to_all(values, axes, split_axis=0, concat_axis=0, tiled=True)  28.8 us
    unnamed x71, local copies, waits for them, and re-layouts  26.2 us
    ppermute x8, waiting for transfers between devices, around_z(): tiles[n] = lax.ppermute(tiles[n - 1], axes, down)  20.7 us
    ppermute x8, starting transfers between devices, around_z(): tiles[n] = lax.ppermute(tiles[n - 1], axes, down)  13.9 us
  transfers between devices with their start and end apart: 18, of which 13 were waited for; matrix products, arithmetic and copies ran while one was open for 0% of the time, Pallas kernels for 5%

profile of v6, /device:TPU:2, one launch (start us, length us, event | category | flops | bytes accessed | tf_op | source)
XLA Modules:
  0.0 289.9 jit_solution(17314735346485041143)
XLA Ops:
  4.8 21.6 %all_to_all.45 = f32[4,616,128]{2,1,0:T(8,128)S(1)} all-to-all(f32[4,616,128]{2,1,0:T(8,128)S(1)} %shard_map.91), channel_id=1, replica_groups=mesh['zl'=2,'y'=4,'zh'=4,'x'=4,'c'=2] {'y'}, dimensions={0} | all-to-all | bytes 2523136 | tf_op jit(solution)/shard_map/all_to_all | solution.py:526
  27.5 11.6 %all-to-all-start.1 = ((f32[32,64,128]{2,1,0:T(8,128)}), f32[32,64,128]{2,1,0:T(8,128)S(1)}, u32[]{:S(2)}, u32[]{:S(2)}) async-start(f32[32,64,128]{2,1,0:T(8,128)} %bitcast.14), calls=%async_computation.1 | async-start | bytes 2097152 | tf_op jit(solution)/shard_map/all_to_all | solution.py:526
  40.0 7.5 %shard_map.92 = (f32[2,256,1024]{2,1,0:T(8,128)S(1)}, f32[2,256,1024]{2,1,0:T(8,128)S(1)}, f32[2,256,1024]{2,1,0:T(8,128)S(1)}) custom-call(s32[3]{0:T(128)S(1)} %pad_add_fusion.place, f32[4]{0:T(128)S(1)} %slice_reduce_fusion.freqs, f32[3,2]{1,0:T(4,128)S(1)} %copy.13.ref_slow), custom_call_target="tpu_custom_call" | custom-call | tf_op jit(solution)/shard_map/pallas_call | solution.py:515
  51.6 16.0 %all-to-all-done.1 = f32[32,64,128]{2,1,0:T(8,128)S(1)} async-done(((f32[32,64,128]{2,1,0:T(8,128)}), f32[32,64,128]{2,1,0:T(8,128)S(1)}, u32[]{:S(2)}, u32[]{:S(2)}) %all-to-all-start.1) | async-done | bytes 1048608 | tf_op jit(solution)/shard_map/all_to_all | solution.py:526
  69.2 4.6 %shard_map.93 = f32[32,2,64,128]{3,2,1,0:T(8,128)} custom-call(f32[2048,128]{1,0:T(8,128)S(1)} %bitcast.11, f32[2,256,1024]{2,1,0:T(8,128)S(1)} %copy-done.20, bf16[2,256,256]{2,1,0:T(8,128)(2,1)S(1)} %copy-done.9, bf16[2,256,256]{2,1,0:T(8,128)(2,1)S(1)} %copy-done.12, f32[2,8,128,128]{3,2,1,0:T(8,128)S(1)} %copy-done), custom_call_target="tpu_custom_call" | custom-call | tf_op jit(solution)/shard_map/pallas_call | solution.py:515
  73.8 5.3 %all-to-all-start.2 = ((f32[32,2,64,128]{3,2,1,0:T(8,128)}), f32[32,2,64,128]{3,2,1,0:T(8,128)S(1)}, u32[]{:S(2)}, u32[]{:S(2)}) async-start(f32[32,2,64,128]{3,2,1,0:T(8,128)} %shard_map.93), calls=%async_computation.2 | async-start | bytes 4194304 | tf_op jit(solution)/shard_map/all_to_all | solution.py:526
  81.2 2.4 collective-permute-done.refs_1_
  85.7 2.2 collective-permute-done.1.refs_2_
  87.9 3.0 %collective-permute-start.2 = (f32[4,32,128]{2,1,0:T(8,128)S(1)}, f32[4,32,128]{2,1,0:T(8,128)S(1)}, u32[]{:S(2)}, u32[]{:S(2)}) collective-permute-start(f32[4,32,128]{2,1,0:T(8,128)S(1)} %collective-permute-done.1.refs_2_), channel_id=1, source_target_pairs={{0,152},{128,0},{8,128},{136,8},{16,136},{144,16},{24,144},{152,24... | collective-permute-start | bytes 196616 | tf_op jit(solution)/shard_map/ppermute | solution.py:536
  92.8 3.6 %collective-permute-start.3 = (f32[4,32,128]{2,1,0:T(8,128)S(1)}, f32[4,32,128]{2,1,0:T(8,128)S(1)}, u32[]{:S(2)}, u32[]{:S(2)}) collective-permute-start(f32[4,32,128]{2,1,0:T(8,128)S(1)} %collective-permute-done.2.refs_3_), channel_id=1, source_target_pairs={{0,152},{128,0},{8,128},{136,8},{16,136},{144,16},{24,144},{152,24... | collective-permute-start | bytes 196616 | tf_op jit(solution)/shard_map/ppermute | solution.py:536
  96.4 1.9 collective-permute-done.3.refs_4_
  99.2 2.3 shard_map.94.weights
  102.9 4.1 %all-to-all-done.2.moved = f32[32,2,64,128]{3,2,1,0:T(8,128)S(1)} async-done(((f32[32,2,64,128]{3,2,1,0:T(8,128)}), f32[32,2,64,128]{3,2,1,0:T(8,128)S(1)}, u32[]{:S(2)}, u32[]{:S(2)}) %all-to-all-start.2) | async-done | bytes 2097184 | tf_op jit(solution)/shard_map/all_to_all | solution.py:526
  109.5 3.1 %shard_map.95 = f32[32,64,128]{2,1,0:T(8,128)S(1)} custom-call(f32[32,2,64,128]{3,2,1,0:T(8,128)S(1)} %all-to-all-done.2.moved, f32[4,16,64,128]{3,2,1,0:T(8,128)S(1)} %copy-done.2, bf16[2,256,256]{2,1,0:T(8,128)(2,1)S(1)} %copy-done.6, bf16[2,256,256]{2,1,0:T(8,128)(2,1)S(1)} %copy-done.4), custom_call_target="tpu_custom_call" | custom-call | tf_op jit(solution)/shard_map/pallas_call | solution.py:515
  113.5 6.1 %all-to-all-start.3 = ((f32[32,64,128]{2,1,0:T(8,128)}), f32[32,64,128]{2,1,0:T(8,128)S(1)}, u32[]{:S(2)}, u32[]{:S(2)}) async-start(f32[32,64,128]{2,1,0:T(8,128)} %copy-done.5), calls=%async_computation.3 | async-start | bytes 2097152 | tf_op jit(solution)/shard_map/all_to_all | solution.py:526
  121.7 3.5 %collective-permute-done.7.refs_1_ = f32[4,64,128]{2,1,0:T(8,128)S(1)} collective-permute-done((f32[4,64,128]{2,1,0:T(8,128)S(1)}, f32[4,64,128]{2,1,0:T(8,128)S(1)}, u32[]{:S(2)}, u32[]{:S(2)}) %collective-permute-start.7) | collective-permute-done | bytes 131104 | tf_op jit(solution)/shard_map/ppermute | solution.py:536
  125.2 2.2 collective-permute-start.8
  130.9 3.5 %collective-permute-done.10.refs_6_ = f32[4,64,128]{2,1,0:T(8,128)} collective-permute-done((f32[4,64,128]{2,1,0:T(8,128)S(1)}, f32[4,64,128]{2,1,0:T(8,128)}, u32[]{:S(2)}, u32[]{:S(2)}) %collective-permute-start.10) | collective-permute-done | bytes 131104 | tf_op jit(solution)/shard_map/ppermute | solution.py:538
  137.4 4.6 %shard_map.96 = f32[32,2,64,128]{3,2,1,0:T(8,128)} custom-call(f32[2048,128]{1,0:T(8,128)S(1)} %bitcast.12, f32[2,256,1024]{2,1,0:T(8,128)S(1)} %copy-done.18, bf16[2,256,256]{2,1,0:T(8,128)(2,1)S(1)} %copy-done.10, bf16[2,256,256]{2,1,0:T(8,128)(2,1)S(1)} %copy-done.13, f32[2,8,128,128]{3,2,1,0:T(8,128)S(1)} %copy-done), custom_call_target="tpu_custom_call" | custom-call | tf_op jit(solution)/shard_map/pallas_call | solution.py:515
  142.0 5.9 %all-to-all-start.4 = ((f32[32,2,64,128]{3,2,1,0:T(8,128)}), f32[32,2,64,128]{3,2,1,0:T(8,128)S(1)}, u32[]{:S(2)}, u32[]{:S(2)}) async-start(f32[32,2,64,128]{3,2,1,0:T(8,128)} %shard_map.96), calls=%async_computation.4 | async-start | bytes 4194304 | tf_op jit(solution)/shard_map/all_to_all | solution.py:526
  148.1 1.9 collective-permute-start.13
  150.0 3.7 %collective-permute-done.11.refs_3_ = f32[4,64,128]{2,1,0:T(8,128)S(1)} collective-permute-done((f32[4,64,128]{2,1,0:T(8,128)}, f32[4,64,128]{2,1,0:T(8,128)S(1)}, u32[]{:S(2)}, u32[]{:S(2)}) %collective-permute-start.11) | collective-permute-done | bytes 131104 | tf_op jit(solution)/shard_map/ppermute | solution.py:536
  155.2 3.5 %collective-permute-done.12.refs_4_ = f32[4,64,128]{2,1,0:T(8,128)S(1)} collective-permute-done((f32[4,64,128]{2,1,0:T(8,128)S(1)}, f32[4,64,128]{2,1,0:T(8,128)S(1)}, u32[]{:S(2)}, u32[]{:S(2)}) %collective-permute-start.12) | collective-permute-done | bytes 131104 | tf_op jit(solution)/shard_map/ppermute | solution.py:536
  161.4 4.4 %shard_map.97 = (f32[4,16,64,128]{3,2,1,0:T(8,128)S(1)}, f32[4,16,64,128]{3,2,1,0:T(8,128)S(1)}) custom-call(s32[3]{0:T(128)S(1)} %pad_add_fusion.place, f32[4]{0:T(128)S(1)} %slice_reduce_fusion.freqs, f32[3,2]{1,0:T(4,128)S(1)} %copy.13.ref_slow, f32[4,64,128]{2,1,0:T(8,128)S(1)} %slice.18.refs_0_, f32[4,64,128]{2,1,0:T(8,128)S(1)} %copy-done.29, ...), custom_call_target="tpu_custom_call" | custom-call | tf_op jit(solution)/shard_map/pallas_call | solution.py:515
  168.5 7.2 %all-to-all-done.4.moved = f32[32,2,64,128]{3,2,1,0:T(8,128)S(1)} async-done(((f32[32,2,64,128]{3,2,1,0:T(8,128)}), f32[32,2,64,128]{3,2,1,0:T(8,128)S(1)}, u32[]{:S(2)}, u32[]{:S(2)}) %all-to-all-start.4) | async-done | bytes 2097184 | tf_op jit(solution)/shard_map/all_to_all | solution.py:526
  178.3 3.1 %shard_map.98 = f32[32,64,128]{2,1,0:T(8,128)S(1)} custom-call(f32[32,2,64,128]{3,2,1,0:T(8,128)S(1)} %all-to-all-done.4.moved, f32[4,16,64,128]{3,2,1,0:T(8,128)S(1)} %copy-done.24, bf16[2,256,256]{2,1,0:T(8,128)(2,1)S(1)} %copy-done.7, bf16[2,256,256]{2,1,0:T(8,128)(2,1)S(1)} %copy-done.4), custom_call_target="tpu_custom_call" | custom-call | tf_op jit(solution)/shard_map/pallas_call | solution.py:515
  181.4 21.4 %all_to_all.46 = f32[32,64,128]{2,1,0:T(8,128)S(1)} all-to-all(f32[32,64,128]{2,1,0:T(8,128)S(1)} %shard_map.98), channel_id=1, replica_groups=mesh['zl'=2,'y'=4,'zh'=4,'x'=4,'c'=2] {'y','x','c'}, dimensions={0} | all-to-all | bytes 2097152 | tf_op jit(solution)/shard_map/all_to_all | solution.py:526
  202.8 3.2 %shard_map.99 = f32[32,2,64,128]{3,2,1,0:T(8,128)S(1)} custom-call(f32[2048,128]{1,0:T(8,128)S(1)} %bitcast.13, f32[2,256,1024]{2,1,0:T(8,128)S(1)} %copy-done.16, bf16[2,256,256]{2,1,0:T(8,128)(2,1)S(1)} %copy-done.11, bf16[2,256,256]{2,1,0:T(8,128)(2,1)S(1)} %copy-done.14, f32[2,8,128,128]{3,2,1,0:T(8,128)S(1)} %copy-done), custom_call_target="tpu_custom_call" | custom-call | tf_op jit(solution)/shard_map/pallas_call | solution.py:515
  206.0 32.0 %all_to_all.47.moved = f32[32,2,64,128]{3,2,1,0:T(8,128)S(1)} all-to-all(f32[32,2,64,128]{3,2,1,0:T(8,128)S(1)} %shard_map.99), channel_id=1, replica_groups=mesh['zl'=2,'y'=4,'zh'=4,'x'=4,'c'=2] {'y','x','c'}, dimensions={0} | all-to-all | bytes 4194304 | tf_op jit(solution)/shard_map/all_to_all | solution.py:526
  238.0 2.0 shard_map.100
  240.0 31.1 %all_to_all.48 = f32[4,2,16,2048]{3,2,1,0:T(8,128)S(1)} all-to-all(f32[4,2,16,2048]{3,2,1,0:T(8,128)S(1)} %shard_map.100), channel_id=1, replica_groups=mesh['zl'=2,'y'=4,'zh'=4,'x'=4,'c'=2] {'zh'}, dimensions={0} | all-to-all | bytes 2097152 | tf_op jit(solution)/shard_map/all_to_all | solution.py:526
  271.1 17.8 %all_to_all.49 = f32[4,2,16,2048]{3,2,1,0:T(8,128)S(1)} all-to-all(f32[4,2,16,2048]{3,2,1,0:T(8,128)S(1)} %all_to_all.48), channel_id=1, replica_groups=mesh['zl'=2,'y'=4,'zh'=4,'x'=4,'c'=2] {'y'}, dimensions={0} | all-to-all | bytes 2097152 | tf_op jit(solution)/shard_map/all_to_all | solution.py:526
  (97 shorter events, 42.9 us)
Async XLA Ops:
  26.4 12.7 %copy-start.34 = (f32[3,2]{0,1:T(2,128)S(1)}, f32[3,2]{0,1:T(2,128)}, u32[]{:S(2)}) copy-start(f32[3,2]{0,1:T(2,128)} %param.12) | copy-start | bytes 76
  26.4 41.2 %copy-start = (f32[2,8,128,128]{3,2,1,0:T(8,128)S(1)}, f32[2,8,128,128]{3,2,1,0:T(8,128)}, u32[]{:S(2)}) copy-start(f32[2,8,128,128]{3,2,1,0:T(8,128)} %constant.36.clone.turns) | copy-start | bytes 3145732
  26.4 41.2 %copy-start.9 = (bf16[2,256,256]{2,1,0:T(8,128)(2,1)S(1)}, bf16[2,256,256]{2,1,0:T(8,128)(2,1)}, u32[]{:S(2)}) copy-start(bf16[2,256,256]{2,1,0:T(8,128)(2,1)} %constant.34.clone.there_matrices) | copy-start | bytes 786436
  26.4 41.2 %copy-start.12 = (bf16[2,256,256]{2,1,0:T(8,128)(2,1)S(1)}, bf16[2,256,256]{2,1,0:T(8,128)(2,1)}, u32[]{:S(2)}) copy-start(bf16[2,256,256]{2,1,0:T(8,128)(2,1)} %constant.35.clone.back_matrices) | copy-start | bytes 786436
  27.5 40.2 %all-to-all-start.1 = ((f32[32,64,128]{2,1,0:T(8,128)}), f32[32,64,128]{2,1,0:T(8,128)S(1)}, u32[]{:S(2)}, u32[]{:S(2)}) async-start(f32[32,64,128]{2,1,0:T(8,128)} %bitcast.14), calls=%async_computation.1 | async-start | bytes 2097152 | tf_op jit(solution)/shard_map/all_to_all | solution.py:526
  67.6 1.6 copy-start.20
  73.8 33.1 %all-to-all-start.2 = ((f32[32,2,64,128]{3,2,1,0:T(8,128)}), f32[32,2,64,128]{3,2,1,0:T(8,128)S(1)}, u32[]{:S(2)}, u32[]{:S(2)}) async-start(f32[32,2,64,128]{3,2,1,0:T(8,128)} %shard_map.93), calls=%async_computation.2 | async-start | bytes 4194304 | tf_op jit(solution)/shard_map/all_to_all | solution.py:526
  79.1 27.9 %copy-start.4 = (bf16[2,256,256]{2,1,0:T(8,128)(2,1)S(1)}, bf16[2,256,256]{2,1,0:T(8,128)(2,1)}, u32[]{:S(2)}) copy-start(bf16[2,256,256]{2,1,0:T(8,128)(2,1)} %constant.33.clone.matrices) | copy-start | bytes 786436
  79.1 4.6 %collective-permute-start = (f32[4,32,128]{2,1,0:T(8,128)}, f32[4,32,128]{2,1,0:T(8,128)S(1)}, u32[]{:S(2)}, u32[]{:S(2)}) collective-permute-start(f32[4,32,128]{2,1,0:T(8,128)} %slice.17.refs_0_), channel_id=1, source_target_pairs={{0,152},{128,0},{8,128},{136,8},{16,136},{144,16},{24,144},{152,24... | collective-permute-start | bytes 196616 | tf_op jit(solution)/shard_map/ppermute | solution.py:536
  79.8 5.7 %collective-permute-start.4 = (f32[4,32,128]{2,1,0:T(8,128)}, f32[4,32,128]{2,1,0:T(8,128)S(1)}, u32[]{:S(2)}, u32[]{:S(2)}) collective-permute-start(f32[4,32,128]{2,1,0:T(8,128)} %slice.17.refs_0_), channel_id=1, source_target_pairs={{152,0},{0,128},{128,8},{8,136},{136,16},{16,144},{144,24},{24,152... | collective-permute-start | bytes 196616 | tf_op jit(solution)/shard_map/ppermute | solution.py:538
  83.6 4.3 %collective-permute-start.1 = (f32[4,32,128]{2,1,0:T(8,128)S(1)}, f32[4,32,128]{2,1,0:T(8,128)S(1)}, u32[]{:S(2)}, u32[]{:S(2)}) collective-permute-start(f32[4,32,128]{2,1,0:T(8,128)S(1)} %collective-permute-done.refs_1_), channel_id=1, source_target_pairs={{0,152},{128,0},{8,128},{136,8},{16,136},{144,16},{24,144},{152,24... | collective-permute-start | bytes 196616 | tf_op jit(solution)/shard_map/ppermute | solution.py:536
  85.5 5.5 %collective-permute-start.5 = (f32[4,32,128]{2,1,0:T(8,128)S(1)}, f32[4,32,128]{2,1,0:T(8,128)S(1)}, u32[]{:S(2)}, u32[]{:S(2)}) collective-permute-start(f32[4,32,128]{2,1,0:T(8,128)S(1)} %collective-permute-done.4.refs_7_), channel_id=1, source_target_pairs={{152,0},{0,128},{128,8},{8,136},{136,16},{16,144},{144,24},{24,152... | collective-permute-start | bytes 196616 | tf_op jit(solution)/shard_map/ppermute | solution.py:538
  87.9 4.9 %collective-permute-start.2 = (f32[4,32,128]{2,1,0:T(8,128)S(1)}, f32[4,32,128]{2,1,0:T(8,128)S(1)}, u32[]{:S(2)}, u32[]{:S(2)}) collective-permute-start(f32[4,32,128]{2,1,0:T(8,128)S(1)} %collective-permute-done.1.refs_2_), channel_id=1, source_target_pairs={{0,152},{128,0},{8,128},{136,8},{16,136},{144,16},{24,144},{152,24... | collective-permute-start | bytes 196616 | tf_op jit(solution)/shard_map/ppermute | solution.py:536
  90.9 5.5 %collective-permute-start.6 = (f32[4,32,128]{2,1,0:T(8,128)S(1)}, f32[4,32,128]{2,1,0:T(8,128)S(1)}, u32[]{:S(2)}, u32[]{:S(2)}) collective-permute-start(f32[4,32,128]{2,1,0:T(8,128)S(1)} %collective-permute-done.5.refs_6_), channel_id=1, source_target_pairs={{152,0},{0,128},{128,8},{8,136},{136,16},{16,144},{144,24},{24,152... | collective-permute-start | bytes 196616 | tf_op jit(solution)/shard_map/ppermute | solution.py:538
  92.8 5.5 %collective-permute-start.3 = (f32[4,32,128]{2,1,0:T(8,128)S(1)}, f32[4,32,128]{2,1,0:T(8,128)S(1)}, u32[]{:S(2)}, u32[]{:S(2)}) collective-permute-start(f32[4,32,128]{2,1,0:T(8,128)S(1)} %collective-permute-done.2.refs_3_), channel_id=1, source_target_pairs={{0,152},{128,0},{8,128},{136,8},{16,136},{144,16},{24,144},{152,24... | collective-permute-start | bytes 196616 | tf_op jit(solution)/shard_map/ppermute | solution.py:536
  113.5 22.3 %copy-start.10 = (bf16[2,256,256]{2,1,0:T(8,128)(2,1)S(1)}, bf16[2,256,256]{2,1,0:T(8,128)(2,1)}, u32[]{:S(2)}) copy-start(bf16[2,256,256]{2,1,0:T(8,128)(2,1)} %constant.34.clone.there_matrices) | copy-start | bytes 786436
  113.5 22.3 %copy-start.13 = (bf16[2,256,256]{2,1,0:T(8,128)(2,1)S(1)}, bf16[2,256,256]{2,1,0:T(8,128)(2,1)}, u32[]{:S(2)}) copy-start(bf16[2,256,256]{2,1,0:T(8,128)(2,1)} %constant.35.clone.back_matrices) | copy-start | bytes 786436
  113.5 22.3 %all-to-all-start.3 = ((f32[32,64,128]{2,1,0:T(8,128)}), f32[32,64,128]{2,1,0:T(8,128)S(1)}, u32[]{:S(2)}, u32[]{:S(2)}) async-start(f32[32,64,128]{2,1,0:T(8,128)} %copy-done.5), calls=%async_computation.3 | async-start | bytes 2097152 | tf_op jit(solution)/shard_map/all_to_all | solution.py:526
  119.6 5.6 %collective-permute-start.7 = (f32[4,64,128]{2,1,0:T(8,128)S(1)}, f32[4,64,128]{2,1,0:T(8,128)S(1)}, u32[]{:S(2)}, u32[]{:S(2)}) collective-permute-start(f32[4,64,128]{2,1,0:T(8,128)S(1)} %slice.18.refs_0_), channel_id=1, source_target_pairs={{0,152},{128,0},{8,128},{136,8},{16,136},{144,16},{24,144},{152,24... | collective-permute-start | bytes 393224 | tf_op jit(solution)/shard_map/ppermute | solution.py:536
  120.6 7.4 %collective-permute-start.9 = (f32[4,64,128]{2,1,0:T(8,128)S(1)}, f32[4,64,128]{2,1,0:T(8,128)S(1)}, u32[]{:S(2)}, u32[]{:S(2)}) collective-permute-start(f32[4,64,128]{2,1,0:T(8,128)S(1)} %slice.18.refs_0_), channel_id=1, source_target_pairs={{152,0},{0,128},{128,8},{8,136},{136,16},{16,144},{144,24},{24,152... | collective-permute-start | bytes 393224 | tf_op jit(solution)/shard_map/ppermute | solution.py:538
  125.2 5.0 %collective-permute-start.8 = (f32[4,64,128]{2,1,0:T(8,128)S(1)}, f32[4,64,128]{2,1,0:T(8,128)S(1)}, u32[]{:S(2)}, u32[]{:S(2)}) collective-permute-start(f32[4,64,128]{2,1,0:T(8,128)S(1)} %collective-permute-done.7.refs_1_), channel_id=1, source_target_pairs={{0,152},{128,0},{8,128},{136,8},{16,136},{144,16},{24,144},{152,24... | collective-permute-start | bytes 393224 | tf_op jit(solution)/shard_map/ppermute | solution.py:536
  128.1 6.3 %collective-permute-start.10 = (f32[4,64,128]{2,1,0:T(8,128)S(1)}, f32[4,64,128]{2,1,0:T(8,128)}, u32[]{:S(2)}, u32[]{:S(2)}) collective-permute-start(f32[4,64,128]{2,1,0:T(8,128)S(1)} %collective-permute-done.9.refs_7_), channel_id=1, source_target_pairs={{152,0},{0,128},{128,8},{8,136},{136,16},{16,144},{144,24},{24,152... | collective-permute-start | bytes 393224 | tf_op jit(solution)/shard_map/ppermute | solution.py:538
  135.8 1.6 copy-start.18
  142.0 33.8 %all-to-all-start.4 = ((f32[32,2,64,128]{3,2,1,0:T(8,128)}), f32[32,2,64,128]{3,2,1,0:T(8,128)S(1)}, u32[]{:S(2)}, u32[]{:S(2)}) async-start(f32[32,2,64,128]{3,2,1,0:T(8,128)} %shard_map.96), calls=%async_computation.4 | async-start | bytes 4194304 | tf_op jit(solution)/shard_map/all_to_all | solution.py:526
  147.9 5.8 %collective-permute-start.11 = (f32[4,64,128]{2,1,0:T(8,128)}, f32[4,64,128]{2,1,0:T(8,128)S(1)}, u32[]{:S(2)}, u32[]{:S(2)}) collective-permute-start(f32[4,64,128]{2,1,0:T(8,128)} %copy-done.32), channel_id=1, source_target_pairs={{0,152},{128,0},{8,128},{136,8},{16,136},{144,16},{24,144},{152,24... | collective-permute-start | bytes 393224 | tf_op jit(solution)/shard_map/ppermute | solution.py:536
  148.1 7.2 %collective-permute-start.13 = (f32[4,64,128]{2,1,0:T(8,128)}, f32[4,64,128]{2,1,0:T(8,128)S(1)}, u32[]{:S(2)}, u32[]{:S(2)}) collective-permute-start(f32[4,64,128]{2,1,0:T(8,128)} %collective-permute-done.10.refs_6_), channel_id=1, source_target_pairs={{152,0},{0,128},{128,8},{8,136},{136,16},{16,144},{144,24},{24,152... | collective-permute-start | bytes 393224 | tf_op jit(solution)/shard_map/ppermute | solution.py:538
  153.7 5.0 %collective-permute-start.12 = (f32[4,64,128]{2,1,0:T(8,128)S(1)}, f32[4,64,128]{2,1,0:T(8,128)S(1)}, u32[]{:S(2)}, u32[]{:S(2)}) collective-permute-start(f32[4,64,128]{2,1,0:T(8,128)S(1)} %collective-permute-done.11.refs_3_), channel_id=1, source_target_pairs={{0,152},{128,0},{8,128},{136,8},{16,136},{144,16},{24,144},{152,24... | collective-permute-start | bytes 393224 | tf_op jit(solution)/shard_map/ppermute | solution.py:536
  178.3 24.5 %copy-start.16 = (f32[2,256,1024]{2,1,0:T(8,128)S(1)}, f32[2,256,1024]{2,1,0:T(8,128)}, u32[]{:S(2)}) copy-start(f32[2,256,1024]{2,1,0:T(8,128)} %copy-done.15) | copy-start | bytes 6291460
  181.4 21.4 %copy-start.11 = (bf16[2,256,256]{2,1,0:T(8,128)(2,1)S(1)}, bf16[2,256,256]{2,1,0:T(8,128)(2,1)}, u32[]{:S(2)}) copy-start(bf16[2,256,256]{2,1,0:T(8,128)(2,1)} %constant.34.clone.there_matrices) | copy-start | bytes 786436
  181.4 21.4 %copy-start.14 = (bf16[2,256,256]{2,1,0:T(8,128)(2,1)S(1)}, bf16[2,256,256]{2,1,0:T(8,128)(2,1)}, u32[]{:S(2)}) copy-start(bf16[2,256,256]{2,1,0:T(8,128)(2,1)} %constant.35.clone.back_matrices) | copy-start | bytes 786436
  206.0 32.0 %copy-start.8 = (bf16[2,256,256]{2,1,0:T(8,128)(2,1)S(1)}, bf16[2,256,256]{2,1,0:T(8,128)(2,1)}, u32[]{:S(2)}) copy-start(bf16[2,256,256]{2,1,0:T(8,128)(2,1)} %constant.37.clone.back_matrices) | copy-start | bytes 786436
  206.0 32.0 %copy-start.22 = (f32[4,16,64,128]{3,2,1,0:T(8,128)S(1)}, f32[4,16,64,128]{3,2,1,0:T(8,128)}, u32[]{:S(2)}) copy-start(f32[4,16,64,128]{3,2,1,0:T(8,128)} %copy-done.21) | copy-start | bytes 6291460
  (21 other events, 22.9 us)

commit v7 on v6

--- a/solution.py
+++ b/solution.py
@@ -250,20 +250,12 @@
         out[y, freq_start:, :] = jnp.full((sub, inner), freqs[0], jnp.float32)
 
 
-def combine_kernel(
-    last,
-    moved,
-    weights,
-    back_matrices,
-    matrices,
-    out,
-    fields,
-    summed,
-    spectrum,
-    turns,
-):
-    fill_y_turns(turns)
-    turn_cos, turn_sin = turns[0], turns[1]
+def combine_kernel(last, moved, weights, back_matrices, matrices, out, fields, *scratch):
+    fields_kernel(moved, back_matrices, fields)
+    sum_kernel(last, fields, weights, matrices, out, *scratch)
+
+
+def fields_kernel(moved, back_matrices, fields):
     matrix = (back_matrices[0], back_matrices[1])
     for branch in range(2):
         for k in range(0, outer, 4):
@@ -276,6 +268,11 @@
             )
             result = mix(cut(block), matrix)
             fields[branch, k : k + 4] = result.reshape(4, rows, 2 * inner)
+
+
+def sum_kernel(last, fields, weights, matrices, out, summed, spectrum, turns):
+    fill_y_turns(turns)
+    turn_cos, turn_sin = turns[0], turns[1]
 
     def back(c, carry):
         here = block_rows(c)
@@ -415,18 +412,12 @@
     return chunk * rows + row
 
 
-def shift_kernel(
-    rows_of,
-    arrived,
-    table,
-    there_matrices,
-    back_matrices,
-    turns,
-    out,
-    spectrum,
-    shifted,
-    lane_turn,
-):
+def shift_kernel(rows_of, arrived, table, there_matrices, back_matrices, turns, out, spectrum, *scratch):
+    forward_x_kernel(rows_of, arrived, there_matrices, turns, spectrum, scratch[1])
+    back_x_kernel(spectrum, table, back_matrices, turns, out, *scratch)
+
+
+def forward_x_kernel(rows_of, arrived, there_matrices, turns, spectrum, lane_turn):
     fill_lane_turns(lane_turn)
     lane = lax.broadcasted_iota(jnp.int32, (sub, inner), 1)
     low_lanes = lane < half
@@ -462,6 +453,14 @@
     for n in range(4):
         columns = slice(n * 2 * inner, (n + 1) * 2 * inner)
         spectrum[:, columns] = mix(matrix, cut(spectrum[:, columns]))
+
+
+def back_x_kernel(spectrum, table, back_matrices, turns, out, shifted, lane_turn):
+    fill_lane_turns(lane_turn)
+    lane = lax.broadcasted_iota(jnp.int32, (sub, inner), 1)
+    low_lanes = lane < half
+    groups = outer // 2
+    steps = inner // sub
 
     def propagate(c, carry):
         here = block_rows(c)
@@ -592,22 +591,51 @@
                 common,
                 [tiles[n] for n in range(ring)],
             )
-        (shifted,) = call(
-            functools.partial(shift_kernel, plane_rows if level else slab_rows),
-            [(parts, 2, rows, inner)],
-            [folded_shape, (2, *folded_shape), (2, outer // 2, inner)],
-            (),
-            (arrived.reshape(length, inner), tables[level], fx_matrix, ix_matrix, turn_x),
-        )
-        moved = exchange(shifted, plane)
         last = level == depth - 1
-        (sent,) = call(
-            functools.partial(combine_kernel, last),
-            [(4, 2, quarter, length) if last else packed],
-            [(2, *spectrum_shape), (2, outer, rows, inner), spectrum_shape, y_turns_shape],
-            (),
-            (moved, weights[level], iy_matrix, fy_matrix),
-        )
+        read = plane_rows if level else slab_rows
+        arrived = arrived.reshape(length, inner)
+        x_scratch = [(2, *folded_shape), (2, outer // 2, inner)]
+        y_scratch = [(2, outer, rows, inner), spectrum_shape, y_turns_shape]
+        if last:
+            (shifted,) = call(
+                functools.partial(shift_kernel, read),
+                [(parts, 2, rows, inner)],
+                [folded_shape, *x_scratch],
+                (),
+                (arrived, tables[level], fx_matrix, ix_matrix, turn_x),
+            )
+            moved = exchange(shifted, plane)
+            (sent,) = call(
+                functools.partial(combine_kernel, last),
+                [(4, 2, quarter, length)],
+                [(2, *spectrum_shape), *y_scratch],
+                (),
+                (moved, weights[level], iy_matrix, fy_matrix),
+            )
+        else:
+            (spectrum,) = call(
+                functools.partial(forward_x_kernel, read),
+                [folded_shape],
+                x_scratch[1:],
+                (),
+                (arrived, fx_matrix, turn_x),
+            )
+            (shifted,) = call(
+                back_x_kernel,
+                [(parts, 2, rows, inner)],
+                x_scratch,
+                (),
+                (spectrum, tables[level], ix_matrix, turn_x),
+            )
+            moved = exchange(shifted, plane)
+            (fields,) = call(fields_kernel, [(2, *spectrum_shape)], [], (), (moved, iy_matrix))
+            (sent,) = call(
+                functools.partial(sum_kernel, last),
+                [packed],
+                y_scratch,
+                (),
+                (fields, weights[level], fy_matrix),
+            )
     back = exchange(exchange(sent, ("zh",)), ("y",))
     return back.transpose(1, 0, 2, 3).reshape(2, 1, rows, length)
 

time: 291 us -> 286 us (0.983)
  local copies, waits for them, and re-layouts: 29 us -> 21.4 us
  waiting for transfers between devices: 53 us -> 56.5 us
    unnamed x71, local copies, waits for them, and re-layouts: 26.2 us -> 19.1 us
    all_to_all x4, waiting for transfers between devices: 28.8 us -> 31.8 us  [exchange(): return lax.all_to_all(values, axes, split_axis=0, concat_axis=0, tiled=True)]
    pallas_call x10 -> x14, Pallas kernels: 35.6 us -> 35.8 us  [call(): pl.pallas_call(kernel, out_shape=[jax.ShapeDtypeStruct(s, jnp.float32) fo...]
where the time goes in v7:
time: 286 us; the launch traced here: 285 us
  blocking collectives  124 us (43%)
  waiting for transfers between devices  56.5 us (20%)
  starting transfers between devices  46.4 us (16%)
  Pallas kernels  35.8 us (13%)
  local copies, waits for them, and re-layouts  21.4 us (7%)
    all_to_all x5, blocking collectives, exchange(): return lax.all_to_all(values, axes, split_axis=0, concat_axis=0, tiled=True)  124 us
    pallas_call x14, Pallas kernels, call(): pl.pallas_call(kernel, out_shape=[jax.ShapeDtypeStruct(s, jnp.float32) fo...  35.8 us
    all_to_all x4, waiting for transfers between devices, exchange(): return lax.all_to_all(values, axes, split_axis=0, concat_axis=0, tiled=True)  31.8 us
    all_to_all x4, starting transfers between devices, exchange(): return lax.all_to_all(values, axes, split_axis=0, concat_axis=0, tiled=True)  28.4 us
    ppermute x8, waiting for transfers between devices, around_z(): tiles[n] = lax.ppermute(tiles[n - 1], axes, down)  21.9 us
    unnamed x71, local copies, waits for them, and re-layouts  19.1 us
    ppermute x8, starting transfers between devices, around_z(): tiles[n] = lax.ppermute(tiles[n - 1], axes, down)  11.2 us
    ppermute x6, starting transfers between devices, around_z(): tiles[ring - n] = lax.ppermute(tiles[(ring + 1 - n) % ring], axes, up)  6.8 us
  transfers between devices with their start and end apart: 18, of which 13 were waited for; matrix products, arithmetic and copies ran while one was open for 0% of the time, Pallas kernels for 5%

profile of v7, /device:TPU:2, one launch (start us, length us, event | category | flops | bytes accessed | tf_op | source)
XLA Modules:
  0.0 285.0 jit_solution(4886310006930028205)
XLA Ops:
  4.7 21.6 %all_to_all.45 = f32[4,616,128]{2,1,0:T(8,128)S(1)} all-to-all(f32[4,616,128]{2,1,0:T(8,128)S(1)} %shard_map.91), channel_id=1, replica_groups=mesh['zl'=2,'y'=4,'zh'=4,'x'=4,'c'=2] {'y'}, dimensions={0} | all-to-all | bytes 2523136 | tf_op jit(solution)/shard_map/all_to_all | solution.py:525
  27.4 11.6 %all-to-all-start.1 = ((f32[32,64,128]{2,1,0:T(8,128)}), f32[32,64,128]{2,1,0:T(8,128)S(1)}, u32[]{:S(2)}, u32[]{:S(2)}) async-start(f32[32,64,128]{2,1,0:T(8,128)} %bitcast.14), calls=%async_computation.1 | async-start | bytes 2097152 | tf_op jit(solution)/shard_map/all_to_all | solution.py:525
  39.4 7.5 %shard_map.93 = (f32[2,256,1024]{2,1,0:T(8,128)S(1)}, f32[2,256,1024]{2,1,0:T(8,128)S(1)}, f32[2,256,1024]{2,1,0:T(8,128)S(1)}) custom-call(s32[3]{0:T(128)S(1)} %pad_add_fusion.place, f32[4]{0:T(128)S(1)} %slice_reduce_fusion.freqs, f32[3,2]{1,0:T(4,128)S(1)} %copy.13.ref_slow), custom_call_target="tpu_custom_call" | custom-call | tf_op jit(solution)/shard_map/pallas_call | solution.py:514
  51.0 16.6 %all-to-all-done.1 = f32[32,64,128]{2,1,0:T(8,128)S(1)} async-done(((f32[32,64,128]{2,1,0:T(8,128)}), f32[32,64,128]{2,1,0:T(8,128)S(1)}, u32[]{:S(2)}, u32[]{:S(2)}) %all-to-all-start.1) | async-done | bytes 1048608 | tf_op jit(solution)/shard_map/all_to_all | solution.py:525
  69.2 3.4 %shard_map.94 = f32[32,2,64,128]{3,2,1,0:T(8,128)} custom-call(f32[256,1024]{1,0:T(8,128)S(1)} %shard_map.92.spectrum, f32[2,256,1024]{2,1,0:T(8,128)S(1)} %copy-done.17, bf16[2,256,256]{2,1,0:T(8,128)(2,1)S(1)} %copy-done.8, f32[2,8,128,128]{3,2,1,0:T(8,128)S(1)} %copy-done), custom_call_target="tpu_custom_call" | custom-call | tf_op jit(solution)/shard_map/pallas_call | solution.py:514
  72.6 5.5 %all-to-all-start.2 = ((f32[32,2,64,128]{3,2,1,0:T(8,128)}), f32[32,2,64,128]{3,2,1,0:T(8,128)S(1)}, u32[]{:S(2)}, u32[]{:S(2)}) async-start(f32[32,2,64,128]{3,2,1,0:T(8,128)} %shard_map.94), calls=%async_computation.2 | async-start | bytes 4194304 | tf_op jit(solution)/shard_map/all_to_all | solution.py:525
  78.4 1.9 collective-permute-start.4
  80.3 2.2 collective-permute-done.refs_1_
  84.6 2.2 collective-permute-done.1.refs_2_
  86.8 2.6 collective-permute-start.2
  91.3 3.6 %collective-permute-start.3 = (f32[4,32,128]{2,1,0:T(8,128)S(1)}, f32[4,32,128]{2,1,0:T(8,128)S(1)}, u32[]{:S(2)}, u32[]{:S(2)}) collective-permute-start(f32[4,32,128]{2,1,0:T(8,128)S(1)} %collective-permute-done.2.refs_3_), channel_id=1, source_target_pairs={{0,152},{128,0},{8,128},{136,8},{16,136},{144,16},{24,144},{152,24... | collective-permute-start | bytes 196616 | tf_op jit(solution)/shard_map/ppermute | solution.py:535
  96.8 2.3 shard_map.96.weights
  100.5 5.6 %all-to-all-done.2.moved = f32[32,2,64,128]{3,2,1,0:T(8,128)S(1)} async-done(((f32[32,2,64,128]{3,2,1,0:T(8,128)}), f32[32,2,64,128]{3,2,1,0:T(8,128)S(1)}, u32[]{:S(2)}, u32[]{:S(2)}) %all-to-all-start.2) | async-done | bytes 2097184 | tf_op jit(solution)/shard_map/all_to_all | solution.py:525
  108.6 3.0 %shard_map.97 = f32[32,64,128]{2,1,0:T(8,128)} custom-call(f32[2,16,64,256]{3,2,1,0:T(8,128)S(1)} %shard_map.95.fields, f32[4,16,64,128]{3,2,1,0:T(8,128)S(1)} %copy-done.2, bf16[2,256,256]{2,1,0:T(8,128)(2,1)S(1)} %copy-done.4), custom_call_target="tpu_custom_call" | custom-call | tf_op jit(solution)/shard_map/pallas_call | solution.py:514
  111.6 6.1 %all-to-all-start.3 = ((f32[32,64,128]{2,1,0:T(8,128)}), f32[32,64,128]{2,1,0:T(8,128)S(1)}, u32[]{:S(2)}, u32[]{:S(2)}) async-start(f32[32,64,128]{2,1,0:T(8,128)} %shard_map.97), calls=%async_computation.3 | async-start | bytes 2097152 | tf_op jit(solution)/shard_map/all_to_all | solution.py:525
  119.8 3.5 %collective-permute-done.7.refs_1_ = f32[4,64,128]{2,1,0:T(8,128)S(1)} collective-permute-done((f32[4,64,128]{2,1,0:T(8,128)S(1)}, f32[4,64,128]{2,1,0:T(8,128)S(1)}, u32[]{:S(2)}, u32[]{:S(2)}) %collective-permute-start.7) | collective-permute-done | bytes 131104 | tf_op jit(solution)/shard_map/ppermute | solution.py:535
  125.3 2.9 %collective-permute-done.8.refs_2_ = f32[4,64,128]{2,1,0:T(8,128)S(1)} collective-permute-done((f32[4,64,128]{2,1,0:T(8,128)S(1)}, f32[4,64,128]{2,1,0:T(8,128)S(1)}, u32[]{:S(2)}, u32[]{:S(2)}) %collective-permute-start.8) | collective-permute-done | bytes 131104 | tf_op jit(solution)/shard_map/ppermute | solution.py:535
  128.3 2.7 collective-permute-done.10.refs_6_
  131.0 2.9 %all-to-all-done.3 = f32[32,64,128]{2,1,0:T(8,128)S(1)} async-done(((f32[32,64,128]{2,1,0:T(8,128)}), f32[32,64,128]{2,1,0:T(8,128)S(1)}, u32[]{:S(2)}, u32[]{:S(2)}) %all-to-all-start.3) | async-done | bytes 1048608 | tf_op jit(solution)/shard_map/all_to_all | solution.py:525
  135.5 3.4 %shard_map.99 = f32[32,2,64,128]{3,2,1,0:T(8,128)} custom-call(f32[256,1024]{1,0:T(8,128)S(1)} %shard_map.98.spectrum, f32[2,256,1024]{2,1,0:T(8,128)S(1)} %copy-done.15, bf16[2,256,256]{2,1,0:T(8,128)(2,1)S(1)} %copy-done.9, f32[2,8,128,128]{3,2,1,0:T(8,128)S(1)} %copy-done), custom_call_target="tpu_custom_call" | custom-call | tf_op jit(solution)/shard_map/pallas_call | solution.py:514
  138.9 5.1 %all-to-all-start.4 = ((f32[32,2,64,128]{3,2,1,0:T(8,128)}), f32[32,2,64,128]{3,2,1,0:T(8,128)S(1)}, u32[]{:S(2)}, u32[]{:S(2)}) async-start(f32[32,2,64,128]{3,2,1,0:T(8,128)} %shard_map.99), calls=%async_computation.4 | async-start | bytes 4194304 | tf_op jit(solution)/shard_map/all_to_all | solution.py:525
  146.2 3.7 %collective-permute-done.11.refs_3_ = f32[4,64,128]{2,1,0:T(8,128)S(1)} collective-permute-done((f32[4,64,128]{2,1,0:T(8,128)}, f32[4,64,128]{2,1,0:T(8,128)S(1)}, u32[]{:S(2)}, u32[]{:S(2)}) %collective-permute-start.11) | collective-permute-done | bytes 131104 | tf_op jit(solution)/shard_map/ppermute | solution.py:535
  151.4 3.5 %collective-permute-done.12.refs_4_ = f32[4,64,128]{2,1,0:T(8,128)S(1)} collective-permute-done((f32[4,64,128]{2,1,0:T(8,128)S(1)}, f32[4,64,128]{2,1,0:T(8,128)S(1)}, u32[]{:S(2)}, u32[]{:S(2)}) %collective-permute-start.12) | collective-permute-done | bytes 131104 | tf_op jit(solution)/shard_map/ppermute | solution.py:535
  158.5 4.0 %shard_map.101 = (f32[4,16,64,128]{3,2,1,0:T(8,128)S(1)}, f32[4,16,64,128]{3,2,1,0:T(8,128)S(1)}) custom-call(s32[3]{0:T(128)S(1)} %pad_add_fusion.place, f32[4]{0:T(128)S(1)} %slice_reduce_fusion.freqs, f32[3,2]{1,0:T(4,128)S(1)} %copy.13.ref_slow, f32[4,64,128]{2,1,0:T(8,128)S(1)} %slice.18.refs_0_, f32[4,64,128]{2,1,0:T(8,128)S(1)} %copy-done.27, ...), custom_call_target="tpu_custom_call" | custom-call | tf_op jit(solution)/shard_map/pallas_call | solution.py:514
  165.3 6.8 %all-to-all-done.4.moved = f32[32,2,64,128]{3,2,1,0:T(8,128)S(1)} async-done(((f32[32,2,64,128]{3,2,1,0:T(8,128)}), f32[32,2,64,128]{3,2,1,0:T(8,128)S(1)}, u32[]{:S(2)}, u32[]{:S(2)}) %all-to-all-start.4) | async-done | bytes 2097184 | tf_op jit(solution)/shard_map/all_to_all | solution.py:525
  174.6 2.0 shard_map.102
  176.6 21.4 %all_to_all.46 = f32[32,64,128]{2,1,0:T(8,128)S(1)} all-to-all(f32[32,64,128]{2,1,0:T(8,128)S(1)} %shard_map.102), channel_id=1, replica_groups=mesh['zl'=2,'y'=4,'zh'=4,'x'=4,'c'=2] {'y','x','c'}, dimensions={0} | all-to-all | bytes 2097152 | tf_op jit(solution)/shard_map/all_to_all | solution.py:525
  198.0 3.1 %shard_map.103 = f32[32,2,64,128]{3,2,1,0:T(8,128)S(1)} custom-call(f32[2048,128]{1,0:T(8,128)S(1)} %bitcast.13, f32[2,256,1024]{2,1,0:T(8,128)S(1)} %copy-done.19, bf16[2,256,256]{2,1,0:T(8,128)(2,1)S(1)} %copy-done.13, bf16[2,256,256]{2,1,0:T(8,128)(2,1)S(1)} %copy-done.10, f32[2,8,128,128]{3,2,1,0:T(8,128)S(1)} %copy-done), custom_call_target="tpu_custom_call" | custom-call | tf_op jit(solution)/shard_map/pallas_call | solution.py:514
  201.2 32.0 %all_to_all.47.moved = f32[32,2,64,128]{3,2,1,0:T(8,128)S(1)} all-to-all(f32[32,2,64,128]{3,2,1,0:T(8,128)S(1)} %shard_map.103), channel_id=1, replica_groups=mesh['zl'=2,'y'=4,'zh'=4,'x'=4,'c'=2] {'y','x','c'}, dimensions={0} | all-to-all | bytes 4194304 | tf_op jit(solution)/shard_map/all_to_all | solution.py:525
  233.2 1.9 shard_map.104
  235.1 31.1 %all_to_all.48 = f32[4,2,16,2048]{3,2,1,0:T(8,128)S(1)} all-to-all(f32[4,2,16,2048]{3,2,1,0:T(8,128)S(1)} %shard_map.104), channel_id=1, replica_groups=mesh['zl'=2,'y'=4,'zh'=4,'x'=4,'c'=2] {'zh'}, dimensions={0} | all-to-all | bytes 2097152 | tf_op jit(solution)/shard_map/all_to_all | solution.py:525
  266.2 17.7 %all_to_all.49 = f32[4,2,16,2048]{3,2,1,0:T(8,128)S(1)} all-to-all(f32[4,2,16,2048]{3,2,1,0:T(8,128)S(1)} %all_to_all.48), channel_id=1, replica_groups=mesh['zl'=2,'y'=4,'zh'=4,'x'=4,'c'=2] {'y'}, dimensions={0} | all-to-all | bytes 2097152 | tf_op jit(solution)/shard_map/all_to_all | solution.py:525
  (101 shorter events, 40.3 us)
Async XLA Ops:
  26.4 12.7 %copy-start.34 = (f32[3,2]{0,1:T(2,128)S(1)}, f32[3,2]{0,1:T(2,128)}, u32[]{:S(2)}) copy-start(f32[3,2]{0,1:T(2,128)} %param.12) | copy-start | bytes 76
  26.4 41.2 %copy-start = (f32[2,8,128,128]{3,2,1,0:T(8,128)S(1)}, f32[2,8,128,128]{3,2,1,0:T(8,128)}, u32[]{:S(2)}) copy-start(f32[2,8,128,128]{3,2,1,0:T(8,128)} %constant.35.clone.turns) | copy-start | bytes 3145732
  26.4 41.2 %copy-start.11 = (bf16[2,256,256]{2,1,0:T(8,128)(2,1)S(1)}, bf16[2,256,256]{2,1,0:T(8,128)(2,1)}, u32[]{:S(2)}) copy-start(bf16[2,256,256]{2,1,0:T(8,128)(2,1)} %constant.34.clone.there_matrices) | copy-start | bytes 786436
  27.4 40.2 %all-to-all-start.1 = ((f32[32,64,128]{2,1,0:T(8,128)}), f32[32,64,128]{2,1,0:T(8,128)S(1)}, u32[]{:S(2)}, u32[]{:S(2)}) async-start(f32[32,64,128]{2,1,0:T(8,128)} %bitcast.14), calls=%async_computation.1 | async-start | bytes 2097152 | tf_op jit(solution)/shard_map/all_to_all | solution.py:525
  39.1 29.6 %copy-start.8 = (bf16[2,256,256]{2,1,0:T(8,128)(2,1)S(1)}, bf16[2,256,256]{2,1,0:T(8,128)(2,1)}, u32[]{:S(2)}) copy-start(bf16[2,256,256]{2,1,0:T(8,128)(2,1)} %constant.36.clone.back_matrices) | copy-start | bytes 786436
  72.6 33.4 %all-to-all-start.2 = ((f32[32,2,64,128]{3,2,1,0:T(8,128)}), f32[32,2,64,128]{3,2,1,0:T(8,128)S(1)}, u32[]{:S(2)}, u32[]{:S(2)}) async-start(f32[32,2,64,128]{3,2,1,0:T(8,128)} %shard_map.94), calls=%async_computation.2 | async-start | bytes 4194304 | tf_op jit(solution)/shard_map/all_to_all | solution.py:525
  78.2 4.3 %collective-permute-start = (f32[4,32,128]{2,1,0:T(8,128)S(1)}, f32[4,32,128]{2,1,0:T(8,128)S(1)}, u32[]{:S(2)}, u32[]{:S(2)}) collective-permute-start(f32[4,32,128]{2,1,0:T(8,128)S(1)} %slice.17.refs_0_), channel_id=1, source_target_pairs={{0,152},{128,0},{8,128},{136,8},{16,136},{144,16},{24,144},{152,24... | collective-permute-start | bytes 196616 | tf_op jit(solution)/shard_map/ppermute | solution.py:535
  78.4 5.6 %collective-permute-start.4 = (f32[4,32,128]{2,1,0:T(8,128)S(1)}, f32[4,32,128]{2,1,0:T(8,128)S(1)}, u32[]{:S(2)}, u32[]{:S(2)}) collective-permute-start(f32[4,32,128]{2,1,0:T(8,128)S(1)} %slice.17.refs_0_), channel_id=1, source_target_pairs={{152,0},{0,128},{128,8},{8,136},{136,16},{16,144},{144,24},{24,152... | collective-permute-start | bytes 196616 | tf_op jit(solution)/shard_map/ppermute | solution.py:537
  82.5 4.3 %collective-permute-start.1 = (f32[4,32,128]{2,1,0:T(8,128)S(1)}, f32[4,32,128]{2,1,0:T(8,128)S(1)}, u32[]{:S(2)}, u32[]{:S(2)}) collective-permute-start(f32[4,32,128]{2,1,0:T(8,128)S(1)} %collective-permute-done.refs_1_), channel_id=1, source_target_pairs={{0,152},{128,0},{8,128},{136,8},{16,136},{144,16},{24,144},{152,24... | collective-permute-start | bytes 196616 | tf_op jit(solution)/shard_map/ppermute | solution.py:535
  83.9 5.5 %collective-permute-start.5 = (f32[4,32,128]{2,1,0:T(8,128)S(1)}, f32[4,32,128]{2,1,0:T(8,128)S(1)}, u32[]{:S(2)}, u32[]{:S(2)}) collective-permute-start(f32[4,32,128]{2,1,0:T(8,128)S(1)} %collective-permute-done.4.refs_7_), channel_id=1, source_target_pairs={{152,0},{0,128},{128,8},{8,136},{136,16},{16,144},{144,24},{24,152... | collective-permute-start | bytes 196616 | tf_op jit(solution)/shard_map/ppermute | solution.py:537
  86.8 4.5 %collective-permute-start.2 = (f32[4,32,128]{2,1,0:T(8,128)S(1)}, f32[4,32,128]{2,1,0:T(8,128)S(1)}, u32[]{:S(2)}, u32[]{:S(2)}) collective-permute-start(f32[4,32,128]{2,1,0:T(8,128)S(1)} %collective-permute-done.1.refs_2_), channel_id=1, source_target_pairs={{0,152},{128,0},{8,128},{136,8},{16,136},{144,16},{24,144},{152,24... | collective-permute-start | bytes 196616 | tf_op jit(solution)/shard_map/ppermute | solution.py:535
  89.4 5.5 %collective-permute-start.6 = (f32[4,32,128]{2,1,0:T(8,128)S(1)}, f32[4,32,128]{2,1,0:T(8,128)S(1)}, u32[]{:S(2)}, u32[]{:S(2)}) collective-permute-start(f32[4,32,128]{2,1,0:T(8,128)S(1)} %collective-permute-done.5.refs_6_), channel_id=1, source_target_pairs={{152,0},{0,128},{128,8},{8,136},{136,16},{16,144},{144,24},{24,152... | collective-permute-start | bytes 196616 | tf_op jit(solution)/shard_map/ppermute | solution.py:537
  91.3 5.5 %collective-permute-start.3 = (f32[4,32,128]{2,1,0:T(8,128)S(1)}, f32[4,32,128]{2,1,0:T(8,128)S(1)}, u32[]{:S(2)}, u32[]{:S(2)}) collective-permute-start(f32[4,32,128]{2,1,0:T(8,128)S(1)} %collective-permute-done.2.refs_3_), channel_id=1, source_target_pairs={{0,152},{128,0},{8,128},{136,8},{16,136},{144,16},{24,144},{152,24... | collective-permute-start | bytes 196616 | tf_op jit(solution)/shard_map/ppermute | solution.py:535
  111.6 22.3 %copy-start.12 = (bf16[2,256,256]{2,1,0:T(8,128)(2,1)S(1)}, bf16[2,256,256]{2,1,0:T(8,128)(2,1)}, u32[]{:S(2)}) copy-start(bf16[2,256,256]{2,1,0:T(8,128)(2,1)} %constant.34.clone.there_matrices) | copy-start | bytes 786436
  111.6 22.3 %all-to-all-start.3 = ((f32[32,64,128]{2,1,0:T(8,128)}), f32[32,64,128]{2,1,0:T(8,128)S(1)}, u32[]{:S(2)}, u32[]{:S(2)}) async-start(f32[32,64,128]{2,1,0:T(8,128)} %shard_map.97), calls=%async_computation.3 | async-start | bytes 2097152 | tf_op jit(solution)/shard_map/all_to_all | solution.py:525
  117.7 17.3 %copy-start.9 = (bf16[2,256,256]{2,1,0:T(8,128)(2,1)S(1)}, bf16[2,256,256]{2,1,0:T(8,128)(2,1)}, u32[]{:S(2)}) copy-start(bf16[2,256,256]{2,1,0:T(8,128)(2,1)} %constant.36.clone.back_matrices) | copy-start | bytes 786436
  117.7 5.6 %collective-permute-start.7 = (f32[4,64,128]{2,1,0:T(8,128)S(1)}, f32[4,64,128]{2,1,0:T(8,128)S(1)}, u32[]{:S(2)}, u32[]{:S(2)}) collective-permute-start(f32[4,64,128]{2,1,0:T(8,128)S(1)} %slice.18.refs_0_), channel_id=1, source_target_pairs={{0,152},{128,0},{8,128},{136,8},{16,136},{144,16},{24,144},{152,24... | collective-permute-start | bytes 393224 | tf_op jit(solution)/shard_map/ppermute | solution.py:535
  117.9 6.9 %collective-permute-start.9 = (f32[4,64,128]{2,1,0:T(8,128)S(1)}, f32[4,64,128]{2,1,0:T(8,128)S(1)}, u32[]{:S(2)}, u32[]{:S(2)}) collective-permute-start(f32[4,64,128]{2,1,0:T(8,128)S(1)} %slice.18.refs_0_), channel_id=1, source_target_pairs={{152,0},{0,128},{128,8},{8,136},{136,16},{16,144},{144,24},{24,152... | collective-permute-start | bytes 393224 | tf_op jit(solution)/shard_map/ppermute | solution.py:537
  123.3 15.6 %copy-start.26 = (f32[4,64,128]{2,1,0:T(8,128)}, f32[4,64,128]{2,1,0:T(8,128)S(1)}, u32[]{:S(2)}) copy-start(f32[4,64,128]{2,1,0:T(8,128)S(1)} %collective-permute-done.7.refs_1_) | copy-start | bytes 393220
  123.3 5.0 %collective-permute-start.8 = (f32[4,64,128]{2,1,0:T(8,128)S(1)}, f32[4,64,128]{2,1,0:T(8,128)S(1)}, u32[]{:S(2)}, u32[]{:S(2)}) collective-permute-start(f32[4,64,128]{2,1,0:T(8,128)S(1)} %collective-permute-done.7.refs_1_), channel_id=1, source_target_pairs={{0,152},{128,0},{8,128},{136,8},{16,136},{144,16},{24,144},{152,24... | collective-permute-start | bytes 393224 | tf_op jit(solution)/shard_map/ppermute | solution.py:535
  124.8 14.1 %copy-start.28 = (f32[4,64,128]{2,1,0:T(8,128)}, f32[4,64,128]{2,1,0:T(8,128)S(1)}, u32[]{:S(2)}) copy-start(f32[4,64,128]{2,1,0:T(8,128)S(1)} %collective-permute-done.9.refs_7_) | copy-start | bytes 393220
  124.8 6.2 %collective-permute-start.10 = (f32[4,64,128]{2,1,0:T(8,128)S(1)}, f32[4,64,128]{2,1,0:T(8,128)S(1)}, u32[]{:S(2)}, u32[]{:S(2)}) collective-permute-start(f32[4,64,128]{2,1,0:T(8,128)S(1)} %collective-permute-done.9.refs_7_), channel_id=1, source_target_pairs={{152,0},{0,128},{128,8},{8,136},{136,16},{16,144},{144,24},{24,152... | collective-permute-start | bytes 393224 | tf_op jit(solution)/shard_map/ppermute | solution.py:537
  128.3 10.6 %copy-start.30 = (f32[4,64,128]{2,1,0:T(8,128)}, f32[4,64,128]{2,1,0:T(8,128)S(1)}, u32[]{:S(2)}) copy-start(f32[4,64,128]{2,1,0:T(8,128)S(1)} %collective-permute-done.8.refs_2_) | copy-start | bytes 393220
  138.9 33.1 %all-to-all-start.4 = ((f32[32,2,64,128]{3,2,1,0:T(8,128)}), f32[32,2,64,128]{3,2,1,0:T(8,128)S(1)}, u32[]{:S(2)}, u32[]{:S(2)}) async-start(f32[32,2,64,128]{3,2,1,0:T(8,128)} %shard_map.99), calls=%async_computation.4 | async-start | bytes 4194304 | tf_op jit(solution)/shard_map/all_to_all | solution.py:525
  144.1 5.8 %collective-permute-start.11 = (f32[4,64,128]{2,1,0:T(8,128)}, f32[4,64,128]{2,1,0:T(8,128)S(1)}, u32[]{:S(2)}, u32[]{:S(2)}) collective-permute-start(f32[4,64,128]{2,1,0:T(8,128)} %copy-done.30), channel_id=1, source_target_pairs={{0,152},{128,0},{8,128},{136,8},{16,136},{144,16},{24,144},{152,24... | collective-permute-start | bytes 393224 | tf_op jit(solution)/shard_map/ppermute | solution.py:535
  144.3 7.1 %collective-permute-start.13 = (f32[4,64,128]{2,1,0:T(8,128)}, f32[4,64,128]{2,1,0:T(8,128)S(1)}, u32[]{:S(2)}, u32[]{:S(2)}) collective-permute-start(f32[4,64,128]{2,1,0:T(8,128)} %copy-done.32), channel_id=1, source_target_pairs={{152,0},{0,128},{128,8},{8,136},{136,16},{16,144},{144,24},{24,152... | collective-permute-start | bytes 393224 | tf_op jit(solution)/shard_map/ppermute | solution.py:537
  149.9 5.0 %collective-permute-start.12 = (f32[4,64,128]{2,1,0:T(8,128)S(1)}, f32[4,64,128]{2,1,0:T(8,128)S(1)}, u32[]{:S(2)}, u32[]{:S(2)}) collective-permute-start(f32[4,64,128]{2,1,0:T(8,128)S(1)} %collective-permute-done.11.refs_3_), channel_id=1, source_target_pairs={{0,152},{128,0},{8,128},{136,8},{16,136},{144,16},{24,144},{152,24... | collective-permute-start | bytes 393224 | tf_op jit(solution)/shard_map/ppermute | solution.py:535
  174.6 23.4 %copy-start.19 = (f32[2,256,1024]{2,1,0:T(8,128)S(1)}, f32[2,256,1024]{2,1,0:T(8,128)}, u32[]{:S(2)}) copy-start(f32[2,256,1024]{2,1,0:T(8,128)} %copy-done.18) | copy-start | bytes 6291460
  176.6 21.4 %copy-start.10 = (bf16[2,256,256]{2,1,0:T(8,128)(2,1)S(1)}, bf16[2,256,256]{2,1,0:T(8,128)(2,1)}, u32[]{:S(2)}) copy-start(bf16[2,256,256]{2,1,0:T(8,128)(2,1)} %constant.36.clone.back_matrices) | copy-start | bytes 786436
  176.6 21.4 %copy-start.13 = (bf16[2,256,256]{2,1,0:T(8,128)(2,1)S(1)}, bf16[2,256,256]{2,1,0:T(8,128)(2,1)}, u32[]{:S(2)}) copy-start(bf16[2,256,256]{2,1,0:T(8,128)(2,1)} %constant.34.clone.there_matrices) | copy-start | bytes 786436
  201.1 32.0 %copy-start.7 = (bf16[2,256,256]{2,1,0:T(8,128)(2,1)S(1)}, bf16[2,256,256]{2,1,0:T(8,128)(2,1)}, u32[]{:S(2)}) copy-start(bf16[2,256,256]{2,1,0:T(8,128)(2,1)} %constant.37.clone.back_matrices) | copy-start | bytes 786436
  201.1 32.0 %copy-start.23 = (f32[4,16,64,128]{3,2,1,0:T(8,128)S(1)}, f32[4,16,64,128]{3,2,1,0:T(8,128)}, u32[]{:S(2)}) copy-start(f32[4,16,64,128]{3,2,1,0:T(8,128)} %copy-done.22) | copy-start | bytes 6291460
  (21 other events, 38.6 us)

commit v8 on v7

--- a/solution.py
+++ b/solution.py
@@ -474,7 +474,7 @@
                 shifted[branch, second_half, columns] = moved[1]
         return carry
 
-    lax.fori_loop(0, steps, propagate, 0)
+    lax.fori_loop(0, steps, propagate, 0, unroll=4)
     matrix = (back_matrices[0], back_matrices[1])
     for branch in range(2):
         for n in range(4):

time: 286 us -> 286 us (level)
  no operation moved by 1% of the time
where the time goes in v8:
time: 286 us; the launch traced here: 285 us
  blocking collectives  124 us (43%)
  waiting for transfers between devices  56.5 us (20%)
  starting transfers between devices  46.4 us (16%)
  Pallas kernels  35.6 us (12%)
  local copies, waits for them, and re-layouts  21.4 us (7%)
    all_to_all x5, blocking collectives, exchange(): return lax.all_to_all(values, axes, split_axis=0, concat_axis=0, tiled=True)  124 us
    pallas_call x14, Pallas kernels, call(): pl.pallas_call(kernel, out_shape=[jax.ShapeDtypeStruct(s, jnp.float32) fo...  35.6 us
    all_to_all x4, waiting for transfers between devices, exchange(): return lax.all_to_all(values, axes, split_axis=0, concat_axis=0, tiled=True)  31.8 us
    all_to_all x4, starting transfers between devices, exchange(): return lax.all_to_all(values, axes, split_axis=0, concat_axis=0, tiled=True)  28.4 us
    ppermute x8, waiting for transfers between devices, around_z(): tiles[n] = lax.ppermute(tiles[n - 1], axes, down)  21.9 us
    unnamed x71, local copies, waits for them, and re-layouts  19.1 us
    ppermute x8, starting transfers between devices, around_z(): tiles[n] = lax.ppermute(tiles[n - 1], axes, down)  11.2 us
    ppermute x6, starting transfers between devices, around_z(): tiles[ring - n] = lax.ppermute(tiles[(ring + 1 - n) % ring], axes, up)  6.8 us
  transfers between devices with their start and end apart: 18, of which 13 were waited for; matrix products, arithmetic and copies ran while one was open for 0% of the time, Pallas kernels for 5%

profile of v8, /device:TPU:2, one launch (start us, length us, event | category | flops | bytes accessed | tf_op | source)
XLA Modules:
  0.0 284.8 jit_solution(9996876412062489486)
XLA Ops:
  4.7 21.6 %all_to_all.45 = f32[4,616,128]{2,1,0:T(8,128)S(1)} all-to-all(f32[4,616,128]{2,1,0:T(8,128)S(1)} %shard_map.91), channel_id=1, replica_groups=mesh['zl'=2,'y'=4,'zh'=4,'x'=4,'c'=2] {'y'}, dimensions={0} | all-to-all | bytes 2523136 | tf_op jit(solution)/shard_map/all_to_all | solution.py:525
  27.4 11.6 %all-to-all-start.1 = ((f32[32,64,128]{2,1,0:T(8,128)}), f32[32,64,128]{2,1,0:T(8,128)S(1)}, u32[]{:S(2)}, u32[]{:S(2)}) async-start(f32[32,64,128]{2,1,0:T(8,128)} %bitcast.14), calls=%async_computation.1 | async-start | bytes 2097152 | tf_op jit(solution)/shard_map/all_to_all | solution.py:525
  39.4 7.5 %shard_map.93 = (f32[2,256,1024]{2,1,0:T(8,128)S(1)}, f32[2,256,1024]{2,1,0:T(8,128)S(1)}, f32[2,256,1024]{2,1,0:T(8,128)S(1)}) custom-call(s32[3]{0:T(128)S(1)} %pad_add_fusion.place, f32[4]{0:T(128)S(1)} %slice_reduce_fusion.freqs, f32[3,2]{1,0:T(4,128)S(1)} %copy.13.ref_slow), custom_call_target="tpu_custom_call" | custom-call | tf_op jit(solution)/shard_map/pallas_call | solution.py:514
  51.0 16.6 %all-to-all-done.1 = f32[32,64,128]{2,1,0:T(8,128)S(1)} async-done(((f32[32,64,128]{2,1,0:T(8,128)}), f32[32,64,128]{2,1,0:T(8,128)S(1)}, u32[]{:S(2)}, u32[]{:S(2)}) %all-to-all-start.1) | async-done | bytes 1048608 | tf_op jit(solution)/shard_map/all_to_all | solution.py:525
  69.2 3.4 %shard_map.94 = f32[32,2,64,128]{3,2,1,0:T(8,128)} custom-call(f32[256,1024]{1,0:T(8,128)S(1)} %shard_map.92.spectrum, f32[2,256,1024]{2,1,0:T(8,128)S(1)} %copy-done.17, bf16[2,256,256]{2,1,0:T(8,128)(2,1)S(1)} %copy-done.8, f32[2,8,128,128]{3,2,1,0:T(8,128)S(1)} %copy-done), custom_call_target="tpu_custom_call" | custom-call | tf_op jit(solution)/shard_map/pallas_call | solution.py:514
  72.6 5.5 %all-to-all-start.2 = ((f32[32,2,64,128]{3,2,1,0:T(8,128)}), f32[32,2,64,128]{3,2,1,0:T(8,128)S(1)}, u32[]{:S(2)}, u32[]{:S(2)}) async-start(f32[32,2,64,128]{3,2,1,0:T(8,128)} %shard_map.94), calls=%async_computation.2 | async-start | bytes 4194304 | tf_op jit(solution)/shard_map/all_to_all | solution.py:525
  78.3 1.9 collective-permute-start.4
  80.2 2.2 collective-permute-done.refs_1_
  84.5 2.2 collective-permute-done.1.refs_2_
  86.7 2.6 collective-permute-start.2
  91.2 3.6 %collective-permute-start.3 = (f32[4,32,128]{2,1,0:T(8,128)S(1)}, f32[4,32,128]{2,1,0:T(8,128)S(1)}, u32[]{:S(2)}, u32[]{:S(2)}) collective-permute-start(f32[4,32,128]{2,1,0:T(8,128)S(1)} %collective-permute-done.2.refs_3_), channel_id=1, source_target_pairs={{0,152},{128,0},{8,128},{136,8},{16,136},{144,16},{24,144},{152,24... | collective-permute-start | bytes 196616 | tf_op jit(solution)/shard_map/ppermute | solution.py:535
  96.7 2.3 shard_map.96.weights
  100.4 5.6 %all-to-all-done.2.moved = f32[32,2,64,128]{3,2,1,0:T(8,128)S(1)} async-done(((f32[32,2,64,128]{3,2,1,0:T(8,128)}), f32[32,2,64,128]{3,2,1,0:T(8,128)S(1)}, u32[]{:S(2)}, u32[]{:S(2)}) %all-to-all-start.2) | async-done | bytes 2097184 | tf_op jit(solution)/shard_map/all_to_all | solution.py:525
  108.5 3.0 %shard_map.97 = f32[32,64,128]{2,1,0:T(8,128)} custom-call(f32[2,16,64,256]{3,2,1,0:T(8,128)S(1)} %shard_map.95.fields, f32[4,16,64,128]{3,2,1,0:T(8,128)S(1)} %copy-done.2, bf16[2,256,256]{2,1,0:T(8,128)(2,1)S(1)} %copy-done.4), custom_call_target="tpu_custom_call" | custom-call | tf_op jit(solution)/shard_map/pallas_call | solution.py:514
  111.5 6.1 %all-to-all-start.3 = ((f32[32,64,128]{2,1,0:T(8,128)}), f32[32,64,128]{2,1,0:T(8,128)S(1)}, u32[]{:S(2)}, u32[]{:S(2)}) async-start(f32[32,64,128]{2,1,0:T(8,128)} %shard_map.97), calls=%async_computation.3 | async-start | bytes 2097152 | tf_op jit(solution)/shard_map/all_to_all | solution.py:525
  119.7 3.5 %collective-permute-done.7.refs_1_ = f32[4,64,128]{2,1,0:T(8,128)S(1)} collective-permute-done((f32[4,64,128]{2,1,0:T(8,128)S(1)}, f32[4,64,128]{2,1,0:T(8,128)S(1)}, u32[]{:S(2)}, u32[]{:S(2)}) %collective-permute-start.7) | collective-permute-done | bytes 131104 | tf_op jit(solution)/shard_map/ppermute | solution.py:535
  125.3 2.9 %collective-permute-done.8.refs_2_ = f32[4,64,128]{2,1,0:T(8,128)S(1)} collective-permute-done((f32[4,64,128]{2,1,0:T(8,128)S(1)}, f32[4,64,128]{2,1,0:T(8,128)S(1)}, u32[]{:S(2)}, u32[]{:S(2)}) %collective-permute-start.8) | collective-permute-done | bytes 131104 | tf_op jit(solution)/shard_map/ppermute | solution.py:535
  128.2 2.7 collective-permute-done.10.refs_6_
  130.9 2.9 %all-to-all-done.3 = f32[32,64,128]{2,1,0:T(8,128)S(1)} async-done(((f32[32,64,128]{2,1,0:T(8,128)}), f32[32,64,128]{2,1,0:T(8,128)S(1)}, u32[]{:S(2)}, u32[]{:S(2)}) %all-to-all-start.3) | async-done | bytes 1048608 | tf_op jit(solution)/shard_map/all_to_all | solution.py:525
  135.4 3.4 %shard_map.99 = f32[32,2,64,128]{3,2,1,0:T(8,128)} custom-call(f32[256,1024]{1,0:T(8,128)S(1)} %shard_map.98.spectrum, f32[2,256,1024]{2,1,0:T(8,128)S(1)} %copy-done.15, bf16[2,256,256]{2,1,0:T(8,128)(2,1)S(1)} %copy-done.9, f32[2,8,128,128]{3,2,1,0:T(8,128)S(1)} %copy-done), custom_call_target="tpu_custom_call" | custom-call | tf_op jit(solution)/shard_map/pallas_call | solution.py:514
  138.8 5.1 %all-to-all-start.4 = ((f32[32,2,64,128]{3,2,1,0:T(8,128)}), f32[32,2,64,128]{3,2,1,0:T(8,128)S(1)}, u32[]{:S(2)}, u32[]{:S(2)}) async-start(f32[32,2,64,128]{3,2,1,0:T(8,128)} %shard_map.99), calls=%async_computation.4 | async-start | bytes 4194304 | tf_op jit(solution)/shard_map/all_to_all | solution.py:525
  146.1 3.7 %collective-permute-done.11.refs_3_ = f32[4,64,128]{2,1,0:T(8,128)S(1)} collective-permute-done((f32[4,64,128]{2,1,0:T(8,128)}, f32[4,64,128]{2,1,0:T(8,128)S(1)}, u32[]{:S(2)}, u32[]{:S(2)}) %collective-permute-start.11) | collective-permute-done | bytes 131104 | tf_op jit(solution)/shard_map/ppermute | solution.py:535
  151.3 3.5 %collective-permute-done.12.refs_4_ = f32[4,64,128]{2,1,0:T(8,128)S(1)} collective-permute-done((f32[4,64,128]{2,1,0:T(8,128)S(1)}, f32[4,64,128]{2,1,0:T(8,128)S(1)}, u32[]{:S(2)}, u32[]{:S(2)}) %collective-permute-start.12) | collective-permute-done | bytes 131104 | tf_op jit(solution)/shard_map/ppermute | solution.py:535
  158.4 4.0 %shard_map.101 = (f32[4,16,64,128]{3,2,1,0:T(8,128)S(1)}, f32[4,16,64,128]{3,2,1,0:T(8,128)S(1)}) custom-call(s32[3]{0:T(128)S(1)} %pad_add_fusion.place, f32[4]{0:T(128)S(1)} %slice_reduce_fusion.freqs, f32[3,2]{1,0:T(4,128)S(1)} %copy.13.ref_slow, f32[4,64,128]{2,1,0:T(8,128)S(1)} %slice.18.refs_0_, f32[4,64,128]{2,1,0:T(8,128)S(1)} %copy-done.27, ...), custom_call_target="tpu_custom_call" | custom-call | tf_op jit(solution)/shard_map/pallas_call | solution.py:514
  165.2 6.8 %all-to-all-done.4.moved = f32[32,2,64,128]{3,2,1,0:T(8,128)S(1)} async-done(((f32[32,2,64,128]{3,2,1,0:T(8,128)}), f32[32,2,64,128]{3,2,1,0:T(8,128)S(1)}, u32[]{:S(2)}, u32[]{:S(2)}) %all-to-all-start.4) | async-done | bytes 2097184 | tf_op jit(solution)/shard_map/all_to_all | solution.py:525
  174.5 2.0 shard_map.102
  176.5 21.4 %all_to_all.46 = f32[32,64,128]{2,1,0:T(8,128)S(1)} all-to-all(f32[32,64,128]{2,1,0:T(8,128)S(1)} %shard_map.102), channel_id=1, replica_groups=mesh['zl'=2,'y'=4,'zh'=4,'x'=4,'c'=2] {'y','x','c'}, dimensions={0} | all-to-all | bytes 2097152 | tf_op jit(solution)/shard_map/all_to_all | solution.py:525
  197.9 3.0 %shard_map.103 = f32[32,2,64,128]{3,2,1,0:T(8,128)S(1)} custom-call(f32[2048,128]{1,0:T(8,128)S(1)} %bitcast.13, f32[2,256,1024]{2,1,0:T(8,128)S(1)} %copy-done.19, bf16[2,256,256]{2,1,0:T(8,128)(2,1)S(1)} %copy-done.13, bf16[2,256,256]{2,1,0:T(8,128)(2,1)S(1)} %copy-done.10, f32[2,8,128,128]{3,2,1,0:T(8,128)S(1)} %copy-done), custom_call_target="tpu_custom_call" | custom-call | tf_op jit(solution)/shard_map/pallas_call | solution.py:514
  201.0 32.0 %all_to_all.47.moved = f32[32,2,64,128]{3,2,1,0:T(8,128)S(1)} all-to-all(f32[32,2,64,128]{3,2,1,0:T(8,128)S(1)} %shard_map.103), channel_id=1, replica_groups=mesh['zl'=2,'y'=4,'zh'=4,'x'=4,'c'=2] {'y','x','c'}, dimensions={0} | all-to-all | bytes 4194304 | tf_op jit(solution)/shard_map/all_to_all | solution.py:525
  233.0 1.9 shard_map.104
  234.9 31.1 %all_to_all.48 = f32[4,2,16,2048]{3,2,1,0:T(8,128)S(1)} all-to-all(f32[4,2,16,2048]{3,2,1,0:T(8,128)S(1)} %shard_map.104), channel_id=1, replica_groups=mesh['zl'=2,'y'=4,'zh'=4,'x'=4,'c'=2] {'zh'}, dimensions={0} | all-to-all | bytes 2097152 | tf_op jit(solution)/shard_map/all_to_all | solution.py:525
  266.0 17.7 %all_to_all.49 = f32[4,2,16,2048]{3,2,1,0:T(8,128)S(1)} all-to-all(f32[4,2,16,2048]{3,2,1,0:T(8,128)S(1)} %all_to_all.48), channel_id=1, replica_groups=mesh['zl'=2,'y'=4,'zh'=4,'x'=4,'c'=2] {'y'}, dimensions={0} | all-to-all | bytes 2097152 | tf_op jit(solution)/shard_map/all_to_all | solution.py:525
  (101 shorter events, 40.3 us)
Async XLA Ops:
  26.4 12.7 %copy-start.34 = (f32[3,2]{0,1:T(2,128)S(1)}, f32[3,2]{0,1:T(2,128)}, u32[]{:S(2)}) copy-start(f32[3,2]{0,1:T(2,128)} %param.12) | copy-start | bytes 76
  26.4 41.2 %copy-start = (f32[2,8,128,128]{3,2,1,0:T(8,128)S(1)}, f32[2,8,128,128]{3,2,1,0:T(8,128)}, u32[]{:S(2)}) copy-start(f32[2,8,128,128]{3,2,1,0:T(8,128)} %constant.35.clone.turns) | copy-start | bytes 3145732
  26.4 41.2 %copy-start.11 = (bf16[2,256,256]{2,1,0:T(8,128)(2,1)S(1)}, bf16[2,256,256]{2,1,0:T(8,128)(2,1)}, u32[]{:S(2)}) copy-start(bf16[2,256,256]{2,1,0:T(8,128)(2,1)} %constant.34.clone.there_matrices) | copy-start | bytes 786436
  27.4 40.2 %all-to-all-start.1 = ((f32[32,64,128]{2,1,0:T(8,128)}), f32[32,64,128]{2,1,0:T(8,128)S(1)}, u32[]{:S(2)}, u32[]{:S(2)}) async-start(f32[32,64,128]{2,1,0:T(8,128)} %bitcast.14), calls=%async_computation.1 | async-start | bytes 2097152 | tf_op jit(solution)/shard_map/all_to_all | solution.py:525
  39.1 29.6 %copy-start.8 = (bf16[2,256,256]{2,1,0:T(8,128)(2,1)S(1)}, bf16[2,256,256]{2,1,0:T(8,128)(2,1)}, u32[]{:S(2)}) copy-start(bf16[2,256,256]{2,1,0:T(8,128)(2,1)} %constant.36.clone.back_matrices) | copy-start | bytes 786436
  72.6 33.4 %all-to-all-start.2 = ((f32[32,2,64,128]{3,2,1,0:T(8,128)}), f32[32,2,64,128]{3,2,1,0:T(8,128)S(1)}, u32[]{:S(2)}, u32[]{:S(2)}) async-start(f32[32,2,64,128]{3,2,1,0:T(8,128)} %shard_map.94), calls=%async_computation.2 | async-start | bytes 4194304 | tf_op jit(solution)/shard_map/all_to_all | solution.py:525
  78.1 4.3 %collective-permute-start = (f32[4,32,128]{2,1,0:T(8,128)S(1)}, f32[4,32,128]{2,1,0:T(8,128)S(1)}, u32[]{:S(2)}, u32[]{:S(2)}) collective-permute-start(f32[4,32,128]{2,1,0:T(8,128)S(1)} %slice.17.refs_0_), channel_id=1, source_target_pairs={{0,152},{128,0},{8,128},{136,8},{16,136},{144,16},{24,144},{152,24... | collective-permute-start | bytes 196616 | tf_op jit(solution)/shard_map/ppermute | solution.py:535
  78.3 5.6 %collective-permute-start.4 = (f32[4,32,128]{2,1,0:T(8,128)S(1)}, f32[4,32,128]{2,1,0:T(8,128)S(1)}, u32[]{:S(2)}, u32[]{:S(2)}) collective-permute-start(f32[4,32,128]{2,1,0:T(8,128)S(1)} %slice.17.refs_0_), channel_id=1, source_target_pairs={{152,0},{0,128},{128,8},{8,136},{136,16},{16,144},{144,24},{24,152... | collective-permute-start | bytes 196616 | tf_op jit(solution)/shard_map/ppermute | solution.py:537
  82.5 4.3 %collective-permute-start.1 = (f32[4,32,128]{2,1,0:T(8,128)S(1)}, f32[4,32,128]{2,1,0:T(8,128)S(1)}, u32[]{:S(2)}, u32[]{:S(2)}) collective-permute-start(f32[4,32,128]{2,1,0:T(8,128)S(1)} %collective-permute-done.refs_1_), channel_id=1, source_target_pairs={{0,152},{128,0},{8,128},{136,8},{16,136},{144,16},{24,144},{152,24... | collective-permute-start | bytes 196616 | tf_op jit(solution)/shard_map/ppermute | solution.py:535
  83.8 5.5 %collective-permute-start.5 = (f32[4,32,128]{2,1,0:T(8,128)S(1)}, f32[4,32,128]{2,1,0:T(8,128)S(1)}, u32[]{:S(2)}, u32[]{:S(2)}) collective-permute-start(f32[4,32,128]{2,1,0:T(8,128)S(1)} %collective-permute-done.4.refs_7_), channel_id=1, source_target_pairs={{152,0},{0,128},{128,8},{8,136},{136,16},{16,144},{144,24},{24,152... | collective-permute-start | bytes 196616 | tf_op jit(solution)/shard_map/ppermute | solution.py:537
  86.7 4.5 %collective-permute-start.2 = (f32[4,32,128]{2,1,0:T(8,128)S(1)}, f32[4,32,128]{2,1,0:T(8,128)S(1)}, u32[]{:S(2)}, u32[]{:S(2)}) collective-permute-start(f32[4,32,128]{2,1,0:T(8,128)S(1)} %collective-permute-done.1.refs_2_), channel_id=1, source_target_pairs={{0,152},{128,0},{8,128},{136,8},{16,136},{144,16},{24,144},{152,24... | collective-permute-start | bytes 196616 | tf_op jit(solution)/shard_map/ppermute | solution.py:535
  89.3 5.5 %collective-permute-start.6 = (f32[4,32,128]{2,1,0:T(8,128)S(1)}, f32[4,32,128]{2,1,0:T(8,128)S(1)}, u32[]{:S(2)}, u32[]{:S(2)}) collective-permute-start(f32[4,32,128]{2,1,0:T(8,128)S(1)} %collective-permute-done.5.refs_6_), channel_id=1, source_target_pairs={{152,0},{0,128},{128,8},{8,136},{136,16},{16,144},{144,24},{24,152... | collective-permute-start | bytes 196616 | tf_op jit(solution)/shard_map/ppermute | solution.py:537
  91.2 5.5 %collective-permute-start.3 = (f32[4,32,128]{2,1,0:T(8,128)S(1)}, f32[4,32,128]{2,1,0:T(8,128)S(1)}, u32[]{:S(2)}, u32[]{:S(2)}) collective-permute-start(f32[4,32,128]{2,1,0:T(8,128)S(1)} %collective-permute-done.2.refs_3_), channel_id=1, source_target_pairs={{0,152},{128,0},{8,128},{136,8},{16,136},{144,16},{24,144},{152,24... | collective-permute-start | bytes 196616 | tf_op jit(solution)/shard_map/ppermute | solution.py:535
  111.5 22.3 %copy-start.12 = (bf16[2,256,256]{2,1,0:T(8,128)(2,1)S(1)}, bf16[2,256,256]{2,1,0:T(8,128)(2,1)}, u32[]{:S(2)}) copy-start(bf16[2,256,256]{2,1,0:T(8,128)(2,1)} %constant.34.clone.there_matrices) | copy-start | bytes 786436
  111.5 22.3 %all-to-all-start.3 = ((f32[32,64,128]{2,1,0:T(8,128)}), f32[32,64,128]{2,1,0:T(8,128)S(1)}, u32[]{:S(2)}, u32[]{:S(2)}) async-start(f32[32,64,128]{2,1,0:T(8,128)} %shard_map.97), calls=%async_computation.3 | async-start | bytes 2097152 | tf_op jit(solution)/shard_map/all_to_all | solution.py:525
  117.6 17.3 %copy-start.9 = (bf16[2,256,256]{2,1,0:T(8,128)(2,1)S(1)}, bf16[2,256,256]{2,1,0:T(8,128)(2,1)}, u32[]{:S(2)}) copy-start(bf16[2,256,256]{2,1,0:T(8,128)(2,1)} %constant.36.clone.back_matrices) | copy-start | bytes 786436
  117.6 5.6 %collective-permute-start.7 = (f32[4,64,128]{2,1,0:T(8,128)S(1)}, f32[4,64,128]{2,1,0:T(8,128)S(1)}, u32[]{:S(2)}, u32[]{:S(2)}) collective-permute-start(f32[4,64,128]{2,1,0:T(8,128)S(1)} %slice.18.refs_0_), channel_id=1, source_target_pairs={{0,152},{128,0},{8,128},{136,8},{16,136},{144,16},{24,144},{152,24... | collective-permute-start | bytes 393224 | tf_op jit(solution)/shard_map/ppermute | solution.py:535
  117.9 6.9 %collective-permute-start.9 = (f32[4,64,128]{2,1,0:T(8,128)S(1)}, f32[4,64,128]{2,1,0:T(8,128)S(1)}, u32[]{:S(2)}, u32[]{:S(2)}) collective-permute-start(f32[4,64,128]{2,1,0:T(8,128)S(1)} %slice.18.refs_0_), channel_id=1, source_target_pairs={{152,0},{0,128},{128,8},{8,136},{136,16},{16,144},{144,24},{24,152... | collective-permute-start | bytes 393224 | tf_op jit(solution)/shard_map/ppermute | solution.py:537
  123.2 15.5 %copy-start.26 = (f32[4,64,128]{2,1,0:T(8,128)}, f32[4,64,128]{2,1,0:T(8,128)S(1)}, u32[]{:S(2)}) copy-start(f32[4,64,128]{2,1,0:T(8,128)S(1)} %collective-permute-done.7.refs_1_) | copy-start | bytes 393220
  123.2 5.0 %collective-permute-start.8 = (f32[4,64,128]{2,1,0:T(8,128)S(1)}, f32[4,64,128]{2,1,0:T(8,128)S(1)}, u32[]{:S(2)}, u32[]{:S(2)}) collective-permute-start(f32[4,64,128]{2,1,0:T(8,128)S(1)} %collective-permute-done.7.refs_1_), channel_id=1, source_target_pairs={{0,152},{128,0},{8,128},{136,8},{16,136},{144,16},{24,144},{152,24... | collective-permute-start | bytes 393224 | tf_op jit(solution)/shard_map/ppermute | solution.py:535
  124.7 14.0 %copy-start.28 = (f32[4,64,128]{2,1,0:T(8,128)}, f32[4,64,128]{2,1,0:T(8,128)S(1)}, u32[]{:S(2)}) copy-start(f32[4,64,128]{2,1,0:T(8,128)S(1)} %collective-permute-done.9.refs_7_) | copy-start | bytes 393220
  124.7 6.2 %collective-permute-start.10 = (f32[4,64,128]{2,1,0:T(8,128)S(1)}, f32[4,64,128]{2,1,0:T(8,128)S(1)}, u32[]{:S(2)}, u32[]{:S(2)}) collective-permute-start(f32[4,64,128]{2,1,0:T(8,128)S(1)} %collective-permute-done.9.refs_7_), channel_id=1, source_target_pairs={{152,0},{0,128},{128,8},{8,136},{136,16},{16,144},{144,24},{24,152... | collective-permute-start | bytes 393224 | tf_op jit(solution)/shard_map/ppermute | solution.py:537
  128.2 10.6 %copy-start.30 = (f32[4,64,128]{2,1,0:T(8,128)}, f32[4,64,128]{2,1,0:T(8,128)S(1)}, u32[]{:S(2)}) copy-start(f32[4,64,128]{2,1,0:T(8,128)S(1)} %collective-permute-done.8.refs_2_) | copy-start | bytes 393220
  138.8 33.1 %all-to-all-start.4 = ((f32[32,2,64,128]{3,2,1,0:T(8,128)}), f32[32,2,64,128]{3,2,1,0:T(8,128)S(1)}, u32[]{:S(2)}, u32[]{:S(2)}) async-start(f32[32,2,64,128]{3,2,1,0:T(8,128)} %shard_map.99), calls=%async_computation.4 | async-start | bytes 4194304 | tf_op jit(solution)/shard_map/all_to_all | solution.py:525
  143.9 5.8 %collective-permute-start.11 = (f32[4,64,128]{2,1,0:T(8,128)}, f32[4,64,128]{2,1,0:T(8,128)S(1)}, u32[]{:S(2)}, u32[]{:S(2)}) collective-permute-start(f32[4,64,128]{2,1,0:T(8,128)} %copy-done.30), channel_id=1, source_target_pairs={{0,152},{128,0},{8,128},{136,8},{16,136},{144,16},{24,144},{152,24... | collective-permute-start | bytes 393224 | tf_op jit(solution)/shard_map/ppermute | solution.py:535
  144.2 7.1 %collective-permute-start.13 = (f32[4,64,128]{2,1,0:T(8,128)}, f32[4,64,128]{2,1,0:T(8,128)S(1)}, u32[]{:S(2)}, u32[]{:S(2)}) collective-permute-start(f32[4,64,128]{2,1,0:T(8,128)} %copy-done.32), channel_id=1, source_target_pairs={{152,0},{0,128},{128,8},{8,136},{136,16},{16,144},{144,24},{24,152... | collective-permute-start | bytes 393224 | tf_op jit(solution)/shard_map/ppermute | solution.py:537
  149.8 5.0 %collective-permute-start.12 = (f32[4,64,128]{2,1,0:T(8,128)S(1)}, f32[4,64,128]{2,1,0:T(8,128)S(1)}, u32[]{:S(2)}, u32[]{:S(2)}) collective-permute-start(f32[4,64,128]{2,1,0:T(8,128)S(1)} %collective-permute-done.11.refs_3_), channel_id=1, source_target_pairs={{0,152},{128,0},{8,128},{136,8},{16,136},{144,16},{24,144},{152,24... | collective-permute-start | bytes 393224 | tf_op jit(solution)/shard_map/ppermute | solution.py:535
  174.5 23.4 %copy-start.19 = (f32[2,256,1024]{2,1,0:T(8,128)S(1)}, f32[2,256,1024]{2,1,0:T(8,128)}, u32[]{:S(2)}) copy-start(f32[2,256,1024]{2,1,0:T(8,128)} %copy-done.18) | copy-start | bytes 6291460
  176.5 21.4 %copy-start.10 = (bf16[2,256,256]{2,1,0:T(8,128)(2,1)S(1)}, bf16[2,256,256]{2,1,0:T(8,128)(2,1)}, u32[]{:S(2)}) copy-start(bf16[2,256,256]{2,1,0:T(8,128)(2,1)} %constant.36.clone.back_matrices) | copy-start | bytes 786436
  176.5 21.4 %copy-start.13 = (bf16[2,256,256]{2,1,0:T(8,128)(2,1)S(1)}, bf16[2,256,256]{2,1,0:T(8,128)(2,1)}, u32[]{:S(2)}) copy-start(bf16[2,256,256]{2,1,0:T(8,128)(2,1)} %constant.34.clone.there_matrices) | copy-start | bytes 786436
  200.9 32.0 %copy-start.7 = (bf16[2,256,256]{2,1,0:T(8,128)(2,1)S(1)}, bf16[2,256,256]{2,1,0:T(8,128)(2,1)}, u32[]{:S(2)}) copy-start(bf16[2,256,256]{2,1,0:T(8,128)(2,1)} %constant.37.clone.back_matrices) | copy-start | bytes 786436
  200.9 32.0 %copy-start.23 = (f32[4,16,64,128]{3,2,1,0:T(8,128)S(1)}, f32[4,16,64,128]{3,2,1,0:T(8,128)}, u32[]{:S(2)}) copy-start(f32[4,16,64,128]{3,2,1,0:T(8,128)} %copy-done.22) | copy-start | bytes 6291460
  (21 other events, 38.6 us)

commit v9 on v8

--- a/solution.py
+++ b/solution.py
@@ -227,7 +227,17 @@
             write(2 * (k + n) + 1, one[:, inner:])
 
 
-def start_kernel(freqs, wavefield, velocity, matrices, out, spectrum, turns):
+def fill_forward_y(matrices):
+    row = lax.broadcasted_iota(jnp.int32, (2 * inner, 2 * inner), 0)
+    column = lax.broadcasted_iota(jnp.int32, (2 * inner, 2 * inner), 1)
+    j = column % half + half * (column // inner)
+    turn = 32 * (row // inner - column // half % 2) - (row % inner) * j
+    cosine, _ = cis((turn % inner).astype(jnp.float32) * (1.0 / inner))
+    matrices[0], matrices[1] = cut(cosine * (1.0 / math.sqrt(length)))
+
+
+def start_kernel(freqs, wavefield, velocity, out, spectrum, turns, matrices):
+    fill_forward_y(matrices)
     fill_y_turns(turns)
 
     def read(here, a):
@@ -516,7 +526,7 @@
         out_shape=[jax.ShapeDtypeStruct(s, jnp.float32) for s in shapes],
         in_specs=[smem] * len(scalars) + [vmem] * len(operands),
         out_specs=[vmem] * len(shapes),
-        scratch_shapes=[pltpu.VMEM(s, jnp.float32) for s in scratch],
+        scratch_shapes=[pltpu.VMEM(s, jnp.float32) if isinstance(s, tuple) else s for s in scratch],
         compiler_params=pltpu.CompilerParams(vmem_limit_bytes=12 * 1024 * 1024),
     )(*scalars, *operands)
 
@@ -558,9 +568,13 @@
     (sent,) = call(
         start_kernel,
         [(4, message, inner)],
-        [spectrum_shape, y_turns_shape],
+        [
+            spectrum_shape,
+            y_turns_shape,
+            pltpu.VMEM((2, 2 * inner, 2 * inner), jnp.bfloat16),
+        ],
         (freqs,),
-        (wavefield, velocity, fy_matrix),
+        (wavefield, velocity),
     )
     sent = exchange(sent, ("y",))
     sent, cells = lax.optimization_barrier((sent[:, :cell_start], sent[:, cell_start:]))

time: 286 us -> 284 us (level)
  waiting for transfers between devices: 56.5 us -> 53.6 us
    unnamed x71 -> x65, local copies, waits for them, and re-layouts: 19.1 us -> 18.1 us
where the time goes in v9:
time: 284 us; the launch traced here: 283 us
  blocking collectives  124 us (44%)
  waiting for transfers between devices  53.6 us (19%)
  starting transfers between devices  46.7 us (16%)
  Pallas kernels  36.8 us (13%)
  local copies, waits for them, and re-layouts  21 us (7%)
    all_to_all x5, blocking collectives, exchange(): return lax.all_to_all(values, axes, split_axis=0, concat_axis=0, tiled=True)  124 us
    pallas_call x14, Pallas kernels, call(): pl.pallas_call(kernel, out_shape=[jax.ShapeDtypeStruct(s, jnp.float32) fo...  36.8 us
    all_to_all x4, waiting for transfers between devices, exchange(): return lax.all_to_all(values, axes, split_axis=0, concat_axis=0, tiled=True)  29.6 us
    all_to_all x4, starting transfers between devices, exchange(): return lax.all_to_all(values, axes, split_axis=0, concat_axis=0, tiled=True)  28.7 us
    ppermute x8, waiting for transfers between devices, around_z(): tiles[n] = lax.ppermute(tiles[n - 1], axes, down)  20.8 us
    unnamed x65, local copies, waits for them, and re-layouts  18.1 us
    ppermute x8, starting transfers between devices, around_z(): tiles[n] = lax.ppermute(tiles[n - 1], axes, down)  11.6 us
    ppermute x6, starting transfers between devices, around_z(): tiles[ring - n] = lax.ppermute(tiles[(ring + 1 - n) % ring], axes, up)  6.37 us
  transfers between devices with their start and end apart: 18, of which 13 were waited for; matrix products, arithmetic and copies ran while one was open for 0% of the time, Pallas kernels for 5%

profile of v9, /device:TPU:2, one launch (start us, length us, event | category | flops | bytes accessed | tf_op | source)
XLA Modules:
  0.0 283.0 jit_solution(6271182357366007016)
XLA Ops:
  4.1 21.6 %all_to_all.45 = f32[4,616,128]{2,1,0:T(8,128)S(1)} all-to-all(f32[4,616,128]{2,1,0:T(8,128)S(1)} %shard_map.91), channel_id=1, replica_groups=mesh['zl'=2,'y'=4,'zh'=4,'x'=4,'c'=2] {'y'}, dimensions={0} | all-to-all | bytes 2523136 | tf_op jit(solution)/shard_map/all_to_all | solution.py:535
  26.9 11.6 %all-to-all-start.1 = ((f32[32,64,128]{2,1,0:T(8,128)}), f32[32,64,128]{2,1,0:T(8,128)S(1)}, u32[]{:S(2)}, u32[]{:S(2)}) async-start(f32[32,64,128]{2,1,0:T(8,128)} %bitcast.14), calls=%async_computation.1 | async-start | bytes 2097152 | tf_op jit(solution)/shard_map/all_to_all | solution.py:535
  39.4 7.5 %shard_map.93 = (f32[2,256,1024]{2,1,0:T(8,128)S(1)}, f32[2,256,1024]{2,1,0:T(8,128)S(1)}, f32[2,256,1024]{2,1,0:T(8,128)S(1)}) custom-call(s32[3]{0:T(128)S(1)} %pad_add_fusion.place, f32[4]{0:T(128)S(1)} %slice_reduce_fusion.freqs, f32[3,2]{1,0:T(4,128)S(1)} %copy.13.ref_slow), custom_call_target="tpu_custom_call" | custom-call | tf_op jit(solution)/shard_map/pallas_call | solution.py:524
  51.0 16.0 %all-to-all-done.1 = f32[32,64,128]{2,1,0:T(8,128)S(1)} async-done(((f32[32,64,128]{2,1,0:T(8,128)}), f32[32,64,128]{2,1,0:T(8,128)S(1)}, u32[]{:S(2)}, u32[]{:S(2)}) %all-to-all-start.1) | async-done | bytes 1048608 | tf_op jit(solution)/shard_map/all_to_all | solution.py:535
  68.6 3.4 %shard_map.94 = f32[32,2,64,128]{3,2,1,0:T(8,128)} custom-call(f32[256,1024]{1,0:T(8,128)S(1)} %shard_map.92.spectrum, f32[2,256,1024]{2,1,0:T(8,128)S(1)} %copy-done.15, bf16[2,256,256]{2,1,0:T(8,128)(2,1)S(1)} %copy-done.4, f32[2,8,128,128]{3,2,1,0:T(8,128)S(1)} %copy-done), custom_call_target="tpu_custom_call" | custom-call | tf_op jit(solution)/shard_map/pallas_call | solution.py:524
  72.0 5.5 %all-to-all-start.2 = ((f32[32,2,64,128]{3,2,1,0:T(8,128)}), f32[32,2,64,128]{3,2,1,0:T(8,128)S(1)}, u32[]{:S(2)}, u32[]{:S(2)}) async-start(f32[32,2,64,128]{3,2,1,0:T(8,128)} %shard_map.94), calls=%async_computation.2 | async-start | bytes 4194304 | tf_op jit(solution)/shard_map/all_to_all | solution.py:535
  77.8 1.9 collective-permute-start.4
  79.7 2.4 collective-permute-done.refs_1_
  84.2 2.2 collective-permute-done.1.refs_2_
  86.4 2.6 collective-permute-start.2
  90.9 3.6 %collective-permute-start.3 = (f32[4,32,128]{2,1,0:T(8,128)S(1)}, f32[4,32,128]{2,1,0:T(8,128)S(1)}, u32[]{:S(2)}, u32[]{:S(2)}) collective-permute-start(f32[4,32,128]{2,1,0:T(8,128)S(1)} %collective-permute-done.2.refs_3_), channel_id=1, source_target_pairs={{0,152},{128,0},{8,128},{136,8},{16,136},{144,16},{24,144},{152,24... | collective-permute-start | bytes 196616 | tf_op jit(solution)/shard_map/ppermute | solution.py:545
  94.5 1.9 collective-permute-done.3.refs_4_
  97.2 2.3 shard_map.96.weights
  100.9 4.5 %all-to-all-done.2.moved = f32[32,2,64,128]{3,2,1,0:T(8,128)S(1)} async-done(((f32[32,2,64,128]{3,2,1,0:T(8,128)}), f32[32,2,64,128]{3,2,1,0:T(8,128)S(1)}, u32[]{:S(2)}, u32[]{:S(2)}) %all-to-all-start.2) | async-done | bytes 2097184 | tf_op jit(solution)/shard_map/all_to_all | solution.py:535
  107.1 3.0 %shard_map.97 = f32[32,64,128]{2,1,0:T(8,128)} custom-call(f32[2,16,64,256]{3,2,1,0:T(8,128)S(1)} %shard_map.95.fields, f32[4,16,64,128]{3,2,1,0:T(8,128)S(1)} %copy-done.2, bf16[2,256,256]{2,1,0:T(8,128)(2,1)S(1)} %copy-done.7), custom_call_target="tpu_custom_call" | custom-call | tf_op jit(solution)/shard_map/pallas_call | solution.py:524
  110.0 6.1 %all-to-all-start.3 = ((f32[32,64,128]{2,1,0:T(8,128)}), f32[32,64,128]{2,1,0:T(8,128)S(1)}, u32[]{:S(2)}, u32[]{:S(2)}) async-start(f32[32,64,128]{2,1,0:T(8,128)} %shard_map.97), calls=%async_computation.3 | async-start | bytes 2097152 | tf_op jit(solution)/shard_map/all_to_all | solution.py:535
  118.2 3.5 %collective-permute-done.7.refs_1_ = f32[4,64,128]{2,1,0:T(8,128)S(1)} collective-permute-done((f32[4,64,128]{2,1,0:T(8,128)S(1)}, f32[4,64,128]{2,1,0:T(8,128)S(1)}, u32[]{:S(2)}, u32[]{:S(2)}) %collective-permute-start.7) | collective-permute-done | bytes 131104 | tf_op jit(solution)/shard_map/ppermute | solution.py:545
  127.4 3.1 %collective-permute-done.10.refs_6_ = f32[4,64,128]{2,1,0:T(8,128)} collective-permute-done((f32[4,64,128]{2,1,0:T(8,128)S(1)}, f32[4,64,128]{2,1,0:T(8,128)}, u32[]{:S(2)}, u32[]{:S(2)}) %collective-permute-start.10) | collective-permute-done | bytes 131104 | tf_op jit(solution)/shard_map/ppermute | solution.py:547
  133.9 3.4 %shard_map.99 = f32[32,2,64,128]{3,2,1,0:T(8,128)} custom-call(f32[256,1024]{1,0:T(8,128)S(1)} %shard_map.98.spectrum, f32[2,256,1024]{2,1,0:T(8,128)S(1)} %copy-done.13, bf16[2,256,256]{2,1,0:T(8,128)(2,1)S(1)} %copy-done.5, f32[2,8,128,128]{3,2,1,0:T(8,128)S(1)} %copy-done), custom_call_target="tpu_custom_call" | custom-call | tf_op jit(solution)/shard_map/pallas_call | solution.py:524
  137.4 5.5 %all-to-all-start.4 = ((f32[32,2,64,128]{3,2,1,0:T(8,128)}), f32[32,2,64,128]{3,2,1,0:T(8,128)S(1)}, u32[]{:S(2)}, u32[]{:S(2)}) async-start(f32[32,2,64,128]{3,2,1,0:T(8,128)} %shard_map.99), calls=%async_computation.4 | async-start | bytes 4194304 | tf_op jit(solution)/shard_map/all_to_all | solution.py:535
  143.0 2.0 collective-permute-start.13
  145.0 3.7 %collective-permute-done.11.refs_3_ = f32[4,64,128]{2,1,0:T(8,128)S(1)} collective-permute-done((f32[4,64,128]{2,1,0:T(8,128)}, f32[4,64,128]{2,1,0:T(8,128)S(1)}, u32[]{:S(2)}, u32[]{:S(2)}) %collective-permute-start.11) | collective-permute-done | bytes 131104 | tf_op jit(solution)/shard_map/ppermute | solution.py:545
  150.2 3.5 %collective-permute-done.12.refs_4_ = f32[4,64,128]{2,1,0:T(8,128)S(1)} collective-permute-done((f32[4,64,128]{2,1,0:T(8,128)S(1)}, f32[4,64,128]{2,1,0:T(8,128)S(1)}, u32[]{:S(2)}, u32[]{:S(2)}) %collective-permute-start.12) | collective-permute-done | bytes 131104 | tf_op jit(solution)/shard_map/ppermute | solution.py:545
  156.4 4.4 %shard_map.101 = (f32[4,16,64,128]{3,2,1,0:T(8,128)S(1)}, f32[4,16,64,128]{3,2,1,0:T(8,128)S(1)}) custom-call(s32[3]{0:T(128)S(1)} %pad_add_fusion.place, f32[4]{0:T(128)S(1)} %slice_reduce_fusion.freqs, f32[3,2]{1,0:T(4,128)S(1)} %copy.13.ref_slow, f32[4,64,128]{2,1,0:T(8,128)S(1)} %slice.18.refs_0_, f32[4,64,128]{2,1,0:T(8,128)S(1)} %copy-done.26, ...), custom_call_target="tpu_custom_call" | custom-call | tf_op jit(solution)/shard_map/pallas_call | solution.py:524
  163.5 7.2 %all-to-all-done.4.moved = f32[32,2,64,128]{3,2,1,0:T(8,128)S(1)} async-done(((f32[32,2,64,128]{3,2,1,0:T(8,128)}), f32[32,2,64,128]{3,2,1,0:T(8,128)S(1)}, u32[]{:S(2)}, u32[]{:S(2)}) %all-to-all-start.4) | async-done | bytes 2097184 | tf_op jit(solution)/shard_map/all_to_all | solution.py:535
  172.4 2.0 shard_map.102
  174.5 21.4 %all_to_all.46 = f32[32,64,128]{2,1,0:T(8,128)S(1)} all-to-all(f32[32,64,128]{2,1,0:T(8,128)S(1)} %shard_map.102), channel_id=1, replica_groups=mesh['zl'=2,'y'=4,'zh'=4,'x'=4,'c'=2] {'y','x','c'}, dimensions={0} | all-to-all | bytes 2097152 | tf_op jit(solution)/shard_map/all_to_all | solution.py:535
  195.9 3.1 %shard_map.103 = f32[32,2,64,128]{3,2,1,0:T(8,128)S(1)} custom-call(f32[2048,128]{1,0:T(8,128)S(1)} %bitcast.13, f32[2,256,1024]{2,1,0:T(8,128)S(1)} %copy-done.17, bf16[2,256,256]{2,1,0:T(8,128)(2,1)S(1)} %copy-done.11, bf16[2,256,256]{2,1,0:T(8,128)(2,1)S(1)} %copy-done.6, f32[2,8,128,128]{3,2,1,0:T(8,128)S(1)} %copy-done), custom_call_target="tpu_custom_call" | custom-call | tf_op jit(solution)/shard_map/pallas_call | solution.py:524
  199.0 32.0 %all_to_all.47.moved = f32[32,2,64,128]{3,2,1,0:T(8,128)S(1)} all-to-all(f32[32,2,64,128]{3,2,1,0:T(8,128)S(1)} %shard_map.103), channel_id=1, replica_groups=mesh['zl'=2,'y'=4,'zh'=4,'x'=4,'c'=2] {'y','x','c'}, dimensions={0} | all-to-all | bytes 4194304 | tf_op jit(solution)/shard_map/all_to_all | solution.py:535
  231.0 2.0 shard_map.104
  233.0 31.1 %all_to_all.48 = f32[4,2,16,2048]{3,2,1,0:T(8,128)S(1)} all-to-all(f32[4,2,16,2048]{3,2,1,0:T(8,128)S(1)} %shard_map.104), channel_id=1, replica_groups=mesh['zl'=2,'y'=4,'zh'=4,'x'=4,'c'=2] {'zh'}, dimensions={0} | all-to-all | bytes 2097152 | tf_op jit(solution)/shard_map/all_to_all | solution.py:535
  264.1 17.8 %all_to_all.49 = f32[4,2,16,2048]{3,2,1,0:T(8,128)S(1)} all-to-all(f32[4,2,16,2048]{3,2,1,0:T(8,128)S(1)} %all_to_all.48), channel_id=1, replica_groups=mesh['zl'=2,'y'=4,'zh'=4,'x'=4,'c'=2] {'y'}, dimensions={0} | all-to-all | bytes 2097152 | tf_op jit(solution)/shard_map/all_to_all | solution.py:535
  (95 shorter events, 40.0 us)
Async XLA Ops:
  25.8 12.7 %copy-start.31 = (f32[3,2]{0,1:T(2,128)S(1)}, f32[3,2]{0,1:T(2,128)}, u32[]{:S(2)}) copy-start(f32[3,2]{0,1:T(2,128)} %param.12) | copy-start | bytes 76
  25.8 41.2 %copy-start = (f32[2,8,128,128]{3,2,1,0:T(8,128)S(1)}, f32[2,8,128,128]{3,2,1,0:T(8,128)}, u32[]{:S(2)}) copy-start(f32[2,8,128,128]{3,2,1,0:T(8,128)} %constant.34.clone.turns) | copy-start | bytes 3145732
  25.8 41.2 %copy-start.9 = (bf16[2,256,256]{2,1,0:T(8,128)(2,1)S(1)}, bf16[2,256,256]{2,1,0:T(8,128)(2,1)}, u32[]{:S(2)}) copy-start(bf16[2,256,256]{2,1,0:T(8,128)(2,1)} %constant.33.clone.there_matrices) | copy-start | bytes 786436
  26.9 40.2 %all-to-all-start.1 = ((f32[32,64,128]{2,1,0:T(8,128)}), f32[32,64,128]{2,1,0:T(8,128)S(1)}, u32[]{:S(2)}, u32[]{:S(2)}) async-start(f32[32,64,128]{2,1,0:T(8,128)} %bitcast.14), calls=%async_computation.1 | async-start | bytes 2097152 | tf_op jit(solution)/shard_map/all_to_all | solution.py:535
  38.5 29.7 %copy-start.4 = (bf16[2,256,256]{2,1,0:T(8,128)(2,1)S(1)}, bf16[2,256,256]{2,1,0:T(8,128)(2,1)}, u32[]{:S(2)}) copy-start(bf16[2,256,256]{2,1,0:T(8,128)(2,1)} %constant.35.clone.back_matrices) | copy-start | bytes 786436
  72.0 33.4 %all-to-all-start.2 = ((f32[32,2,64,128]{3,2,1,0:T(8,128)}), f32[32,2,64,128]{3,2,1,0:T(8,128)S(1)}, u32[]{:S(2)}, u32[]{:S(2)}) async-start(f32[32,2,64,128]{3,2,1,0:T(8,128)} %shard_map.94), calls=%async_computation.2 | async-start | bytes 4194304 | tf_op jit(solution)/shard_map/all_to_all | solution.py:535
  77.6 27.9 %copy-start.3 = (bf16[2,256,256]{2,1,0:T(8,128)(2,1)S(1)}, bf16[2,256,256]{2,1,0:T(8,128)(2,1)}, u32[]{:S(2)}) copy-start(bf16[2,256,256]{2,1,0:T(8,128)(2,1)} %constant.36.clone.back_matrices) | copy-start | bytes 786436
  77.6 4.6 %collective-permute-start = (f32[4,32,128]{2,1,0:T(8,128)}, f32[4,32,128]{2,1,0:T(8,128)S(1)}, u32[]{:S(2)}, u32[]{:S(2)}) collective-permute-start(f32[4,32,128]{2,1,0:T(8,128)} %slice.17.refs_0_), channel_id=1, source_target_pairs={{0,152},{128,0},{8,128},{136,8},{16,136},{144,16},{24,144},{152,24... | collective-permute-start | bytes 196616 | tf_op jit(solution)/shard_map/ppermute | solution.py:545
  77.8 5.8 %collective-permute-start.4 = (f32[4,32,128]{2,1,0:T(8,128)}, f32[4,32,128]{2,1,0:T(8,128)S(1)}, u32[]{:S(2)}, u32[]{:S(2)}) collective-permute-start(f32[4,32,128]{2,1,0:T(8,128)} %slice.17.refs_0_), channel_id=1, source_target_pairs={{152,0},{0,128},{128,8},{8,136},{136,16},{16,144},{144,24},{24,152... | collective-permute-start | bytes 196616 | tf_op jit(solution)/shard_map/ppermute | solution.py:547
  82.1 4.3 %collective-permute-start.1 = (f32[4,32,128]{2,1,0:T(8,128)S(1)}, f32[4,32,128]{2,1,0:T(8,128)S(1)}, u32[]{:S(2)}, u32[]{:S(2)}) collective-permute-start(f32[4,32,128]{2,1,0:T(8,128)S(1)} %collective-permute-done.refs_1_), channel_id=1, source_target_pairs={{0,152},{128,0},{8,128},{136,8},{16,136},{144,16},{24,144},{152,24... | collective-permute-start | bytes 196616 | tf_op jit(solution)/shard_map/ppermute | solution.py:545
  83.5 5.5 %collective-permute-start.5 = (f32[4,32,128]{2,1,0:T(8,128)S(1)}, f32[4,32,128]{2,1,0:T(8,128)S(1)}, u32[]{:S(2)}, u32[]{:S(2)}) collective-permute-start(f32[4,32,128]{2,1,0:T(8,128)S(1)} %collective-permute-done.4.refs_7_), channel_id=1, source_target_pairs={{152,0},{0,128},{128,8},{8,136},{136,16},{16,144},{144,24},{24,152... | collective-permute-start | bytes 196616 | tf_op jit(solution)/shard_map/ppermute | solution.py:547
  86.4 4.5 %collective-permute-start.2 = (f32[4,32,128]{2,1,0:T(8,128)S(1)}, f32[4,32,128]{2,1,0:T(8,128)S(1)}, u32[]{:S(2)}, u32[]{:S(2)}) collective-permute-start(f32[4,32,128]{2,1,0:T(8,128)S(1)} %collective-permute-done.1.refs_2_), channel_id=1, source_target_pairs={{0,152},{128,0},{8,128},{136,8},{16,136},{144,16},{24,144},{152,24... | collective-permute-start | bytes 196616 | tf_op jit(solution)/shard_map/ppermute | solution.py:545
  89.0 5.5 %collective-permute-start.6 = (f32[4,32,128]{2,1,0:T(8,128)S(1)}, f32[4,32,128]{2,1,0:T(8,128)S(1)}, u32[]{:S(2)}, u32[]{:S(2)}) collective-permute-start(f32[4,32,128]{2,1,0:T(8,128)S(1)} %collective-permute-done.5.refs_6_), channel_id=1, source_target_pairs={{152,0},{0,128},{128,8},{8,136},{136,16},{16,144},{144,24},{24,152... | collective-permute-start | bytes 196616 | tf_op jit(solution)/shard_map/ppermute | solution.py:547
  90.9 5.5 %collective-permute-start.3 = (f32[4,32,128]{2,1,0:T(8,128)S(1)}, f32[4,32,128]{2,1,0:T(8,128)S(1)}, u32[]{:S(2)}, u32[]{:S(2)}) collective-permute-start(f32[4,32,128]{2,1,0:T(8,128)S(1)} %collective-permute-done.2.refs_3_), channel_id=1, source_target_pairs={{0,152},{128,0},{8,128},{136,8},{16,136},{144,16},{24,144},{152,24... | collective-permute-start | bytes 196616 | tf_op jit(solution)/shard_map/ppermute | solution.py:545
  105.5 1.6 copy-start.2
  105.5 1.6 copy-start.7
  110.0 22.3 %copy-start.10 = (bf16[2,256,256]{2,1,0:T(8,128)(2,1)S(1)}, bf16[2,256,256]{2,1,0:T(8,128)(2,1)}, u32[]{:S(2)}) copy-start(bf16[2,256,256]{2,1,0:T(8,128)(2,1)} %constant.33.clone.there_matrices) | copy-start | bytes 786436
  110.0 22.3 %all-to-all-start.3 = ((f32[32,64,128]{2,1,0:T(8,128)}), f32[32,64,128]{2,1,0:T(8,128)S(1)}, u32[]{:S(2)}, u32[]{:S(2)}) async-start(f32[32,64,128]{2,1,0:T(8,128)} %shard_map.97), calls=%async_computation.3 | async-start | bytes 2097152 | tf_op jit(solution)/shard_map/all_to_all | solution.py:535
  116.1 17.3 %copy-start.5 = (bf16[2,256,256]{2,1,0:T(8,128)(2,1)S(1)}, bf16[2,256,256]{2,1,0:T(8,128)(2,1)}, u32[]{:S(2)}) copy-start(bf16[2,256,256]{2,1,0:T(8,128)(2,1)} %constant.35.clone.back_matrices) | copy-start | bytes 786436
  116.1 5.6 %collective-permute-start.7 = (f32[4,64,128]{2,1,0:T(8,128)S(1)}, f32[4,64,128]{2,1,0:T(8,128)S(1)}, u32[]{:S(2)}, u32[]{:S(2)}) collective-permute-start(f32[4,64,128]{2,1,0:T(8,128)S(1)} %slice.18.refs_0_), channel_id=1, source_target_pairs={{0,152},{128,0},{8,128},{136,8},{16,136},{144,16},{24,144},{152,24... | collective-permute-start | bytes 393224 | tf_op jit(solution)/shard_map/ppermute | solution.py:545
  116.7 7.4 %collective-permute-start.9 = (f32[4,64,128]{2,1,0:T(8,128)S(1)}, f32[4,64,128]{2,1,0:T(8,128)S(1)}, u32[]{:S(2)}, u32[]{:S(2)}) collective-permute-start(f32[4,64,128]{2,1,0:T(8,128)S(1)} %slice.18.refs_0_), channel_id=1, source_target_pairs={{152,0},{0,128},{128,8},{8,136},{136,16},{16,144},{144,24},{24,152... | collective-permute-start | bytes 393224 | tf_op jit(solution)/shard_map/ppermute | solution.py:547
  121.8 5.0 %collective-permute-start.8 = (f32[4,64,128]{2,1,0:T(8,128)S(1)}, f32[4,64,128]{2,1,0:T(8,128)S(1)}, u32[]{:S(2)}, u32[]{:S(2)}) collective-permute-start(f32[4,64,128]{2,1,0:T(8,128)S(1)} %collective-permute-done.7.refs_1_), channel_id=1, source_target_pairs={{0,152},{128,0},{8,128},{136,8},{16,136},{144,16},{24,144},{152,24... | collective-permute-start | bytes 393224 | tf_op jit(solution)/shard_map/ppermute | solution.py:545
  124.2 6.3 %collective-permute-start.10 = (f32[4,64,128]{2,1,0:T(8,128)S(1)}, f32[4,64,128]{2,1,0:T(8,128)}, u32[]{:S(2)}, u32[]{:S(2)}) collective-permute-start(f32[4,64,128]{2,1,0:T(8,128)S(1)} %collective-permute-done.9.refs_7_), channel_id=1, source_target_pairs={{152,0},{0,128},{128,8},{8,136},{136,16},{16,144},{144,24},{24,152... | collective-permute-start | bytes 393224 | tf_op jit(solution)/shard_map/ppermute | solution.py:547
  137.4 33.4 %all-to-all-start.4 = ((f32[32,2,64,128]{3,2,1,0:T(8,128)}), f32[32,2,64,128]{3,2,1,0:T(8,128)S(1)}, u32[]{:S(2)}, u32[]{:S(2)}) async-start(f32[32,2,64,128]{3,2,1,0:T(8,128)} %shard_map.99), calls=%async_computation.4 | async-start | bytes 4194304 | tf_op jit(solution)/shard_map/all_to_all | solution.py:535
  142.9 5.8 %collective-permute-start.11 = (f32[4,64,128]{2,1,0:T(8,128)}, f32[4,64,128]{2,1,0:T(8,128)S(1)}, u32[]{:S(2)}, u32[]{:S(2)}) collective-permute-start(f32[4,64,128]{2,1,0:T(8,128)} %copy-done.29), channel_id=1, source_target_pairs={{0,152},{128,0},{8,128},{136,8},{16,136},{144,16},{24,144},{152,24... | collective-permute-start | bytes 393224 | tf_op jit(solution)/shard_map/ppermute | solution.py:545
  143.0 7.2 %collective-permute-start.13 = (f32[4,64,128]{2,1,0:T(8,128)}, f32[4,64,128]{2,1,0:T(8,128)S(1)}, u32[]{:S(2)}, u32[]{:S(2)}) collective-permute-start(f32[4,64,128]{2,1,0:T(8,128)} %collective-permute-done.10.refs_6_), channel_id=1, source_target_pairs={{152,0},{0,128},{128,8},{8,136},{136,16},{16,144},{144,24},{24,152... | collective-permute-start | bytes 393224 | tf_op jit(solution)/shard_map/ppermute | solution.py:547
  148.7 5.0 %collective-permute-start.12 = (f32[4,64,128]{2,1,0:T(8,128)S(1)}, f32[4,64,128]{2,1,0:T(8,128)S(1)}, u32[]{:S(2)}, u32[]{:S(2)}) collective-permute-start(f32[4,64,128]{2,1,0:T(8,128)S(1)} %collective-permute-done.11.refs_3_), channel_id=1, source_target_pairs={{0,152},{128,0},{8,128},{136,8},{16,136},{144,16},{24,144},{152,24... | collective-permute-start | bytes 393224 | tf_op jit(solution)/shard_map/ppermute | solution.py:545
  170.7 1.7 copy-start.19
  172.4 23.4 %copy-start.17 = (f32[2,256,1024]{2,1,0:T(8,128)S(1)}, f32[2,256,1024]{2,1,0:T(8,128)}, u32[]{:S(2)}) copy-start(f32[2,256,1024]{2,1,0:T(8,128)} %copy-done.16) | copy-start | bytes 6291460
  174.5 21.4 %copy-start.6 = (bf16[2,256,256]{2,1,0:T(8,128)(2,1)S(1)}, bf16[2,256,256]{2,1,0:T(8,128)(2,1)}, u32[]{:S(2)}) copy-start(bf16[2,256,256]{2,1,0:T(8,128)(2,1)} %constant.35.clone.back_matrices) | copy-start | bytes 786436
  174.5 21.4 %copy-start.11 = (bf16[2,256,256]{2,1,0:T(8,128)(2,1)S(1)}, bf16[2,256,256]{2,1,0:T(8,128)(2,1)}, u32[]{:S(2)}) copy-start(bf16[2,256,256]{2,1,0:T(8,128)(2,1)} %constant.33.clone.there_matrices) | copy-start | bytes 786436
  199.0 32.0 %copy-start.21 = (f32[4,16,64,128]{3,2,1,0:T(8,128)S(1)}, f32[4,16,64,128]{3,2,1,0:T(8,128)}, u32[]{:S(2)}) copy-start(f32[4,16,64,128]{3,2,1,0:T(8,128)} %copy-done.20) | copy-start | bytes 6291460
  (18 other events, 20.1 us)
